TPU v7x, 128 devices: a whole 4x4x4 slice. The times are simulated.
128 devices in a mesh: dp: 16 (over y_hi, z, core), tensor: 8 (over x, y_lo).
Axes of the slice: x: 4, y: 4 (y_hi: 2, y_lo: 2; y = y_hi * 2 + y_lo), z: 4, core: 2. Of those that a mesh axis runs over, the one named last changes fastest.
Arguments:
- inputs: bfloat16 [16384, 1024], P(('dp', 'tensor')), may hold values from -6 to 6
- first_gain: bfloat16 [1024], P('dp'), may hold values from 0.5 to 1.5
- query_weight: bfloat16 [1024, 1024], P('dp', 'tensor'), may hold values from -0.65625 to 0.65625
- key_matrix: bfloat16 [1024, 512], P('dp', 'tensor'), may hold values from -0.65625 to 0.65625
- value_matrix: bfloat16 [1024, 512], P('dp', 'tensor'), may hold values from -0.1875 to 0.1875
- output_weight: bfloat16 [1024, 1024], P('tensor', 'dp'), may hold values from -3 to 3
- second_gain: bfloat16 [1024], P('dp'), may hold values from 0.5 to 1.5
- gate_weight: bfloat16 [32, 1024, 512], P('tensor', 'dp'), may hold values from -0.1875 to 0.1875
- up_weight: bfloat16 [32, 1024, 512], P('tensor', 'dp'), may hold values from -0.1875 to 0.1875
- down_weight: bfloat16 [32, 512, 1024], P('tensor', None, 'dp'), may hold values from -4.78125 to 4.78125
- expert_ids: int32 [16384, 8], P('dp'), may hold values from 0 to 31, all different within a row; in each aligned block of 1024 rows (0 to 1023, 1024 to 2047, ...) at most 512 rows name the same one
- gate_values: float32 [16384, 8], P('dp'), may hold values from 0.05 to 0.25
- out_grad: bfloat16 [16384, 1024], P(('dp', 'tensor')), may hold values from -6 to 6
Outputs:
- block_output: bfloat16 [16384, 1024], P(('dp', 'tensor'))
- input_grad: bfloat16 [16384, 1024], P(('dp', 'tensor'))
- first_gain_grad: float32 [1024], P('dp')
- query_weight_grad: float32 [1024, 1024], P('dp', 'tensor')
- key_weight_grad: float32 [1024, 512], P('dp', 'tensor')
- value_weight_grad: float32 [1024, 512], P('dp', 'tensor')
- output_weight_grad: float32 [1024, 1024], P('tensor', 'dp')
- second_gain_grad: float32 [1024], P('dp')
- gate_weight_grad: float32 [32, 1024, 512], P('tensor', 'dp')
- up_weight_grad: float32 [32, 1024, 512], P('tensor', 'dp')
- down_weight_grad: float32 [32, 512, 1024], P('tensor', None, 'dp')
Inputs may be any that keep to these rules, and one draw needn't show every extreme that they name: `expert_ids`: each row names 8 different experts. Within the rows of one sequence no expert is named more than 512 times, and in some sequence some expert is named exactly 512 times.
All inputs are finite; a program needn't handle non-finite values.
Results may differ from a plain program's by a relative error of at most 0.03.
Values may be sent and summed in bfloat16 or wider, within the bound.
A program may use at most 192 MiB of HBM per device.

v0:
```python
import jax
import jax.numpy as jnp
from jax import lax
from jax.sharding import PartitionSpec as P

HEAD_SIZE = 64
NORM_EPSILON = 1e-06
ATT_SCALE = 0.015625
RES_SCALE = 0.22
ROPE_BASE = 10000.0
NEG_FILL = -1e30
F32 = jnp.float32
BF16 = jnp.bfloat16


def rms_normed(activations, gain_vector):
    return (
        activations
        * lax.rsqrt(jnp.mean(activations * activations, axis=-1, keepdims=True) + NORM_EPSILON)
        * gain_vector
    )


def rotary_tables(length):
    half_width = HEAD_SIZE // 2
    positions = jnp.arange(length).astype(F32)
    frequencies = jnp.power(ROPE_BASE, -(jnp.arange(half_width).astype(F32) * 2.0 / HEAD_SIZE))
    angles = positions[:, None] * frequencies[None, :]
    return (jnp.cos(angles)[:, None, :], jnp.sin(angles)[:, None, :])


def apply_rotary(head_data, cosine, sine):
    half_width = head_data.shape[-1] // 2
    first_half = head_data[..., :half_width]
    second_half = head_data[..., half_width:]
    return jnp.concatenate(
        [first_half * cosine - second_half * sine, second_half * cosine + first_half * sine], axis=-1
    )


def mm(a, b, spec):
    return jnp.einsum(spec, a, b, preferred_element_type=F32)


def local(
    inputs, first_gain, query_weight, key_matrix, value_matrix, output_weight, second_gain,
    gate_weight, up_weight, down_weight, expert_ids, gate_values, out_grad,
):
    dp_size = lax.axis_size("dp")
    rank = lax.axis_index("tensor")
    rows = inputs.shape[0] * lax.axis_size("tensor")
    experts, part, units = gate_weight.shape
    width = part * dp_size
    qw = query_weight.shape[1]
    kw = key_matrix.shape[1]
    q_heads, kv_heads = qw // HEAD_SIZE, kw // HEAD_SIZE
    group = q_heads // kv_heads
    cosine, sine = rotary_tables(rows)

    small = jnp.concatenate(
        [query_weight, key_matrix, value_matrix, output_weight.T, first_gain[:, None], second_gain[:, None],
         jnp.zeros((part, 126), BF16)], axis=1)
    small = lax.all_gather(small, "dp", axis=0, tiled=True)
    qkv_full = small[:, : qw + 2 * kw]
    out_t = small[:, qw + 2 * kw : 2 * qw + 2 * kw]
    gain_first = small[:, 2 * qw + 2 * kw].astype(F32)
    gain_second = small[:, 2 * qw + 2 * kw + 1].astype(F32)
    gate_up = lax.all_gather(jnp.concatenate([gate_weight, up_weight], 0), "dp", axis=1, tiled=True)
    down_full = lax.all_gather(down_weight, "dp", axis=2, tiled=True)
    out_grad_full = lax.all_gather(out_grad, "tensor", axis=0, tiled=True)

    x = inputs.astype(F32)
    normed_local = rms_normed(x, gain_first).astype(BF16)
    normed = lax.all_gather(normed_local, "tensor", axis=0, tiled=True)
    qkv = mm(normed, qkv_full, "sd,dq->sq")
    queries = apply_rotary(qkv[:, :qw].reshape(rows, q_heads, HEAD_SIZE), cosine, sine).astype(BF16)
    keys = apply_rotary(qkv[:, qw : qw + kw].reshape(rows, kv_heads, HEAD_SIZE), cosine, sine).astype(BF16)
    values = qkv[:, qw + kw :].astype(BF16).reshape(rows, kv_heads, HEAD_SIZE)
    queries = queries.reshape(rows, kv_heads, group, HEAD_SIZE)
    scores = mm(queries, keys, "qhgd,khd->hgqk") * ATT_SCALE
    mask = jnp.arange(rows)[:, None] >= jnp.arange(rows)[None, :]
    scores = jnp.where(mask, scores, NEG_FILL)
    terms = jnp.exp(scores - jnp.max(scores, axis=-1, keepdims=True))
    probs = terms / jnp.sum(terms, axis=-1, keepdims=True)
    probs_low = probs.astype(BF16)
    attended = mm(probs_low, values, "hgqk,khd->qhgd").astype(BF16).reshape(rows, qw)
    branch = lax.psum_scatter(
        mm(attended, out_t, "sq,dq->sd").astype(BF16), "tensor", scatter_dimension=0, tiled=True
    ).astype(F32)
    hidden = x + RES_SCALE * branch
    normed_two_local = rms_normed(hidden, gain_second).astype(BF16)
    normed_two = lax.all_gather(normed_two_local, "tensor", axis=0, tiled=True)

    expert_index = rank * experts + jnp.arange(experts, dtype=jnp.int32)
    combined = jnp.sum(
        jnp.where(expert_ids[:, :, None] == expert_index, gate_values[:, :, None], 0.0), axis=1)
    gate_full, up_full = gate_up[:experts], gate_up[experts:]
    gate = mm(normed_two, gate_full, "sd,edf->sef")
    up = mm(normed_two, up_full, "sd,edf->sef")
    sig = jax.nn.sigmoid(gate)
    scale = combined[:, :, None]
    hidden_units = (scale * (gate * sig * up)).astype(BF16)
    moe_partial = mm(hidden_units, down_full, "sef,efd->sd")
    down_grad = mm(hidden_units, out_grad_full, "sef,sd->efd") * RES_SCALE
    hidden_grad = mm(out_grad_full, down_full, "sd,efd->sef") * (RES_SCALE * scale)
    gate_pre = (hidden_grad * up * sig * (1.0 + gate * (1.0 - sig))).astype(BF16)
    up_pre = (hidden_grad * gate * sig).astype(BF16)
    gate_grad = mm(normed_two, gate_pre, "sd,sef->edf")
    up_grad = mm(normed_two, up_pre, "sd,sef->edf")
    rows_grad = mm(gate_pre, gate_full, "sef,edf->sd") + mm(up_pre, up_full, "sef,edf->sd")

    moe_local = lax.psum_scatter(
        moe_partial.astype(BF16), "tensor", scatter_dimension=0, tiled=True).astype(F32)
    block_output = (hidden + RES_SCALE * moe_local).astype(BF16)
    normed_two_grad = lax.psum_scatter(
        rows_grad.astype(BF16), "tensor", scatter_dimension=0, tiled=True).astype(F32)
    _, pull_two = jax.vjp(rms_normed, hidden, gain_second)
    state_norm_grad, second_part = pull_two(normed_two_grad)
    state_grad = out_grad.astype(F32) + state_norm_grad
    branch_grad = lax.all_gather(
        (RES_SCALE * state_grad).astype(BF16), "tensor", axis=0, tiled=True)

    output_part = mm(attended, branch_grad, "sq,sd->qd")
    attended_grad = mm(branch_grad, out_t, "sd,dq->sq").astype(BF16)
    attended_grad = attended_grad.reshape(rows, kv_heads, group, HEAD_SIZE)
    value_grad = mm(probs_low, attended_grad, "hgqk,qhgd->khd")
    weight_grad = mm(attended_grad, values, "qhgd,khd->hgqk")
    inner = jnp.sum(weight_grad * probs, axis=-1, keepdims=True)
    score_grad = (probs * (weight_grad - inner)).astype(BF16)
    query_grad = mm(score_grad, keys, "hgqk,khd->qhgd") * ATT_SCALE
    key_grad = mm(score_grad, queries, "hgqk,qhgd->khd") * ATT_SCALE
    query_pre = apply_rotary(query_grad.reshape(rows, q_heads, HEAD_SIZE), cosine, -sine)
    key_pre = apply_rotary(key_grad, cosine, -sine)
    pre = jnp.concatenate(
        [query_pre.reshape(rows, -1), key_pre.reshape(rows, -1), value_grad.reshape(rows, -1)], axis=1
    ).astype(BF16)
    qkv_part = mm(normed, pre, "sd,sq->dq")
    normed_grad = lax.psum_scatter(
        mm(pre, qkv_full, "sq,dq->sd").astype(BF16), "tensor", scatter_dimension=0, tiled=True).astype(F32)
    _, pull_one = jax.vjp(rms_normed, x, gain_first)
    input_norm_grad, first_part = pull_one(normed_grad)
    input_grad = (state_grad + input_norm_grad).astype(BF16)

    gains = lax.psum(jnp.stack([first_part, second_part], 1), "tensor")
    small_grad = jnp.concatenate(
        [qkv_part, output_part.T, gains, jnp.zeros((width, 126), F32)], axis=1).astype(BF16)
    small_grad = lax.psum_scatter(small_grad, "dp", scatter_dimension=0, tiled=True).astype(F32)
    gate_up_grad = lax.psum_scatter(
        jnp.concatenate([gate_grad.astype(BF16), up_grad.astype(BF16)], 0), "dp", scatter_dimension=1, tiled=True
    ).astype(F32)
    down_grad = lax.psum_scatter(
        down_grad.astype(BF16), "dp", scatter_dimension=2, tiled=True).astype(F32)
    return (
        block_output,
        input_grad,
        small_grad[:, 2 * qw + 2 * kw],
        small_grad[:, :qw],
        small_grad[:, qw : qw + kw],
        small_grad[:, qw + kw : qw + 2 * kw],
        small_grad[:, qw + 2 * kw : 2 * qw + 2 * kw].T,
        small_grad[:, 2 * qw + 2 * kw + 1],
        gate_up_grad[:experts],
        gate_up_grad[experts:],
        down_grad,
    )


def solution(mesh):
    in_specs = (
        P(("dp", "tensor"), None),
        P("dp"),
        P("dp", "tensor"),
        P("dp", "tensor"),
        P("dp", "tensor"),
        P("tensor", "dp"),
        P("dp"),
        P("tensor", "dp", None),
        P("tensor", "dp", None),
        P("tensor", None, "dp"),
        P("dp", None),
        P("dp", None),
        P(("dp", "tensor"), None),
    )
    out_specs = (
        P(("dp", "tensor"), None),
        P(("dp", "tensor"), None),
        P("dp"),
        P("dp", "tensor"),
        P("dp", "tensor"),
        P("dp", "tensor"),
        P("tensor", "dp"),
        P("dp"),
        P("tensor", "dp", None),
        P("tensor", "dp", None),
        P("tensor", None, "dp"),
    )
    return jax.shard_map(local, mesh=mesh, in_specs=in_specs, out_specs=out_specs, check_vma=False)
```

profile of v0, /device:TPU:1, one launch (start us, length us, event | category | flops | bytes accessed | tf_op | source)
XLA Modules:
  0.0 961.2 jit_solution(12869049393805590948)
XLA Ops:
  11.9 47.8 %all-gather.8.cloned.1.call-done = bf16[1024,512]{1,0:T(8,128)(2,1)} async-done(((bf16[64,512]{1,0:T(8,128)(2,1)}), bf16[1024,512]{1,0:T(8,128)(2,1)}) %all-gather.8.cloned.1.call-update) | async-done | bytes 1048592 | tf_op jit(solution)/shard_map/all_gather | solution.py:63
  63.8 47.3 %all-gather.10.cloned.1.call-done = bf16[1024,1024]{1,0:T(8,128)(2,1)} async-done(((bf16[128,1024]{1,0:T(8,128)(2,1)}), bf16[1024,1024]{1,0:T(8,128)(2,1)}) %all-gather.10.cloned.1.call-update) | async-done | bytes 2097168 | tf_op jit(solution)/shard_map/all_gather | solution.py:74
  111.1 2.4 fusion.59
  120.0 2.8 fusion.31
  122.9 3.2 convolution_convert_fusion.1
  127.3 50.6 %reduce-scatter.10.cloned.1.call-done = bf16[128,1024]{1,0:T(8,128)(2,1)} async-done(((bf16[1024,1024]{1,0:T(8,128)(2,1)}), bf16[128,1024]{1,0:T(8,128)(2,1)}) %reduce-scatter.10.cloned.1.call-update) | async-done | bytes 262160 | tf_op jit(solution)/shard_map/reduce_scatter | solution.py:87
  185.3 46.0 %all-gather.18.cloned.1.call-done = bf16[1024,1024]{1,0:T(8,128)(2,1)} async-done(((bf16[128,1024]{1,0:T(8,128)(2,1)}), bf16[1024,1024]{1,0:T(8,128)(2,1)}) %all-gather.18.cloned.1.call-update) | async-done | bytes 2097168 | tf_op jit(solution)/shard_map/all_gather | solution.py:70
  231.3 59.7 %all-gather.16.cloned.1.call-done = bf16[4,512,1024]{1,2,0:T(8,128)(2,1)} async-done(((bf16[4,512,64]{1,2,0:T(8,128)(2,1)}), bf16[4,512,1024]{1,2,0:T(8,128)(2,1)}) %all-gather.16.cloned.1.call-update) | async-done | bytes 4194320 | tf_op jit(solution)/shard_map/all_gather | solution.py:69
  291.0 10.5 %fusion.22 = f32[1024,4,512]{2,0,1:T(8,128)} fusion(bf16[4,512,1024]{1,2,0:T(8,128)(2,1)} %all-gather.16.cloned.1.call-done, bf16[1024,1024]{1,0:T(8,128)(2,1)} %all-gather.18.cloned.1.call-done), kind=kOutput, calls=%fused_computation.37 | convolution fusion | flops 4294967296 | bytes 14680064 | tf_op jit(solution)/shard_map/sd,efd->sef/dot_general | solution.py:42
  301.6 38.8 %all-gather.12.cloned.1.call-done = bf16[1024,1024]{1,0:T(8,128)(2,1)} async-done(((bf16[128,1024]{1,0:T(8,128)(2,1)}), bf16[1024,1024]{1,0:T(8,128)(2,1)}) %all-gather.12.cloned.1.call-update) | async-done | bytes 2097168 | tf_op jit(solution)/shard_map/all_gather | solution.py:92
  340.3 78.1 %all-gather.14.cloned.1.call-done = bf16[8,1024,512]{2,1,0:T(8,128)(2,1)} async-done(((bf16[8,64,512]{2,1,0:T(8,128)(2,1)}), bf16[8,1024,512]{2,1,0:T(8,128)(2,1)}) %all-gather.14.cloned.1.call-update) | async-done | bytes 8388624 | tf_op jit(solution)/shard_map/all_gather | solution.py:68
  418.5 10.7 %fusion.14 = f32[1024,4,512]{2,0,1:T(8,128)} fusion(bf16[8,1024,512]{2,1,0:T(8,128)(2,1)} %all-gather.14.cloned.1.call-done, bf16[1024,1024]{1,0:T(8,128)(2,1)} %all-gather.12.cloned.1.call-done), kind=kOutput, calls=%fused_computation.29 | convolution fusion | flops 4294967296 | bytes 14680064 | tf_op jit(solution)/shard_map/sd,edf->sef/dot_general | solution.py:42
  429.2 15.1 %multiply_convert_fusion.2 = (bf16[1024,4,512]{2,0,1:T(8,128)(2,1)S(1)}, bf16[1024,4,512]{2,0,1:T(8,128)(2,1)}, bf16[1024,4,512]{2,0,1:T(8,128)(2,1)}) fusion(f32[1024,4,512]{2,0,1:T(8,128)} %fusion.14, f32[1024,4,512]{2,0,1:T(8,128)} %fusion.22, f32[1024,4]{0,1:T(4,128)S(1)} %broadcast_multiply_fusion, f32[1024,4]{0,1:T(4,128)S(1)} %select_reduce_fusion, ...), kind=kOutput, calls=%fused_computation.9 | convolution fusion | flops 4332716032 | bytes 35684352 | tf_op jit(solution)/shard_map/sd,edf->sef/dot_general | solution.py:42
  444.3 9.1 fusion.12
  453.5 5.8 fusion.7
  459.3 47.6 %reduce-scatter.14.cloned.1.call-done = bf16[128,1024]{1,0:T(8,128)(2,1)} async-done(((bf16[1024,1024]{1,0:T(8,128)(2,1)}), bf16[128,1024]{1,0:T(8,128)(2,1)}) %reduce-scatter.14.cloned.1.call-update) | async-done | bytes 262160 | tf_op jit(solution)/shard_map/reduce_scatter | solution.py:115
  512.0 51.8 %all-gather.20.cloned.1.call-done = bf16[1024,1024]{1,0:T(8,128)(2,1)} async-done(((bf16[128,1024]{1,0:T(8,128)(2,1)}), bf16[1024,1024]{1,0:T(8,128)(2,1)}) %all-gather.20.cloned.1.call-update) | async-done | bytes 2097168 | tf_op jit(solution)/shard_map/all_gather | solution.py:120
  566.3 5.8 fusion
  572.2 2.8 fusion.6
  577.2 2.9 fusion.42
  583.3 9.6 %multiply_convert_fusion = bf16[4,512,1024]{1,2,0:T(8,128)(2,1)} fusion(bf16[1024,4,512]{2,0,1:T(8,128)(2,1)} %get-tuple-element.63, bf16[1024,1024]{1,0:T(8,128)(2,1)} %all-gather.18.cloned.1.call-done), kind=kOutput, calls=%fused_computation.7 | convolution fusion | flops 4299161600 | bytes 10485760 | tf_op jit(solution)/shard_map/sef,sd->efd/dot_general | solution.py:42
  593.0 9.5 bitcast_convert_fusion
  602.8 8.6 convert_bitcast_fusion
  611.4 6.2 convert_bitcast_fusion.1
  617.5 7.5 pad_maximum_fusion
  625.0 12.7 %copy.84 = bf16[8,1024,512]{2,0,1:T(8,128)(2,1)} copy(bf16[8,1024,512]{1,2,0:T(8,128)(2,1)} %pad_maximum_fusion) | data formatting | bytes 16777216 | tf_op jit(solution)/shard_map/concatenate | solution.py:149
  638.6 3.1 convolution_convert_fusion.2
  644.2 15.5 %psum.7 = bf16[1024,2]{0,1:T(2,128)(2,1)S(1)} all-reduce(f32[1024,2]{0,1:T(2,128)S(1)} %pad_maximum_fusion.9), channel_id=1, replica_groups=mesh['dp'=16,'tensor'=8] {'tensor'}, use_global_device_ids=true, to_apply=%region_14.15 | all-reduce | flops 2048 | bytes 12288 | tf_op jit(solution)/shard_map/psum | solution.py:144
  662.4 57.7 %reduce-scatter.20.cloned.1.call-done = bf16[4,512,64]{1,2,0:T(8,128)(2,1)} async-done(((bf16[4,512,1024]{1,2,0:T(8,128)(2,1)}), bf16[4,512,64]{1,2,0:T(8,128)(2,1)}) %reduce-scatter.20.cloned.1.call-update) | async-done | bytes 262160 | tf_op jit(solution)/shard_map/reduce_scatter | solution.py:151
  721.9 51.0 %reduce-scatter.12.cloned.1.call-done = bf16[128,1024]{1,0:T(8,128)(2,1)} async-done(((bf16[1024,1024]{1,0:T(8,128)(2,1)}), bf16[128,1024]{1,0:T(8,128)(2,1)}) %reduce-scatter.12.cloned.1.call-update) | async-done | bytes 262160 | tf_op jit(solution)/shard_map/reduce_scatter | solution.py:112
  775.1 105.8 %reduce-scatter.18.cloned.1.call-done = bf16[8,64,512]{2,0,1:T(8,128)(2,1)} async-done(((bf16[8,1024,512]{2,0,1:T(8,128)(2,1)}), bf16[8,64,512]{2,0,1:T(8,128)(2,1)}) %reduce-scatter.18.cloned.1.call-update) | async-done | bytes 524304 | tf_op jit(solution)/shard_map/reduce_scatter | solution.py:148
  884.3 65.8 %reduce-scatter.22.cloned.1.call-done = bf16[64,512]{1,0:T(8,128)(2,1)} async-done(((bf16[1024,512]{1,0:T(8,128)(2,1)}), bf16[64,512]{1,0:T(8,128)(2,1)}) %reduce-scatter.22.cloned.1.call-update) | async-done | bytes 65552
  (165 shorter events, 54.7 us)
Async XLA Ops:
  7.2 52.5 %all-gather.8.cloned.1.call-start = ((), (), s32[]{:S(2)}) async-start(), calls=%async_computation.7 | async-start | bytes 1114112 | tf_op jit(solution)/shard_map/all_gather | solution.py:63
  10.3 100.8 %all-gather.10.cloned.1.call-start = ((), (), s32[]{:S(2)}) async-start(), calls=%async_computation.8 | async-start | bytes 2359296 | tf_op jit(solution)/shard_map/all_gather | solution.py:74
  11.9 101.6 %copy-start.22 = (f32[128]{0:T(128)}, f32[128]{0:T(128)S(1)}, u32[]{:S(2)}) copy-start(f32[128]{0:T(128)S(1)} %fusion.88) | copy-start | bytes 1540
  61.0 52.5 %copy-start.13 = (f32[1024]{0:T(1024)}, f32[1024]{0:T(1024)S(1)}, u32[]{:S(2)}) copy-start(f32[1024]{0:T(1024)S(1)} %get-tuple-element.55) | copy-start | bytes 12292
  62.8 115.1 %reduce-scatter.10.cloned.1.call-start = ((), (), s32[]{:S(2)}) async-start(), calls=%async_computation.9 | async-start | bytes 2359296 | tf_op jit(solution)/shard_map/reduce_scatter | solution.py:87
  62.9 53.2 %copy-start.20 = (f32[32]{0:T(128)}, f32[32]{0:T(128)S(1)}, u32[]{:S(2)}) copy-start(f32[32]{0:T(128)S(1)} %negate_power_fusion) | copy-start | bytes 388
  122.9 60.9 %copy-start.9 = (bf16[64,2,1024]{2,0,1:T(8,128)(2,1)}, bf16[64,2,1024]{2,0,1:T(8,128)(2,1)S(1)}, u32[]{:S(2)}) copy-start(bf16[64,2,1024]{2,0,1:T(8,128)(2,1)S(1)} %fusion.31) | copy-start | bytes 786436
  122.9 55.0 %copy-start.1 = (bf16[128,1024]{1,0:T(8,128)(2,1)S(1)}, bf16[128,1024]{1,0:T(8,128)(2,1)}, u32[]{:S(2)}) copy-start(bf16[128,1024]{1,0:T(8,128)(2,1)} %param.13) | copy-start | bytes 786436
  122.9 59.1 %copy-start.12 = (bf16[4,64,512]{2,1,0:T(8,128)(2,1)S(1)}, bf16[4,64,512]{2,1,0:T(8,128)(2,1)}, u32[]{:S(2)}) copy-start(bf16[4,64,512]{2,1,0:T(8,128)(2,1)} %param.21) | copy-start | bytes 786436
  126.1 105.2 %all-gather.18.cloned.1.call-start = ((), (), s32[]{:S(2)}) async-start(), calls=%async_computation.14 | async-start | bytes 2359296 | tf_op jit(solution)/shard_map/all_gather | solution.py:70
  126.7 164.3 %all-gather.16.cloned.1.call-start = ((), (), s32[]{:S(2)}) async-start(), calls=%async_computation.12 | async-start | bytes 4456448 | tf_op jit(solution)/shard_map/all_gather | solution.py:69
  127.3 213.0 %all-gather.12.cloned.1.call-start = ((), (), s32[]{:S(2)}) async-start(), calls=%async_computation.10 | async-start | bytes 2359296 | tf_op jit(solution)/shard_map/all_gather | solution.py:92
  181.9 236.5 %all-gather.14.cloned.1.call-start = ((), (), s32[]{:S(2)}) async-start(), calls=%async_computation.11 | async-start | bytes 8912896 | tf_op jit(solution)/shard_map/all_gather | solution.py:68
  183.8 323.1 %reduce-scatter.14.cloned.1.call-start = ((), (), s32[]{:S(2)}) async-start(), calls=%async_computation.15 | async-start | bytes 2359296 | tf_op jit(solution)/shard_map/reduce_scatter | solution.py:115
  418.5 10.7 %copy-start.30 = (bf16[1024,1024]{1,0:T(8,128)(2,1)S(1)}, bf16[1024,1024]{1,0:T(8,128)(2,1)}, u32[]{:S(2)}) copy-start(bf16[1024,1024]{1,0:T(8,128)(2,1)} %all-gather.12.cloned.1.call-done) | copy-start | bytes 6291460
  444.3 9.2 copy-start.29
  453.4 53.5 %copy-start.3 = (bf16[128,1024]{1,0:T(8,128)(2,1)S(1)}, bf16[128,1024]{1,0:T(8,128)(2,1)}, u32[]{:S(2)}) copy-start(bf16[128,1024]{1,0:T(8,128)(2,1)} %reduce-scatter.10.cloned.1.call-done) | copy-start | bytes 786436
  453.4 56.4 %copy-start.6 = (bf16[128,1024]{1,0:T(8,128)(2,1)S(1)}, bf16[128,1024]{1,0:T(8,128)(2,1)}, u32[]{:S(2)}) copy-start(bf16[128,1024]{1,0:T(8,128)(2,1)} %param.25) | copy-start | bytes 786436
  459.3 104.6 %all-gather.20.cloned.1.call-start = ((), (), s32[]{:S(2)}) async-start(), calls=%async_computation.16 | async-start | bytes 2359296 | tf_op jit(solution)/shard_map/all_gather | solution.py:120
  511.8 131.1 %reduce-scatter.16.cloned.1.call-start = ((), (), s32[]{:S(2)}) async-start(), calls=%async_computation.17 | async-start | bytes 2359296 | tf_op jit(solution)/shard_map/reduce_scatter | solution.py:138
  583.0 137.1 %reduce-scatter.20.cloned.1.call-start = ((), (), s32[]{:S(2)}) async-start(), calls=%async_computation.19 | async-start | bytes 4456448 | tf_op jit(solution)/shard_map/reduce_scatter | solution.py:151
  592.9 9.9 %copy-start.31 = (bf16[1024,1024]{1,0:T(8,128)(2,1)S(1)}, bf16[1024,1024]{1,0:T(8,128)(2,1)}, u32[]{:S(2)}) copy-start(bf16[1024,1024]{1,0:T(8,128)(2,1)} %all-gather.12.cloned.1.call-done) | copy-start | bytes 6291460
  592.9 180.0 %reduce-scatter.12.cloned.1.call-start = ((), (), s32[]{:S(2)}) async-start(), calls=%async_computation.13 | async-start | bytes 2359296 | tf_op jit(solution)/shard_map/reduce_scatter | solution.py:112
  602.5 278.5 %reduce-scatter.18.cloned.1.call-start = ((), (), s32[]{:S(2)}) async-start(), calls=%async_computation.18 | async-start | bytes 8912896 | tf_op jit(solution)/shard_map/reduce_scatter | solution.py:148
  637.8 312.3 %reduce-scatter.22.cloned.1.call-start = ((), (), s32[]{:S(2)}) async-start(), calls=%async_computation.20 | async-start | bytes 1114112
  641.7 80.2 %copy-start.27 = (f32[128]{0:T(128)S(1)}, f32[128]{0:T(128)}, u32[]{:S(2)}) copy-start(f32[128]{0:T(128)} %copy-done.26) | copy-start | bytes 1540
  641.7 131.2 %copy-start.4 = (bf16[128,1024]{1,0:T(8,128)(2,1)S(1)}, bf16[128,1024]{1,0:T(8,128)(2,1)}, u32[]{:S(2)}) copy-start(bf16[128,1024]{1,0:T(8,128)(2,1)} %reduce-scatter.10.cloned.1.call-done) | copy-start | bytes 786436
  641.7 131.2 %copy-start.7 = (bf16[128,1024]{1,0:T(8,128)(2,1)S(1)}, bf16[128,1024]{1,0:T(8,128)(2,1)}, u32[]{:S(2)}) copy-start(bf16[128,1024]{1,0:T(8,128)(2,1)} %param.25) | copy-start | bytes 786436
  641.7 131.2 %copy-start.8 = (bf16[128,1024]{1,0:T(8,128)(2,1)S(1)}, bf16[128,1024]{1,0:T(8,128)(2,1)}, u32[]{:S(2)}) copy-start(bf16[128,1024]{1,0:T(8,128)(2,1)} %reduce-scatter.14.cloned.1.call-done) | copy-start | bytes 786436
  641.7 131.2 %copy-start.19 = (f32[128]{0:T(128)S(1)}, f32[128]{0:T(128)}, u32[]{:S(2)}) copy-start(f32[128]{0:T(128)} %copy-done.18) | copy-start | bytes 1540
  641.7 131.2 %copy-start.25 = (f32[128]{0:T(128)S(1)}, f32[128]{0:T(128)}, u32[]{:S(2)}) copy-start(f32[128]{0:T(128)} %copy-done.24) | copy-start | bytes 1540
  642.9 130.1 %copy-start.11 = (bf16[128,1024]{1,0:T(8,128)(2,1)S(1)}, bf16[128,1024]{1,0:T(8,128)(2,1)}, u32[]{:S(2)}) copy-start(bf16[128,1024]{1,0:T(8,128)(2,1)} %reduce-scatter.16.cloned.1.call-done) | copy-start | bytes 786436
  (20 other events, 74.2 us)
Sparse Core Ops, SparseCore 0:
  11.1 48.5 all-gather.7
  63.0 48.1 all-gather.9
  126.2 51.6 reduce-scatter.9
  179.4 51.8 all-gather.17
  233.6 57.3 all-gather.15
  293.1 47.1 all-gather.11
  343.4 75.0 all-gather.13
  459.4 47.4 reduce-scatter.13
  511.9 51.8 all-gather.19
  583.1 51.7 reduce-scatter.15
  638.9 81.1 reduce-scatter.19
  722.5 50.3 reduce-scatter.11
  777.8 103.1 reduce-scatter.17
  885.1 64.9 reduce-scatter.21
where the time goes:
time: 970 us; the launch traced here: 961 us
  waiting for transfers between devices  749 us (77%)
  matrix products  115 us (12%)
  other arithmetic  35.2 us (4%)
  local copies, waits for them, and re-layouts  29.6 us (3%)
  blocking collectives  15.5 us (2%)
  between operations  14.8 us (2%)
    dot_general x21, matrix products, mm(): return jnp.einsum(spec, a, b, preferred_element_type=F32)  115 us
    reduce_scatter x1, waiting for transfers between devices, local(): lax.psum_scatter(jnp.concatenate([gate_grad.astype(BF16), up_grad.astype(...  106 us
    all_gather x1, waiting for transfers between devices, local(): lax.all_gather(jnp.concatenate([gate_weight, up_weight], 0), 'dp', axis=1...  78.1 us
    unnamed x15, waiting for transfers between devices  67 us
    all_gather x1, waiting for transfers between devices, local(): down_full = lax.all_gather(down_weight, 'dp', axis=2, tiled=True)  59.7 us
    reduce_scatter x1, waiting for transfers between devices, local(): lax.psum_scatter(down_grad.astype(BF16), 'dp', scatter_dimension=2, tiled...  57.7 us
    all_gather x1, waiting for transfers between devices, local(): lax.all_gather((RES_SCALE * state_grad).astype(BF16), 'tensor', axis=0, t...  51.8 us
    reduce_scatter x1, waiting for transfers between devices, local(): lax.psum_scatter(moe_partial.astype(BF16), 'tensor', scatter_dimension=0,...  51 us
  transfers between devices with their start and end apart: 14, of which 13 were waited for; matrix products, arithmetic and copies ran while one was open for 9% of the time, Pallas kernels for 0%

commit v1 on v0

v1 whole, which is shorter than its diff:
```python
import functools

import jax
import jax.numpy as jnp
from jax import lax
from jax.experimental import pallas as pl
from jax.experimental.pallas import tpu as pltpu
from jax.sharding import PartitionSpec as P

HEAD_SIZE = 64
NORM_EPSILON = 1e-06
ATT_SCALE = 0.015625
RES_SCALE = 0.22
ROPE_BASE = 10000.0
NEG_FILL = -1e30
F32 = jnp.float32
BF16 = jnp.bfloat16
MESH = pl.DeviceIdType.MESH
NX, NY, NZ, NCORE = 4, 2, 4, 2
ROWS, WIDTH, PART, UNITS = 128, 1024, 64, 512
ANY = pl.BlockSpec(memory_space=pl.ANY)
VMEM = pl.BlockSpec(memory_space=pltpu.VMEM)
DMA = pltpu.SemaphoreType.DMA


class Place:
    def __init__(self):
        d, t = lax.axis_index("dp"), lax.axis_index("tensor")
        self.d, self.t = d, t
        self.tx, self.ty = t // NY, t % NY
        self.dy, self.dz, self.dc = d // (NZ * NCORE), (d // NCORE) % NZ, d % NCORE
        self.pair = self.tx * NY + (1 - self.ty)
        self.d_pair = self.dp(1 - self.dy, self.dz, self.dc)

    def dp(self, y, z, core):
        return (y * NZ + z) * NCORE + core

    def tensor_pair(self):
        return (self.d, self.pair)

    def x(self, j):
        return (self.tx + j) % NX

    def x_dev(self, j):
        return (self.d, self.x(j) * NY + self.ty)

    def z(self, j):
        return (self.dz + j) % NZ

    def z_dev(self, j):
        return (self.dp(self.dy, self.z(j), self.dc), self.t)

    def y_dev(self):
        return (self.d_pair, self.t)

    def core_dev(self):
        return (self.dp(self.dy, self.dz, 1 - self.dc), self.t)


def meet(p):
    barrier = pltpu.get_barrier_semaphore()
    others = [p.tensor_pair(), p.y_dev(), p.core_dev()]
    others += [p.x_dev(j) for j in range(1, NX)] + [p.z_dev(j) for j in range(1, NZ)]
    for other in others:
        pl.semaphore_signal(barrier, inc=1, device_id=other, device_id_type=MESH)
    pl.semaphore_wait(barrier, len(others))


def push(src, dst, sems, number, device):
    copy = pltpu.make_async_remote_copy(
        src_ref=src, dst_ref=dst, send_sem=sems[0].at[number], recv_sem=sems[1].at[number],
        device_id=device, device_id_type=MESH)
    copy.start()
    return copy


def sems(number):
    return [DMA((number,)), DMA((number,))]


class TensorGather:
    SEMS = 7

    def __init__(self, p, src, out, sem, local_sem):
        self.p, self.out, self.sem = p, out, sem
        self.copies = [push(src, out.at[p.t], sem, 0, p.tensor_pair())]
        self.copies += [push(src, out.at[p.t], sem, j, p.x_dev(j)) for j in range(1, NX)]
        self.own = pltpu.make_async_copy(src, out.at[p.t], local_sem)
        self.own.start()

    def forward(self):
        p = self.p
        self.copies[0].wait_recv()
        self.copies += [
            push(self.out.at[p.pair], self.out.at[p.pair], self.sem, 3 + j, p.x_dev(j)) for j in range(1, NX)]

    def finish(self):
        for copy in self.copies[1:]:
            copy.wait_recv()
        for copy in self.copies:
            copy.wait_send()
        self.own.wait()


class TensorScatter:
    SEMS = 7

    @staticmethod
    def scratch():
        return [pltpu.VMEM((NX, NY, ROWS, WIDTH), BF16), pltpu.VMEM((2, ROWS, WIDTH), BF16)] + sems(7) + [DMA((1,))]

    def __init__(self, p, partial, got, pair_buf, send, recv, local):
        self.p, self.got, self.pair_buf = p, got, pair_buf
        self.sem = (send, recv)
        self.copies = []
        for half, c in enumerate((1 - p.ty, p.ty)):
            self.copies.append([
                push(partial.at[p.x(j) * NY + c], got.at[j, c], self.sem, half * 3 + j - 1, p.x_dev(j))
                for j in range(1, NX)])
        self.own = pltpu.make_async_copy(partial.at[pl.ds(p.tx * NY, NY)], got.at[0], local.at[0])
        self.own.start()

    def total(self, c, rows):
        value = self.got[0, c, rows].astype(F32)
        for j in range(1, NX):
            value = value + self.got[j, c, rows].astype(F32)
        return value

    def exchange(self):
        p = self.p
        self.own.wait()
        for copy in self.copies[0]:
            copy.wait_recv()

        def step(i, carry):
            rows = pl.ds(pl.multiple_of(i * 32, 32), 32)
            self.pair_buf[0, rows] = self.total(1 - p.ty, rows).astype(BF16)
            return carry

        lax.fori_loop(0, ROWS // 32, step, 0)
        self.pair = push(self.pair_buf.at[0], self.pair_buf.at[1], self.sem, 6, p.tensor_pair())

    def arrive(self):
        for copy in self.copies[1]:
            copy.wait_recv()
        self.pair.wait_recv()

    def rows(self, rows):
        return self.total(self.p.ty, rows) + self.pair_buf[1, rows].astype(F32)

    def finish(self):
        for copy in self.copies[0] + self.copies[1] + [self.pair]:
            copy.wait_send()


class PartGather:
    SEMS = 15

    def __init__(self, p, shard, out, sem, local_sem):
        self.p, self.out, self.sem = p, out, sem
        mine = out.at[:, p.d]
        self.pair = push(shard, mine, sem, 0, p.y_dev())
        self.along = [push(shard, mine, sem, j, p.z_dev(j)) for j in range(1, NZ)]
        self.core = [push(shard, mine, sem, 4, p.core_dev())]
        self.own = pltpu.make_async_copy(shard, mine, local_sem)
        self.own.start()

    def resend(self, index, number, device):
        return push(self.out.at[:, index], self.out.at[:, index], self.sem, number, device)

    def forward(self):
        p = self.p
        self.pair.wait_recv()
        self.along_pair = [self.resend(p.d_pair, 4 + j, p.z_dev(j)) for j in range(1, NZ)]
        self.core.append(self.resend(p.d_pair, 8, p.core_dev()))

    def spread(self):
        p = self.p
        for first, copies, y in ((9, self.along, p.dy), (12, self.along_pair, 1 - p.dy)):
            for j in range(1, NZ):
                copies[j - 1].wait_recv()
                index = p.dp(y, (p.dz + NZ - j) % NZ, p.dc)
                self.core.append(self.resend(index, first + j - 1, p.core_dev()))

    def finish(self):
        for copy in self.core:
            copy.wait_recv()
        for copy in [self.pair] + self.along + self.along_pair + self.core:
            copy.wait_send()
        self.own.wait()


class PartScatter:
    SEMS = 5

    @staticmethod
    def scratch(n):
        return [
            pltpu.VMEM((n, 2, NZ, PART, UNITS), BF16),
            pltpu.VMEM((n, 2, NZ, PART, UNITS), BF16),
            pltpu.VMEM((NZ, n, 2, PART, UNITS), BF16),
            pltpu.VMEM((2, n, PART, UNITS), BF16),
        ] + sems(5) + [DMA((1,))]

    def __init__(self, p, grads, own, core_buf, z_buf, y_buf, send, recv, local):
        self.p, self.n = p, grads.shape[0]
        self.own, self.core_buf, self.z_buf, self.y_buf = own, core_buf, z_buf, y_buf
        self.sem = (send, recv)
        self.core = push(grads.at[:, :, :, 1 - p.dc], core_buf, self.sem, 0, p.core_dev())
        self.load = pltpu.make_async_copy(grads.at[:, :, :, p.dc], own, local.at[0])
        self.load.start()

    def along(self):
        p = self.p
        self.load.wait()
        self.core.wait_recv()

        def step(i, carry):
            for y in range(2):
                for z in range(NZ):
                    total = self.own[i, y, z].astype(F32) + self.core_buf[i, y, z].astype(F32)
                    self.own[i, y, z] = total.astype(BF16)
            return carry

        lax.fori_loop(0, self.n, step, 0)
        self.z_copies = [
            push(self.own.at[:, :, p.z(j)], self.z_buf.at[j], self.sem, j, p.z_dev(j)) for j in range(1, NZ)]

    def total(self, i, y):
        value = self.own[i, y, self.p.dz].astype(F32)
        for j in range(1, NZ):
            value = value + self.z_buf[j, i, y].astype(F32)
        return value

    def pair(self):
        p = self.p
        for copy in self.z_copies:
            copy.wait_recv()

        def step(i, carry):
            self.y_buf[0, i] = self.total(i, 1 - p.dy).astype(BF16)
            return carry

        lax.fori_loop(0, self.n, step, 0)
        self.y_copy = push(self.y_buf.at[0], self.y_buf.at[1], self.sem, 4, p.y_dev())

    def finish(self, out):
        p = self.p
        self.y_copy.wait_recv()

        def step(i, carry):
            out[i] = self.total(i, p.dy) + self.y_buf[1, i].astype(F32)
            return carry

        lax.fori_loop(0, self.n, step, 0)
        for copy in [self.core, self.y_copy] + self.z_copies:
            copy.wait_send()


def params(number, megabytes):
    return pltpu.CompilerParams(
        collective_id=number, has_side_effects=True, vmem_limit_bytes=megabytes << 20)


def shape(dims, dtype=BF16):
    return jax.ShapeDtypeStruct(dims, dtype)


def first_kernel(x, small, gate, x_out, small_out, gate_out, ts, tr, ss, sr, gs, gr, local):
    p = Place()
    meet(p)
    small_gather = PartGather(p, small, small_out, (ss, sr), local.at[1])
    rows = TensorGather(p, x, x_out, (ts, tr), local.at[0])
    gates = PartGather(p, gate, gate_out, (gs, gr), local.at[2])
    small_gather.forward()
    rows.forward()
    small_gather.spread()
    gates.forward()
    gates.spread()
    small_gather.finish()
    rows.finish()
    gates.finish()


def second_kernel(partial, x, gain, up, down, hidden, normed_out, up_out, down_out, normed, *scratch):
    p = Place()
    meet(p)
    us, ur, ds, dr, ts, tr, local = scratch[-7:]
    branch = TensorScatter(p, partial, *scratch[:5])
    ups = PartGather(p, up, up_out, (us, ur), local.at[1])
    branch.exchange()
    downs = PartGather(p, down, down_out, (ds, dr), local.at[2])
    ups.forward()
    branch.arrive()

    def step(i, carry):
        rows = pl.ds(pl.multiple_of(i * 32, 32), 32)
        state = x[rows].astype(F32) + RES_SCALE * branch.rows(rows)
        hidden[rows] = state
        scale = lax.rsqrt(jnp.mean(state * state, axis=-1, keepdims=True) + NORM_EPSILON)
        normed[rows] = (state * scale * gain[...]).astype(BF16)
        return carry

    lax.fori_loop(0, ROWS // 32, step, 0)
    gather = TensorGather(p, normed, normed_out, (ts, tr), local.at[0])
    downs.forward()
    gather.forward()
    ups.spread()
    downs.spread()
    branch.finish()
    gather.finish()
    ups.finish()
    downs.finish()


def norm_pull(state, gain, grad):
    r = lax.rsqrt(jnp.mean(state * state, axis=-1, keepdims=True) + NORM_EPSILON)
    u = state * r
    w = gain * grad
    return r * (w - u * jnp.mean(w * u, axis=-1, keepdims=True)), jnp.sum(grad * u, axis=0, keepdims=True)


def third_kernel(
    partial, gate_grads, up_grads, hidden, gain, out_grad,
    branch_out, state_grad, gain_part, gate_out, up_out, branch, *scratch,
):
    p = Place()
    meet(p)
    ts, tr, local = scratch[-3:]
    rows_sum = TensorScatter(p, partial, *scratch[:5])
    gates = PartScatter(p, gate_grads, *scratch[5:12])
    ups = PartScatter(p, up_grads, *scratch[12:19])
    gates.along()
    ups.along()
    rows_sum.exchange()
    rows_sum.arrive()
    gain_part[...] = jnp.zeros_like(gain_part)

    def step(i, carry):
        rows = pl.ds(pl.multiple_of(i * 32, 32), 32)
        pulled, part = norm_pull(hidden[rows], gain[...], rows_sum.rows(rows))
        gain_part[0:1] += part
        state = out_grad[rows].astype(F32) + pulled
        state_grad[rows] = state
        branch[rows] = (RES_SCALE * state).astype(BF16)
        return carry

    lax.fori_loop(0, ROWS // 32, step, 0)
    gather = TensorGather(p, branch, branch_out, (ts, tr), local.at[0])
    gather.forward()
    gates.pair()
    ups.pair()
    rows_sum.finish()
    gates.finish(gate_out)
    ups.finish(up_out)
    gather.finish()


def fourth_kernel(
    partial, down_grads, small_grads, x, gain, state_grad, second_part,
    input_grad, down_out, small_out, gains, gain_buf, *scratch,
):
    p = Place()
    meet(p)
    gs, gr = scratch[-2:]
    rows_sum = TensorScatter(p, partial, *scratch[:5])
    smalls = PartScatter(p, small_grads, *scratch[5:12])
    downs = PartScatter(p, down_grads, *scratch[12:19])
    smalls.along()
    downs.along()
    rows_sum.exchange()
    rows_sum.arrive()
    gains[...] = jnp.zeros_like(gains)
    gains[1:2] = second_part[0:1]

    def step(i, carry):
        rows = pl.ds(pl.multiple_of(i * 32, 32), 32)
        pulled, part = norm_pull(x[rows].astype(F32), gain[...], rows_sum.rows(rows))
        gains[0:1] += part
        input_grad[rows] = (state_grad[rows] + pulled).astype(BF16)
        return carry

    lax.fori_loop(0, ROWS // 32, step, 0)

    number = 0
    copies = []
    stages = (
        [p.x_dev(j) for j in range(1, NX)], [p.tensor_pair()], [p.core_dev()],
        [p.z_dev(j) for j in range(1, NZ)], [p.y_dev()])
    between = (smalls.pair, downs.pair, None, None, None)
    for stage, (devices, work) in enumerate(zip(stages, between)):
        gain_buf[9 + stage] = gains[...]
        now = [push(gain_buf.at[9 + stage], gain_buf.at[number + k], (gs, gr), number + k, device)
               for k, device in enumerate(devices)]
        if work is not None:
            work()
        for k, copy in enumerate(now):
            copy.wait_recv()
            gains[...] += gain_buf[number + k]
        number += len(devices)
        copies += now
    rows_sum.finish()
    smalls.finish(small_out)
    downs.finish(down_out)
    for copy in copies:
        copy.wait_send()


def first(x, small, gate):
    return pl.pallas_call(
        first_kernel,
        out_shape=(shape((8, ROWS, WIDTH)), shape((1, 16, PART, UNITS)), shape((4, 16, PART, UNITS))),
        in_specs=[ANY] * 3, out_specs=(ANY,) * 3,
        scratch_shapes=sems(7) + sems(15) + sems(15) + [DMA((3,))],
        compiler_params=params(1, 32), name="first",
    )(x, small, gate)


def second(partial, x, gain, up, down):
    full = shape((4, 16, PART, UNITS))
    return pl.pallas_call(
        second_kernel,
        out_shape=(shape((ROWS, WIDTH), F32), shape((8, ROWS, WIDTH)), full, full),
        in_specs=[ANY, VMEM, VMEM, ANY, ANY], out_specs=(VMEM, ANY, ANY, ANY),
        scratch_shapes=[pltpu.VMEM((ROWS, WIDTH), BF16)] + TensorScatter.scratch()
        + sems(15) + sems(15) + sems(7) + [DMA((3,))],
        compiler_params=params(2, 32), name="second",
    )(partial, x, gain, up, down)


def third(partial, gate_grads, up_grads, hidden, gain, out_grad):
    return pl.pallas_call(
        third_kernel,
        out_shape=(
            shape((8, ROWS, WIDTH)), shape((ROWS, WIDTH), F32), shape((8, WIDTH), F32),
            shape((4, PART, UNITS), F32), shape((4, PART, UNITS), F32)),
        in_specs=[ANY, ANY, ANY, VMEM, VMEM, VMEM], out_specs=(ANY,) + (VMEM,) * 4,
        scratch_shapes=[pltpu.VMEM((ROWS, WIDTH), BF16)] + TensorScatter.scratch()
        + PartScatter.scratch(4) + PartScatter.scratch(4) + sems(7) + [DMA((1,))],
        compiler_params=params(3, 48), name="third",
    )(partial, gate_grads, up_grads, hidden, gain, out_grad)


def fourth(partial, down_grads, small_grads, x, gain, state_grad, second_part):
    return pl.pallas_call(
        fourth_kernel,
        out_shape=(
            shape((ROWS, WIDTH)), shape((4, PART, UNITS), F32), shape((1, PART, UNITS), F32),
            shape((8, WIDTH), F32)),
        in_specs=[ANY, ANY, ANY, VMEM, VMEM, VMEM, VMEM], out_specs=(VMEM,) * 4,
        scratch_shapes=[pltpu.VMEM((14, 8, WIDTH), F32)] + TensorScatter.scratch()
        + PartScatter.scratch(1) + PartScatter.scratch(4) + sems(9),
        compiler_params=params(4, 48), name="fourth",
    )(partial, down_grads, small_grads, x, gain, state_grad, second_part)


def rms_normed(activations, gain_vector):
    return (
        activations
        * lax.rsqrt(jnp.mean(activations * activations, axis=-1, keepdims=True) + NORM_EPSILON)
        * gain_vector
    )


def rotary_tables(length):
    half_width = HEAD_SIZE // 2
    positions = jnp.arange(length).astype(F32)
    frequencies = jnp.power(ROPE_BASE, -(jnp.arange(half_width).astype(F32) * 2.0 / HEAD_SIZE))
    angles = positions[:, None] * frequencies[None, :]
    return (jnp.cos(angles)[:, None, :], jnp.sin(angles)[:, None, :])


def apply_rotary(head_data, cosine, sine):
    half_width = head_data.shape[-1] // 2
    first_half = head_data[..., :half_width]
    second_half = head_data[..., half_width:]
    return jnp.concatenate(
        [first_half * cosine - second_half * sine, second_half * cosine + first_half * sine], axis=-1
    )


def mm(a, b, spec):
    return jnp.einsum(spec, a, b, preferred_element_type=F32)


def local(
    inputs, first_gain, query_weight, key_matrix, value_matrix, output_weight, second_gain,
    gate_weight, up_weight, down_weight, expert_ids, gate_values, out_grad,
):
    rank = lax.axis_index("tensor")
    rows = inputs.shape[0] * lax.axis_size("tensor")
    experts = gate_weight.shape[0]
    qw = query_weight.shape[1]
    kw = key_matrix.shape[1]
    q_heads, kv_heads = qw // HEAD_SIZE, kw // HEAD_SIZE
    group = q_heads // kv_heads
    cosine, sine = rotary_tables(rows)

    small = jnp.concatenate(
        [query_weight, key_matrix, value_matrix, output_weight.T, first_gain[:, None], second_gain[:, None],
         jnp.zeros((PART, 126), BF16)], axis=1)
    x_full, small, gate_full = first(inputs, small[None], gate_weight)
    out_grad_full = lax.all_gather(out_grad, "tensor", axis=0, tiled=True)
    small = small.reshape(WIDTH, UNITS)
    gate_full = gate_full.reshape(experts, WIDTH, UNITS)
    qkv_full = small[:, : qw + 2 * kw]
    out_t = small[:, qw + 2 * kw : 2 * qw + 2 * kw]
    gain_first = small[:, 2 * qw + 2 * kw].astype(F32)
    gain_second = small[:, 2 * qw + 2 * kw + 1].astype(F32)

    normed = rms_normed(x_full.reshape(rows, WIDTH).astype(F32), gain_first).astype(BF16)
    qkv = mm(normed, qkv_full, "sd,dq->sq")
    queries = apply_rotary(qkv[:, :qw].reshape(rows, q_heads, HEAD_SIZE), cosine, sine).astype(BF16)
    keys = apply_rotary(qkv[:, qw : qw + kw].reshape(rows, kv_heads, HEAD_SIZE), cosine, sine).astype(BF16)
    values = qkv[:, qw + kw :].astype(BF16).reshape(rows, kv_heads, HEAD_SIZE)
    queries = queries.reshape(rows, kv_heads, group, HEAD_SIZE)
    scores = mm(queries, keys, "qhgd,khd->hgqk") * ATT_SCALE
    mask = jnp.arange(rows)[:, None] >= jnp.arange(rows)[None, :]
    scores = jnp.where(mask, scores, NEG_FILL)
    terms = jnp.exp(scores - jnp.max(scores, axis=-1, keepdims=True))
    probs = terms / jnp.sum(terms, axis=-1, keepdims=True)
    probs_low = probs.astype(BF16)
    attended = mm(probs_low, values, "hgqk,khd->qhgd").astype(BF16).reshape(rows, qw)
    partial = mm(attended, out_t, "sq,dq->sd").astype(BF16).reshape(-1, ROWS, WIDTH)
    hidden, normed_two, up_full, down_full = second(
        partial, inputs, gain_second[None], up_weight, jnp.swapaxes(down_weight, 1, 2))
    normed_two = normed_two.reshape(rows, WIDTH)
    up_full = up_full.reshape(experts, WIDTH, UNITS)
    down_full = down_full.reshape(experts, WIDTH, UNITS)

    expert_index = rank * experts + jnp.arange(experts, dtype=jnp.int32)
    combined = jnp.sum(
        jnp.where(expert_ids[:, :, None] == expert_index, gate_values[:, :, None], 0.0), axis=1)
    gate = mm(normed_two, gate_full, "sd,edf->esf")
    up = mm(normed_two, up_full, "sd,edf->esf")
    sig = jax.nn.sigmoid(gate)
    scale = combined.T[:, :, None]
    hidden_units = (scale * (gate * sig * up)).astype(BF16)
    moe_partial = mm(hidden_units, down_full, "esf,edf->sd")
    moe_local = lax.psum_scatter(
        moe_partial.astype(BF16), "tensor", scatter_dimension=0, tiled=True).astype(F32)
    block_output = (hidden + RES_SCALE * moe_local).astype(BF16)
    hidden_grad = mm(out_grad_full, down_full, "sd,edf->esf") * (RES_SCALE * scale)
    gate_pre = (hidden_grad * up * sig * (1.0 + gate * (1.0 - sig))).astype(BF16)
    up_pre = (hidden_grad * gate * sig).astype(BF16)
    rows_grad = mm(gate_pre, gate_full, "esf,edf->sd") + mm(up_pre, up_full, "esf,edf->sd")
    gate_grad = mm(normed_two, gate_pre, "sd,esf->edf").astype(BF16)
    up_grad = mm(normed_two, up_pre, "sd,esf->edf").astype(BF16)
    down_grad = (mm(out_grad_full, hidden_units, "sd,esf->edf") * RES_SCALE).astype(BF16)
    parts = (experts, 2, NZ, 2, PART, UNITS)
    branch_grad, state_grad, second_part, gate_grad, up_grad = third(
        rows_grad.astype(BF16).reshape(-1, ROWS, WIDTH), gate_grad.reshape(parts), up_grad.reshape(parts),
        hidden, gain_second[None], out_grad)
    branch_grad = branch_grad.reshape(rows, WIDTH)

    output_part = mm(branch_grad, attended, "sd,sq->dq")
    attended_grad = mm(branch_grad, out_t, "sd,dq->sq").astype(BF16)
    attended_grad = attended_grad.reshape(rows, kv_heads, group, HEAD_SIZE)
    value_grad = mm(probs_low, attended_grad, "hgqk,qhgd->khd")
    weight_grad = mm(attended_grad, values, "qhgd,khd->hgqk")
    inner = jnp.sum(weight_grad * probs, axis=-1, keepdims=True)
    score_grad = (probs * (weight_grad - inner)).astype(BF16)
    query_grad = mm(score_grad, keys, "hgqk,khd->qhgd") * ATT_SCALE
    key_grad = mm(score_grad, queries, "hgqk,qhgd->khd") * ATT_SCALE
    query_pre = apply_rotary(query_grad.reshape(rows, q_heads, HEAD_SIZE), cosine, -sine)
    key_pre = apply_rotary(key_grad, cosine, -sine)
    pre = jnp.concatenate(
        [query_pre.reshape(rows, -1), key_pre.reshape(rows, -1), value_grad.reshape(rows, -1)], axis=1
    ).astype(BF16)
    qkv_part = mm(normed, pre, "sd,sq->dq")
    normed_grad = mm(pre, qkv_full, "sq,dq->sd").astype(BF16)
    small_grad = jnp.concatenate(
        [qkv_part, output_part, jnp.zeros((WIDTH, 128), F32)], axis=1).astype(BF16)
    input_grad, down_grad, small_grad, gains = fourth(
        normed_grad.reshape(-1, ROWS, WIDTH), down_grad.reshape(parts), small_grad.reshape((1,) + parts[1:]),
        inputs, gain_first[None], state_grad, second_part)
    small_grad = small_grad[0]
    gains = lax.dynamic_slice_in_dim(gains, lax.axis_index("dp") * PART, PART, 1)
    return (
        block_output,
        input_grad,
        gains[0],
        small_grad[:, :qw],
        small_grad[:, qw : qw + kw],
        small_grad[:, qw + kw : qw + 2 * kw],
        small_grad[:, qw + 2 * kw : 2 * qw + 2 * kw].T,
        gains[1],
        gate_grad,
        up_grad,
        jnp.swapaxes(down_grad, 1, 2),
    )


def solution(mesh):
    in_specs = (
        P(("dp", "tensor"), None),
        P("dp"),
        P("dp", "tensor"),
        P("dp", "tensor"),
        P("dp", "tensor"),
        P("tensor", "dp"),
        P("dp"),
        P("tensor", "dp", None),
        P("tensor", "dp", None),
        P("tensor", None, "dp"),
        P("dp", None),
        P("dp", None),
        P(("dp", "tensor"), None),
    )
    out_specs = (
        P(("dp", "tensor"), None),
        P(("dp", "tensor"), None),
        P("dp"),
        P("dp", "tensor"),
        P("dp", "tensor"),
        P("dp", "tensor"),
        P("tensor", "dp"),
        P("dp"),
        P("tensor", "dp", None),
        P("tensor", "dp", None),
        P("tensor", None, "dp"),
    )
    return jax.shard_map(local, mesh=mesh, in_specs=in_specs, out_specs=out_specs, check_vma=False)
```

time: 970 us -> 422 us (0.44)
  waiting for transfers between devices: 749 us -> 0.7 us
  Pallas kernels: 0 us -> 219 us
  local copies, waits for them, and re-layouts: 29.6 us -> 54.2 us
  other arithmetic: 35.2 us -> 17.1 us
  blocking collectives: 15.5 us -> 0 us
    all_gather x6 -> x0, waiting for transfers between devices: 323 us -> none  [the longest x1 78.1 us: local(): lax.all_gather(jnp.concatenate([gate_weight, up_weight], 0), 'dp', axis=1...]
    reduce_scatter x5 -> x0, waiting for transfers between devices: 262 us -> none  [the longest x1 106 us: local(): lax.psum_scatter(jnp.concatenate([gate_grad.astype(BF16), up_grad.astype(...]
    pallas_call x0 -> x4, Pallas kernels: none -> 219 us  [the longest x1 62.4 us: third(): pl.pallas_call(third_kernel, out_shape=(shape((8, ROWS, WIDTH)), shape((R...]
    unnamed x15 -> x2, waiting for transfers between devices: 67 us -> 0.7 us
    reduce_scatter x1, waiting for transfers between devices: 51 us -> 0.01 us  [local(): lax.psum_scatter(moe_partial.astype(BF16), 'tensor', scatter_dimension=0,...]
    all_gather x1, waiting for transfers between devices: 46 us -> 0.01 us  [local(): out_grad_full = lax.all_gather(out_grad, 'tensor', axis=0, tiled=True)]
    convert_element_type x0 -> x3, local copies, waits for them, and re-layouts: none -> 18.9 us  [the longest x1 6.43 us: local(): (mm(out_grad_full, hidden_units, 'sd,esf->edf') * RES_SCALE).astype(BF16)]
    psum x1 -> x0, blocking collectives: 15.5 us -> none  [local(): gains = lax.psum(jnp.stack([first_part, second_part], 1), 'tensor')]
  transfers between devices with their start and end apart: 14 -> 2, of which waited for: 13 -> 0; matrix products, arithmetic and copies ran while one was open for 9% -> 28% of each run, Pallas kernels for 0% -> 53%
where the time goes in v1:
time: 422 us; the launch traced here: 414 us
  Pallas kernels  219 us (52%)
  matrix products  108 us (26%)
  local copies, waits for them, and re-layouts  54.2 us (13%)
  other arithmetic  17.1 us (4%)
  between operations  15.1 us (4%)
    dot_general x21, matrix products, mm(): return jnp.einsum(spec, a, b, preferred_element_type=F32)  108 us
    pallas_call x1, Pallas kernels, third(): pl.pallas_call(third_kernel, out_shape=(shape((8, ROWS, WIDTH)), shape((R...  62.4 us
    pallas_call x1, Pallas kernels, first(): pl.pallas_call(first_kernel, out_shape=(shape((8, ROWS, WIDTH)), shape((1...  57.2 us
    pallas_call x1, Pallas kernels, second(): pl.pallas_call(second_kernel, out_shape=(shape((ROWS, WIDTH), F32), shape...  54.5 us
    pallas_call x1, Pallas kernels, fourth(): pl.pallas_call(fourth_kernel, out_shape=(shape((ROWS, WIDTH)), shape((4,...  44.9 us
    unnamed x100, local copies, waits for them, and re-layouts  17.8 us
  transfers between devices with their start and end apart: 2, of which 0 were waited for; matrix products, arithmetic and copies ran while one was open for 28% of the time, Pallas kernels for 53%

profile of v1, /device:TPU:1, one launch (start us, length us, event | category | flops | bytes accessed | tf_op | source)
XLA Modules:
  0.0 414.1 jit_solution(10245351194128088571)
XLA Ops:
  13.5 57.2 %first.1 = (bf16[8,128,1024]{2,1,0:T(8,128)(2,1)S(1)}, bf16[1,16,64,512]{3,2,1,0:T(8,128)(2,1)S(1)}, bf16[4,16,64,512]{3,2,1,0:T(8,128)(2,1)S(1)}) custom-call(bf16[128,1024]{1,0:T(8,128)(2,1)S(1)} %copy-done, bf16[1,64,512]{2,1,0:T(8,128)(2,1)S(1)} %bitcast.262, bf16[4,64,512]{2,1,0:T(8,128)(2,1)S(1)} %copy-done.12), custom_call_target="tpu_custom_call" | custom-call | tf_op jit(solution)/shard_map/first/pallas_call | solution.py:410
  70.8 2.1 copy-done.17
  81.3 3.9 copy.92
  86.9 2.8 fusion.16
  89.8 2.0 fusion.15
  93.1 2.8 fusion.32
  96.8 54.5 %second.1 = (f32[128,1024]{1,0:T(8,128)S(1)}, bf16[8,128,1024]{2,1,0:T(8,128)(2,1)S(1)}, bf16[4,16,64,512]{3,2,1,0:T(8,128)(2,1)S(1)}, bf16[4,16,64,512]{3,2,1,0:T(8,128)(2,1)S(1)}) custom-call(bf16[8,128,1024]{2,1,0:T(8,128)(2,1)S(1)} %bitcast.255, bf16[128,1024]{1,0:T(8,128)(2,1)S(1)} %copy-done.1, f32[1,1024]{1,0:T(1,128)S(1)} %bitcast_convert_fusion.1.gain, ...), custom_call_target="tpu_custom_call" | custom-call | tf_op jit(solution)/shard_map/second/pallas_call | solution.py:421
  152.1 2.1 copy-done.21
  154.3 1.8 copy-done.19
  156.1 7.5 %fusion.87 = f32[4,512,1024]{2,1,0:T(8,128)} fusion(bf16[4,1024,512]{2,1,0:T(8,128)(2,1)S(1)} %bitcast.270, bf16[1024,1024,1]{1,0,2:T(8,128)(2,1)S(1)} %bitcast.274), kind=kOutput, calls=%fused_computation.129 | convolution fusion | flops 4294967296 | bytes 14680064 | tf_op jit(solution)/shard_map/sd,edf->esf/dot_general | solution.py:483
  163.6 10.9 %fusion.28 = f32[4,512,1024]{2,1,0:T(8,128)} fusion(bf16[4,1024,512]{2,1,0:T(8,128)(2,1)} %bitcast.272, bf16[1024,1024]{1,0:T(8,128)(2,1)} %all-gather.2.cloned.1.call-done), kind=kOutput, calls=%fused_computation.46 | convolution fusion | flops 4294967296 | bytes 14680064 | tf_op jit(solution)/shard_map/sd,edf->esf/dot_general | solution.py:483
  174.5 15.6 %fusion.7 = (bf16[4,1024,512]{1,2,0:T(8,128)(2,1)}, bf16[4,1024,512]{1,2,0:T(8,128)(2,1)}, bf16[4,1024,512]{1,2,0:T(8,128)(2,1)}) fusion(f32[4,512,1024]{2,1,0:T(8,128)} %fusion.28, f32[4,1024]{1,0:T(4,128)S(1)} %broadcast_multiply_fusion, f32[4,512,1024]{2,1,0:T(8,128)} %fusion.87, f32[4,1024]{1,0:T(4,128)S(1)} %bitcast.293, ...), kind=kOutput, calls=%fused_computation.12 | convolution fusion | flops 4332716032 | bytes 35684352 | tf_op jit(solution)/shard_map/sd,edf->esf/dot_general | solution.py:483
  190.1 8.6 %fusion.88 = f32[1024,1024,1]{1,0,2:T(8,128)} fusion(bf16[4,1024,512]{1,2,0:T(8,128)(2,1)} %get-tuple-element.44, bf16[4,1024,512]{2,1,0:T(8,128)(2,1)S(1)} %bitcast.269), kind=kOutput, calls=%fused_computation.130 | convolution fusion | flops 4294967296 | bytes 12582912 | tf_op jit(solution)/shard_map/esf,edf->sd/dot_general | solution.py:483
  198.7 6.1 %convert_bitcast_fusion.1 = bf16[4,1024,512]{1,2,0:T(8,128)(2,1)} fusion(bf16[4,1024,512]{1,2,0:T(8,128)(2,1)S(1)} %copy-done.42, bf16[1024,1024,1]{1,0,2:T(8,128)(2,1)S(1)} %bitcast.276), kind=kOutput, calls=%fused_computation.41 | convolution fusion | flops 4297064448 | bytes 10485760 | tf_op jit(solution)/shard_map/sd,esf->edf/dot_general | solution.py:483
  204.8 5.8 %bitcast_convert_fusion = bf16[1024,1024]{1,0:T(8,128)(2,1)} fusion(bf16[4,1024,512]{1,2,0:T(8,128)(2,1)S(1)} %copy-done.43, bf16[4,1024,512]{2,1,0:T(8,128)(2,1)S(1)} %bitcast.273), kind=kOutput, calls=%fused_computation.32 | convolution fusion | flops 4296015872 | bytes 10485760 | tf_op jit(solution)/shard_map/esf,edf->sd/dot_general | solution.py:483
  210.7 8.5 %convert_bitcast_fusion = bf16[4,1024,512]{1,2,0:T(8,128)(2,1)} fusion(bf16[4,1024,512]{1,2,0:T(8,128)(2,1)} %get-tuple-element.43, bf16[1024,1024,1]{1,0,2:T(8,128)(2,1)S(1)} %bitcast.277), kind=kOutput, calls=%fused_computation.40 | convolution fusion | flops 4297064448 | bytes 10485760 | tf_op jit(solution)/shard_map/sd,esf->edf/dot_general | solution.py:483
  219.2 5.8 %fusion.19 = bf16[1024,1024]{1,0:T(8,128)(2,1)} fusion(f32[1024,1024,1]{1,0,2:T(8,128)S(1)} %copy-done.41, bf16[4,1024,512]{1,2,0:T(8,128)(2,1)S(1)} %copy-done.44, bf16[4,1024,512]{2,1,0:T(8,128)(2,1)S(1)} %bitcast.271), kind=kOutput, calls=%fused_computation.31 | convolution fusion | flops 4297064448 | bytes 14680064 | tf_op jit(solution)/shard_map/esf,edf->sd/dot_general | solution.py:483
  225.0 6.2 %copy.83 = bf16[4,1024,512]{2,1,0:T(8,128)(2,1)} copy(bf16[4,1024,512]{1,2,0:T(8,128)(2,1)} %convert_bitcast_fusion.1) | data formatting | bytes 8388608 | tf_op jit(solution)/shard_map/convert_element_type | solution.py:547
  231.2 6.2 %copy.84 = bf16[4,1024,512]{2,1,0:T(8,128)(2,1)} copy(bf16[4,1024,512]{1,2,0:T(8,128)(2,1)} %convert_bitcast_fusion) | data formatting | bytes 8388608 | tf_op jit(solution)/shard_map/convert_element_type | solution.py:548
  239.4 62.4 %third.1 = (bf16[8,128,1024]{2,1,0:T(8,128)(2,1)S(1)}, f32[128,1024]{1,0:T(8,128)S(1)}, f32[8,1024]{1,0:T(8,128)S(1)}, f32[4,64,512]{2,1,0:T(8,128)S(1)}, f32[4,64,512]{2,1,0:T(8,128)S(1)}) custom-call(bf16[8,128,1024]{2,1,0:T(8,128)(2,1)} %bitcast.285, bf16[4,2,4,2,64,512]{5,4,3,2,1,0:T(8,128)(2,1)} %bitcast.281, bf16[4,2,4,2,64,512]{5,4,3,2,1,0:T(8,128)(2,1)} %bitcast.282, ...), custom_call_target="tpu_custom_call" | custom-call | tf_op jit(solution)/shard_map/third/pallas_call | solution.py:432
  302.8 5.6 %fusion = (f32[2,1024]{1,0:T(2,128)S(1)}, f32[1024,1024,2]{1,0,2:T(8,128)S(1)}) fusion(f32[2,1024]{1,0:T(2,128)S(1)} %fusion.15, f32[2,1024]{1,0:T(2,128)S(1)} %get-tuple-element.65, f32[1024,1024,2]{1,0,2:T(8,128)} %copy-done.23, pred[1024,1024]{0,1:T(8,128)(4,1)S(1)} %copy-done.26, bf16[1024,2,64]{0,2,1:T(8,128)(2,1)S(1)} %bitcast.291, ...), kind=kOutput, calls=%fused_computation.3 | convolution fusion | flops 281016320 | bytes 18243584 | tf_op jit(solution)/shard_map/qhgd,khd->hgqk/dot_general | solution.py:483
  308.8 4.2 %fusion.18 = bf16[2,1024,1024]{1,2,0:T(8,128)(2,1)} fusion(f32[1024,1024,2]{1,0,2:T(8,128)S(1)} %get-tuple-element.68, f32[2,1024]{1,0:T(2,128)S(1)} %get-tuple-element.67, f32[2,1024]{1,0:T(2,128)S(1)} %fusion.15, f32[2,1024]{1,0:T(2,128)S(1)} %get-tuple-element.65, f32[1024,1024,2]{1,0,2:T(8,128)S(1)} %bitcast.279, pred[1024,1024]{0,1:T(8,128)(4,1)S(1)} %copy-done.26), kind=kLoop, calls=%fused_computation.29 | loop fusion | flops 14680064 | bytes 22044672 | tf_op jit(solution)/shard_map/reshape.13
  312.9 3.5 fusion.44
  318.2 3.7 fusion.40
  324.9 3.1 fusion.31
  328.8 1.8 copy.88
  330.6 9.4 %fusion.17 = bf16[4,1024,512]{1,2,0:T(8,128)(2,1)} fusion(bf16[4,1024,512]{1,2,0:T(8,128)(2,1)} %get-tuple-element.45, bf16[1024,1024]{1,0:T(8,128)(2,1)} %all-gather.2.cloned.1.call-done), kind=kOutput, calls=%fused_computation.28 | convolution fusion | flops 4299161600 | bytes 10485760 | tf_op jit(solution)/shard_map/sd,esf->edf/dot_general | solution.py:483
  340.0 6.4 %copy.91 = bf16[4,1024,512]{2,1,0:T(8,128)(2,1)} copy(bf16[4,1024,512]{1,2,0:T(8,128)(2,1)} %fusion.17) | data formatting | bytes 8388608 | tf_op jit(solution)/shard_map/convert_element_type | solution.py:549
  346.5 2.5 copy.93
  349.0 2.4 fusion.35
  351.4 2.6 fusion.30
  355.1 44.9 %fourth.1 = (bf16[128,1024]{1,0:T(8,128)(2,1)S(1)}, f32[4,64,512]{2,1,0:T(8,128)S(1)}, f32[1,64,512]{2,1,0:T(8,128)S(1)}, f32[8,1024]{1,0:T(8,128)S(1)}) custom-call(bf16[8,128,1024]{2,1,0:T(8,128)(2,1)S(1)} %bitcast.254, bf16[4,2,4,2,64,512]{5,4,3,2,1,0:T(8,128)(2,1)} %bitcast.283, bf16[1,2,4,2,64,512]{5,4,3,2,1,0:T(8,128)(2,1)S(1)} %maximum_maximum_fusion.small_grads, ...), custom_call_target="tpu_custom_call" | custom-call | tf_op jit(solution)/shard_map/fourth/pallas_call | solution.py:445
  (142 shorter events, 36.0 us)
Async XLA Ops:
  7.2 156.5 %all-gather.2.cloned.1.call-start = ((), (), s32[]{:S(2)}) async-start(), calls=%async_computation.2 | async-start | bytes 2359296 | tf_op jit(solution)/shard_map/all_gather | solution.py:503
  7.9 394.1 %reduce-scatter.2.cloned.1.call-start = ((), (), s32[]{:S(2)}) async-start(), calls=%async_computation.1 | async-start | bytes 2359296 | tf_op jit(solution)/shard_map/reduce_scatter | solution.py:540
  76.9 14.9 %copy-start.27 = (f32[1024,256]{0,1:T(8,128)}, f32[1024,256]{0,1:T(8,128)S(1)}, u32[]{:S(2)}) copy-start(f32[1024,256]{0,1:T(8,128)S(1)} %fusion.49) | copy-start | bytes 3145732
  76.9 10.0 %copy-start.25 = (pred[1024,1024]{0,1:T(8,128)(4,1)S(1)}, pred[1024,1024]{0,1:T(8,128)(4,1)}, u32[]{:S(2)}) copy-start(pred[1024,1024]{0,1:T(8,128)(4,1)} %iota_compare_fusion) | copy-start | bytes 3145732
  79.0 10.8 %copy-start.28 = (f32[1024,32]{0,1:T(8,128)}, f32[1024,32]{0,1:T(8,128)S(1)}, u32[]{:S(2)}) copy-start(f32[1024,32]{0,1:T(8,128)S(1)} %get-tuple-element.62) | copy-start | bytes 393220
  93.1 3.6 copy-start.13
  93.1 3.7 copy-start.14
  96.0 58.2 %copy-start.38 = (f32[1024,8]{0,1:T(8,128)S(1)}, f32[1024,8]{0,1:T(8,128)}, u32[]{:S(2)}) copy-start(f32[1024,8]{0,1:T(8,128)} %param.24) | copy-start | bytes 98308
  96.0 58.2 %copy-start.39 = (s32[1024,8]{0,1:T(8,128)S(1)}, s32[1024,8]{0,1:T(8,128)}, u32[]{:S(2)}) copy-start(s32[1024,8]{0,1:T(8,128)} %param.23) | copy-start | bytes 98308
  163.6 10.9 %copy-start.18 = (bf16[4,16,64,512]{3,2,1,0:T(8,128)(2,1)S(1)}, bf16[4,16,64,512]{3,2,1,0:T(8,128)(2,1)}, u32[]{:S(2)}) copy-start(bf16[4,16,64,512]{3,2,1,0:T(8,128)(2,1)} %copy-done.17) | copy-start | bytes 12582916
  190.1 8.6 %copy-start.42 = (bf16[4,1024,512]{1,2,0:T(8,128)(2,1)S(1)}, bf16[4,1024,512]{1,2,0:T(8,128)(2,1)}, u32[]{:S(2)}) copy-start(bf16[4,1024,512]{1,2,0:T(8,128)(2,1)} %get-tuple-element.44) | copy-start | bytes 12582916
  198.7 6.1 %copy-start.22 = (bf16[4,16,64,512]{3,2,1,0:T(8,128)(2,1)S(1)}, bf16[4,16,64,512]{3,2,1,0:T(8,128)(2,1)}, u32[]{:S(2)}) copy-start(bf16[4,16,64,512]{3,2,1,0:T(8,128)(2,1)} %copy-done.21) | copy-start | bytes 12582916
  198.7 6.1 %copy-start.43 = (bf16[4,1024,512]{1,2,0:T(8,128)(2,1)S(1)}, bf16[4,1024,512]{1,2,0:T(8,128)(2,1)}, u32[]{:S(2)}) copy-start(bf16[4,1024,512]{1,2,0:T(8,128)(2,1)} %get-tuple-element.45) | copy-start | bytes 12582916
  210.7 8.5 %copy-start.20 = (bf16[4,16,64,512]{3,2,1,0:T(8,128)(2,1)S(1)}, bf16[4,16,64,512]{3,2,1,0:T(8,128)(2,1)}, u32[]{:S(2)}) copy-start(bf16[4,16,64,512]{3,2,1,0:T(8,128)(2,1)} %copy-done.19) | copy-start | bytes 12582916
  210.7 8.5 %copy-start.41 = (f32[1024,1024,1]{1,0,2:T(8,128)S(1)}, f32[1024,1024,1]{1,0,2:T(8,128)}, u32[]{:S(2)}) copy-start(f32[1024,1024,1]{1,0,2:T(8,128)} %fusion.88) | copy-start | bytes 12582916
  210.7 8.5 %copy-start.44 = (bf16[4,1024,512]{1,2,0:T(8,128)(2,1)S(1)}, bf16[4,1024,512]{1,2,0:T(8,128)(2,1)}, u32[]{:S(2)}) copy-start(bf16[4,1024,512]{1,2,0:T(8,128)(2,1)} %get-tuple-element.43) | copy-start | bytes 12582916
  239.4 63.3 %copy-start.26 = (pred[1024,1024]{0,1:T(8,128)(4,1)S(1)}, pred[1024,1024]{0,1:T(8,128)(4,1)}, u32[]{:S(2)}) copy-start(pred[1024,1024]{0,1:T(8,128)(4,1)} %iota_compare_fusion) | copy-start | bytes 3145732
  301.9 6.5 %copy-start.6 = (f32[128,1024]{1,0:T(8,128)}, f32[128,1024]{1,0:T(8,128)S(1)}, u32[]{:S(2)}) copy-start(f32[128,1024]{1,0:T(8,128)S(1)} %get-tuple-element.35.state_grad) | copy-start | bytes 1572868
  301.9 6.5 %copy-start.8 = (f32[4,64,512]{2,1,0:T(8,128)}, f32[4,64,512]{2,1,0:T(8,128)S(1)}, u32[]{:S(2)}) copy-start(f32[4,64,512]{2,1,0:T(8,128)S(1)} %get-tuple-element.89) | copy-start | bytes 1572868
  301.9 6.5 %copy-start.10 = (f32[4,64,512]{2,1,0:T(8,128)}, f32[4,64,512]{2,1,0:T(8,128)S(1)}, u32[]{:S(2)}) copy-start(f32[4,64,512]{2,1,0:T(8,128)S(1)} %get-tuple-element.88) | copy-start | bytes 1572868
  302.7 5.7 %slice-start = ((s8[8388608]{0:T(1024)(128)(4,1)}), s8[4194304]{0:T(1024)(128)(4,1)S(1)}, s32[]{:S(2)}) async-start(s8[8388608]{0:T(1024)(128)(4,1)} %bitcast.278), calls=%async_computation.3 | async-start | bytes 8388608
  302.8 6.0 %slice-start.1 = ((s8[8388608]{0:T(1024)(128)(4,1)}), s8[4194304]{0:T(1024)(128)(4,1)S(1)}, s32[]{:S(2)}) async-start(s8[8388608]{0:T(1024)(128)(4,1)} %bitcast.278), calls=%async_computation.4 | async-start | bytes 8388608
  316.4 8.5 %copy-start.37 = (bf16[1024,32]{0,1:T(8,128)(2,1)S(1)}, bf16[1024,32]{0,1:T(8,128)(2,1)}, u32[]{:S(2)}) copy-start(bf16[1024,32]{0,1:T(8,128)(2,1)} %get-tuple-element.54) | copy-start | bytes 196612
  349.0 5.0 %copy-start.40 = (bf16[512]{0:T(512)(128)(2,1)S(1)}, bf16[512]{0:T(512)(128)(2,1)}, u32[]{:S(2)}) copy-start(bf16[512]{0:T(512)(128)(2,1)} %pad.2.clone) | copy-start | bytes 3076
  349.0 5.3 %copy-start.31 = (bf16[1024,64]{1,0:T(8,128)(2,1)S(1)}, bf16[1024,64]{1,0:T(8,128)(2,1)}, u32[]{:S(2)}) copy-start(bf16[1024,64]{1,0:T(8,128)(2,1)} %copy.90) | copy-start | bytes 393220
  349.0 5.3 %copy-start.32 = (bf16[1024,64]{1,0:T(8,128)(2,1)S(1)}, bf16[1024,64]{1,0:T(8,128)(2,1)}, u32[]{:S(2)}) copy-start(bf16[1024,64]{1,0:T(8,128)(2,1)} %copy.89) | copy-start | bytes 393220
  349.0 5.3 %copy-start.33 = (bf16[1024,128]{1,0:T(8,128)(2,1)S(1)}, bf16[1024,128]{1,0:T(8,128)(2,1)}, u32[]{:S(2)}) copy-start(bf16[1024,128]{1,0:T(8,128)(2,1)} %copy.88) | copy-start | bytes 786436
  351.4 3.7 copy-start.7
  351.4 3.7 copy-start.16
  355.1 46.9 %copy-start.4 = (f32[128,1024]{1,0:T(8,128)S(1)}, f32[128,1024]{1,0:T(8,128)}, u32[]{:S(2)}) copy-start(f32[128,1024]{1,0:T(8,128)} %copy-done.2) | copy-start | bytes 1572868
  355.1 49.3 %copy-start.11 = (f32[4,64,512]{2,1,0:T(8,128)S(1)}, f32[4,64,512]{2,1,0:T(8,128)}, u32[]{:S(2)}) copy-start(f32[4,64,512]{2,1,0:T(8,128)} %copy-done.10) | copy-start | bytes 1572868
  355.1 50.1 %copy-start.9 = (f32[4,64,512]{2,1,0:T(8,128)S(1)}, f32[4,64,512]{2,1,0:T(8,128)}, u32[]{:S(2)}) copy-start(f32[4,64,512]{2,1,0:T(8,128)} %copy-done.8) | copy-start | bytes 1572868
  (17 other events, 34.1 us)
Sparse Core Ops, SparseCore 0:
  9.7 63.1 all-gather.1
  210.8 55.4 reduce-scatter.1

commit v2 on v1

--- a/solution.py
+++ b/solution.py
@@ -18,6 +18,7 @@
 MESH = pl.DeviceIdType.MESH
 NX, NY, NZ, NCORE = 4, 2, 4, 2
 ROWS, WIDTH, PART, UNITS = 128, 1024, 64, 512
+QBLOCK = 256
 ANY = pl.BlockSpec(memory_space=pl.ANY)
 VMEM = pl.BlockSpec(memory_space=pltpu.VMEM)
 DMA = pltpu.SemaphoreType.DMA
@@ -266,31 +267,111 @@
     return jax.ShapeDtypeStruct(dims, dtype)
 
 
-def first_kernel(x, small, gate, x_out, small_out, gate_out, ts, tr, ss, sr, gs, gr, local):
+def nn(a, b):
+    return lax.dot_general(a, b, (((1,), (0,)), ((), ())), preferred_element_type=F32)
+
+
+def nt(a, b):
+    return lax.dot_general(a, b, (((1,), (1,)), ((), ())), preferred_element_type=F32)
+
+
+def tn(a, b):
+    return lax.dot_general(a, b, (((0,), (0,)), ((), ())), preferred_element_type=F32)
+
+
+def lanes(rows):
+    return lax.broadcasted_iota(jnp.int32, (rows, 2 * HEAD_SIZE), 1)
+
+
+def rotate(pair, cosine, sine):
+    first = lanes(pair.shape[0]) % HEAD_SIZE < HEAD_SIZE // 2
+    other = jnp.where(first, pltpu.roll(pair, 3 * HEAD_SIZE // 2, 1), pltpu.roll(pair, HEAD_SIZE // 2, 1))
+    return pair * cosine + other * sine
+
+
+def stacked(pair):
+    low = lanes(pair.shape[0]) < HEAD_SIZE
+    zero = jnp.zeros_like(pair)
+    return jnp.concatenate([jnp.where(low, pair, zero), jnp.where(low, zero, pair)], axis=0)
+
+
+def unstacked(both):
+    rows = both.shape[0] // 2
+    return jnp.where(lanes(rows) < HEAD_SIZE, both[:rows], both[rows:])
+
+
+def masked(scores, first_row):
+    rows = lax.broadcasted_iota(jnp.int32, scores.shape, 0) % QBLOCK + first_row
+    columns = lax.broadcasted_iota(jnp.int32, scores.shape, 1)
+    return jnp.where(columns <= rows, scores, NEG_FILL)
+
+
+def doubled(kv, keys, values):
+    low = lanes(kv.shape[0]) < HEAD_SIZE
+    kv = kv.astype(F32)
+    swapped = pltpu.roll(kv, HEAD_SIZE, 1)
+    keys[...] = jnp.where(low, kv, swapped).astype(BF16)
+    values[...] = jnp.where(low, swapped, kv).astype(BF16)
+
+
+def forward_kernel(
+    x, small, gate, up, down, out_grad, tables,
+    hidden, normed_out, grad_out, gate_out, up_out, down_out, normed, qkv, attended, log_total, small_out, gains,
+    x_buf, keys, values, partial, normed_two, *scratch,
+):
     p = Place()
     meet(p)
-    small_gather = PartGather(p, small, small_out, (ss, sr), local.at[1])
-    rows = TensorGather(p, x, x_out, (ts, tr), local.at[0])
-    gates = PartGather(p, gate, gate_out, (gs, gr), local.at[2])
-    small_gather.forward()
-    rows.forward()
-    small_gather.spread()
+    branch_scratch, scratch = scratch[:5], scratch[5:]
+    pairs = [scratch[2 * i : 2 * i + 2] for i in range(7)]
+    local = scratch[14]
+    smalls = PartGather(p, small, small_out, pairs[0], local.at[0])
+    rows_in = TensorGather(p, x, x_buf, pairs[1], local.at[1])
+    smalls.forward()
+    rows_in.forward()
+    gates = PartGather(p, gate, gate_out, pairs[2], local.at[2])
+    smalls.spread()
+    ups = PartGather(p, up, up_out, pairs[3], local.at[3])
+    smalls.finish()
+    pick = (lax.broadcasted_iota(jnp.int32, (8, 128), 0) == lax.broadcasted_iota(jnp.int32, (8, 128), 1))
+    gains[...] = nt(pick.astype(F32).astype(BF16), small_out[0, :, :, 384:].reshape(WIDTH, 128))
     gates.forward()
+    rows_in.finish()
+    grads = TensorGather(p, out_grad, grad_out, pairs[4], local.at[4])
+    downs = PartGather(p, down, down_out, pairs[5], local.at[5])
+    qkv_weight = small_out[0, :, :, :256].reshape(WIDTH, 256)
+
+    def project(i, carry):
+        rows = pl.ds(pl.multiple_of(i * ROWS, ROWS), ROWS)
+        state = x_buf[i].astype(F32)
+        scale = lax.rsqrt(jnp.mean(state * state, axis=-1, keepdims=True) + NORM_EPSILON)
+        normed_rows = (state * scale * gains[0:1]).astype(BF16)
+        normed[rows] = normed_rows
+        pre = nn(normed_rows, qkv_weight)
+        qkv[rows, :128] = rotate(pre[:, :128], tables[0, rows], tables[1, rows]).astype(BF16)
+        qkv[rows, 128:] = rotate(pre[:, 128:], tables[2, rows], tables[3, rows]).astype(BF16)
+        return carry
+
+    lax.fori_loop(0, 8, project, 0)
+    ups.forward()
+    grads.forward()
+    doubled(qkv[:, 128:], keys, values)
+    out_weight = small_out[0, :, :, 256:384].reshape(WIDTH, 128)
+    for b in range(WIDTH // QBLOCK):
+        length = (b + 1) * QBLOCK
+        rows = pl.ds(b * QBLOCK, QBLOCK)
+        scores = masked(nt(stacked(qkv[rows, :128]), keys[:length]) * ATT_SCALE, b * QBLOCK)
+        peak = jnp.max(scores, axis=-1, keepdims=True)
+        terms = jnp.exp(scores - peak)
+        total = jnp.sum(terms, axis=-1, keepdims=True)
+        log_total[b] = peak + jnp.log(total)
+        out = unstacked(nn((terms / total).astype(BF16), values[:length])).astype(BF16)
+        attended[rows] = out
+        partial[2 * b : 2 * b + 2] = nt(out, out_weight).astype(BF16).reshape(2, ROWS, WIDTH)
+    branch = TensorScatter(p, partial, *branch_scratch)
     gates.spread()
-    small_gather.finish()
-    rows.finish()
-    gates.finish()
-
-
-def second_kernel(partial, x, gain, up, down, hidden, normed_out, up_out, down_out, normed, *scratch):
-    p = Place()
-    meet(p)
-    us, ur, ds, dr, ts, tr, local = scratch[-7:]
-    branch = TensorScatter(p, partial, *scratch[:5])
-    ups = PartGather(p, up, up_out, (us, ur), local.at[1])
+    downs.forward()
     branch.exchange()
-    downs = PartGather(p, down, down_out, (ds, dr), local.at[2])
-    ups.forward()
+    ups.spread()
     branch.arrive()
 
     def step(i, carry):
@@ -298,19 +379,39 @@
         state = x[rows].astype(F32) + RES_SCALE * branch.rows(rows)
         hidden[rows] = state
         scale = lax.rsqrt(jnp.mean(state * state, axis=-1, keepdims=True) + NORM_EPSILON)
-        normed[rows] = (state * scale * gain[...]).astype(BF16)
+        normed_two[rows] = (state * scale * gains[1:2]).astype(BF16)
         return carry
 
     lax.fori_loop(0, ROWS // 32, step, 0)
-    gather = TensorGather(p, normed, normed_out, (ts, tr), local.at[0])
-    downs.forward()
+    gather = TensorGather(p, normed_two, normed_out, pairs[6], local.at[6])
     gather.forward()
-    ups.spread()
     downs.spread()
     branch.finish()
     gather.finish()
+    grads.finish()
+    gates.finish()
     ups.finish()
     downs.finish()
+
+
+def forward(x, small, gate, up, down, out_grad, tables):
+    full = shape((4, 16, PART, UNITS))
+    rows = shape((8, ROWS, WIDTH))
+    return pl.pallas_call(
+        forward_kernel,
+        out_shape=(
+            shape((ROWS, WIDTH), F32), rows, rows, full, full, full, shape((WIDTH, WIDTH)), shape((WIDTH, 256)),
+            shape((WIDTH, 128)), shape((WIDTH // QBLOCK, 2 * QBLOCK, 1), F32), shape((1, 16, PART, UNITS)),
+            shape((8, WIDTH), F32)),
+        in_specs=[VMEM, VMEM, ANY, ANY, ANY, ANY, VMEM],
+        out_specs=(VMEM,) + (ANY,) * 5 + (VMEM,) * 6,
+        scratch_shapes=[
+            pltpu.VMEM((8, ROWS, WIDTH), BF16), pltpu.VMEM((WIDTH, 128), BF16), pltpu.VMEM((WIDTH, 128), BF16),
+            pltpu.VMEM((8, ROWS, WIDTH), BF16), pltpu.VMEM((ROWS, WIDTH), BF16)]
+        + TensorScatter.scratch() + sems(15) + sems(7) + sems(15) + sems(15) + sems(7) + sems(15) + sems(7)
+        + [DMA((7,))],
+        compiler_params=params(1, 56), name="forward",
+    )(x, small, gate, up, down, out_grad, tables)
 
 
 def norm_pull(state, gain, grad):
@@ -320,74 +421,116 @@
     return r * (w - u * jnp.mean(w * u, axis=-1, keepdims=True)), jnp.sum(grad * u, axis=0, keepdims=True)
 
 
-def third_kernel(
-    partial, gate_grads, up_grads, hidden, gain, out_grad,
-    branch_out, state_grad, gain_part, gate_out, up_out, branch, *scratch,
+def backward_kernel(
+    rows_partial, gate_grads, up_grads, down_grads, hidden, gains_in, out_grad, x, normed, qkv, attended, log_total,
+    small, tables,
+    input_grad, gate_out, up_out, down_out, small_out, gains,
+    branch, branch_full, state_grad, keys, values, key_grad, value_grad, pre, partial, small_grads, gain_buf, *scratch,
 ):
     p = Place()
     meet(p)
-    ts, tr, local = scratch[-3:]
-    rows_sum = TensorScatter(p, partial, *scratch[:5])
-    gates = PartScatter(p, gate_grads, *scratch[5:12])
-    ups = PartScatter(p, up_grads, *scratch[12:19])
+    sums, scratch = scratch[:5], scratch[5:]
+    more_sums, scratch = scratch[:5], scratch[5:]
+    parts = [scratch[7 * i : 7 * i + 7] for i in range(4)]
+    ts, tr, gs, gr, local = scratch[28:]
+    rows_sum = TensorScatter(p, rows_partial, *sums)
+    gates = PartScatter(p, gate_grads, *parts[0])
+    ups = PartScatter(p, up_grads, *parts[1])
+    downs = PartScatter(p, down_grads, *parts[2])
+    doubled(qkv[:, 128:], keys, values)
+    key_grad[...] = jnp.zeros_like(key_grad)
+    value_grad[...] = jnp.zeros_like(value_grad)
+    gains[...] = jnp.zeros_like(gains)
     gates.along()
-    ups.along()
     rows_sum.exchange()
     rows_sum.arrive()
-    gain_part[...] = jnp.zeros_like(gain_part)
 
     def step(i, carry):
         rows = pl.ds(pl.multiple_of(i * 32, 32), 32)
-        pulled, part = norm_pull(hidden[rows], gain[...], rows_sum.rows(rows))
-        gain_part[0:1] += part
+        pulled, part = norm_pull(hidden[rows], gains_in[1:2], rows_sum.rows(rows))
+        gains[1:2] += part
         state = out_grad[rows].astype(F32) + pulled
         state_grad[rows] = state
         branch[rows] = (RES_SCALE * state).astype(BF16)
         return carry
 
     lax.fori_loop(0, ROWS // 32, step, 0)
-    gather = TensorGather(p, branch, branch_out, (ts, tr), local.at[0])
+    gather = TensorGather(p, branch, branch_full, (ts, tr), local.at[0])
+    ups.along()
     gather.forward()
+    downs.along()
+    rows_sum.finish()
     gates.pair()
+    gather.finish()
+
+    out_weight = small[0, :, :, 256:384].reshape(WIDTH, 128)
+    for b in range(WIDTH // QBLOCK):
+        length = (b + 1) * QBLOCK
+        rows = pl.ds(b * QBLOCK, QBLOCK)
+        grad = stacked(nn(branch_full[2 * b : 2 * b + 2].reshape(QBLOCK, WIDTH), out_weight).astype(BF16))
+        query = stacked(qkv[rows, :128])
+        scores = masked(nt(query, keys[:length]) * ATT_SCALE, b * QBLOCK)
+        probs = jnp.exp(scores - log_total[b])
+        value_grad[:length] += tn(probs.astype(BF16), grad)
+        weight_grad = nt(grad, values[:length])
+        inner = jnp.sum(weight_grad * probs, axis=-1, keepdims=True)
+        score_grad = (probs * (weight_grad - inner)).astype(BF16)
+        key_grad[:length] += tn(score_grad, query)
+        query_grad = unstacked(nn(score_grad, keys[:length])) * ATT_SCALE
+        pre[rows, :128] = rotate(query_grad, tables[0, rows], -tables[1, rows]).astype(BF16)
     ups.pair()
-    rows_sum.finish()
+    low = lanes(WIDTH) < HEAD_SIZE
+    key_sum = key_grad[...] + pltpu.roll(key_grad[...], HEAD_SIZE, 1)
+    value_sum = value_grad[...] + pltpu.roll(value_grad[...], HEAD_SIZE, 1)
+    kv_grad = jnp.where(low, key_sum * ATT_SCALE, value_sum)
+    pre[:, 128:] = rotate(kv_grad, tables[2], -tables[3]).astype(BF16)
+
+    qkv_weight = small[0, :, :, :256].reshape(WIDTH, 256)
+
+    def give(b, carry):
+        rows = pl.ds(pl.multiple_of(b * QBLOCK, QBLOCK), QBLOCK)
+        partial[pl.ds(2 * b, 2)] = nt(pre[rows], qkv_weight).astype(BF16).reshape(2, ROWS, WIDTH)
+        return carry
+
+    lax.fori_loop(0, WIDTH // QBLOCK, give, 0)
+    input_sum = TensorScatter(p, partial, *more_sums)
+
+    def weigh(i, carry):
+        columns = pl.ds(pl.multiple_of(i * 256, 256), 256)
+        of_qkv = tn(normed[:, columns], pre[...]).astype(BF16)
+        of_out = tn(branch_full[:, :, columns].reshape(WIDTH, 256), attended[...]).astype(BF16)
+        for r in range(4):
+            z = (i % 2) * 2 + r // 2
+            part = slice(r * PART, r * PART + PART)
+            small_grads[0, i // 2, z, r % 2, :, :256] = of_qkv[part]
+            small_grads[0, i // 2, z, r % 2, :, 256:384] = of_out[part]
+            small_grads[0, i // 2, z, r % 2, :, 384:] = jnp.zeros((PART, 128), BF16)
+        return carry
+
+    lax.fori_loop(0, 4, weigh, 0)
+    smalls = PartScatter(p, small_grads, *parts[3])
+    downs.pair()
+    smalls.along()
     gates.finish(gate_out)
     ups.finish(up_out)
-    gather.finish()
-
-
-def fourth_kernel(
-    partial, down_grads, small_grads, x, gain, state_grad, second_part,
-    input_grad, down_out, small_out, gains, gain_buf, *scratch,
-):
-    p = Place()
-    meet(p)
-    gs, gr = scratch[-2:]
-    rows_sum = TensorScatter(p, partial, *scratch[:5])
-    smalls = PartScatter(p, small_grads, *scratch[5:12])
-    downs = PartScatter(p, down_grads, *scratch[12:19])
-    smalls.along()
-    downs.along()
-    rows_sum.exchange()
-    rows_sum.arrive()
-    gains[...] = jnp.zeros_like(gains)
-    gains[1:2] = second_part[0:1]
-
-    def step(i, carry):
+    input_sum.exchange()
+    input_sum.arrive()
+
+    def last(i, carry):
         rows = pl.ds(pl.multiple_of(i * 32, 32), 32)
-        pulled, part = norm_pull(x[rows].astype(F32), gain[...], rows_sum.rows(rows))
+        pulled, part = norm_pull(x[rows].astype(F32), gains_in[0:1], input_sum.rows(rows))
         gains[0:1] += part
         input_grad[rows] = (state_grad[rows] + pulled).astype(BF16)
         return carry
 
-    lax.fori_loop(0, ROWS // 32, step, 0)
+    lax.fori_loop(0, ROWS // 32, last, 0)
 
     number = 0
     copies = []
     stages = (
         [p.x_dev(j) for j in range(1, NX)], [p.tensor_pair()], [p.core_dev()],
         [p.z_dev(j) for j in range(1, NZ)], [p.y_dev()])
-    between = (smalls.pair, downs.pair, None, None, None)
+    between = (smalls.pair, lambda: downs.finish(down_out), lambda: smalls.finish(small_out), None, None)
     for stage, (devices, work) in enumerate(zip(stages, between)):
         gain_buf[9 + stage] = gains[...]
         now = [push(gain_buf.at[9 + stage], gain_buf.at[number + k], (gs, gr), number + k, device)
@@ -399,67 +542,28 @@
             gains[...] += gain_buf[number + k]
         number += len(devices)
         copies += now
-    rows_sum.finish()
-    smalls.finish(small_out)
-    downs.finish(down_out)
+    input_sum.finish()
     for copy in copies:
         copy.wait_send()
 
 
-def first(x, small, gate):
+def backward(rows_partial, gate_grads, up_grads, down_grads, *rest):
+    weight = shape((4, PART, UNITS), F32)
     return pl.pallas_call(
-        first_kernel,
-        out_shape=(shape((8, ROWS, WIDTH)), shape((1, 16, PART, UNITS)), shape((4, 16, PART, UNITS))),
-        in_specs=[ANY] * 3, out_specs=(ANY,) * 3,
-        scratch_shapes=sems(7) + sems(15) + sems(15) + [DMA((3,))],
-        compiler_params=params(1, 32), name="first",
-    )(x, small, gate)
-
-
-def second(partial, x, gain, up, down):
-    full = shape((4, 16, PART, UNITS))
-    return pl.pallas_call(
-        second_kernel,
-        out_shape=(shape((ROWS, WIDTH), F32), shape((8, ROWS, WIDTH)), full, full),
-        in_specs=[ANY, VMEM, VMEM, ANY, ANY], out_specs=(VMEM, ANY, ANY, ANY),
-        scratch_shapes=[pltpu.VMEM((ROWS, WIDTH), BF16)] + TensorScatter.scratch()
-        + sems(15) + sems(15) + sems(7) + [DMA((3,))],
-        compiler_params=params(2, 32), name="second",
-    )(partial, x, gain, up, down)
-
-
-def third(partial, gate_grads, up_grads, hidden, gain, out_grad):
-    return pl.pallas_call(
-        third_kernel,
+        backward_kernel,
         out_shape=(
-            shape((8, ROWS, WIDTH)), shape((ROWS, WIDTH), F32), shape((8, WIDTH), F32),
-            shape((4, PART, UNITS), F32), shape((4, PART, UNITS), F32)),
-        in_specs=[ANY, ANY, ANY, VMEM, VMEM, VMEM], out_specs=(ANY,) + (VMEM,) * 4,
-        scratch_shapes=[pltpu.VMEM((ROWS, WIDTH), BF16)] + TensorScatter.scratch()
-        + PartScatter.scratch(4) + PartScatter.scratch(4) + sems(7) + [DMA((1,))],
-        compiler_params=params(3, 48), name="third",
-    )(partial, gate_grads, up_grads, hidden, gain, out_grad)
-
-
-def fourth(partial, down_grads, small_grads, x, gain, state_grad, second_part):
-    return pl.pallas_call(
-        fourth_kernel,
-        out_shape=(
-            shape((ROWS, WIDTH)), shape((4, PART, UNITS), F32), shape((1, PART, UNITS), F32),
-            shape((8, WIDTH), F32)),
-        in_specs=[ANY, ANY, ANY, VMEM, VMEM, VMEM, VMEM], out_specs=(VMEM,) * 4,
-        scratch_shapes=[pltpu.VMEM((14, 8, WIDTH), F32)] + TensorScatter.scratch()
-        + PartScatter.scratch(1) + PartScatter.scratch(4) + sems(9),
-        compiler_params=params(4, 48), name="fourth",
-    )(partial, down_grads, small_grads, x, gain, state_grad, second_part)
-
-
-def rms_normed(activations, gain_vector):
-    return (
-        activations
-        * lax.rsqrt(jnp.mean(activations * activations, axis=-1, keepdims=True) + NORM_EPSILON)
-        * gain_vector
-    )
+            shape((ROWS, WIDTH)), weight, weight, weight, shape((1, PART, UNITS), F32), shape((8, WIDTH), F32)),
+        in_specs=[ANY] * 4 + [VMEM] * 10, out_specs=(VMEM,) * 6,
+        scratch_shapes=[
+            pltpu.VMEM((ROWS, WIDTH), BF16), pltpu.VMEM((8, ROWS, WIDTH), BF16), pltpu.VMEM((ROWS, WIDTH), F32),
+            pltpu.VMEM((WIDTH, 128), BF16), pltpu.VMEM((WIDTH, 128), BF16),
+            pltpu.VMEM((WIDTH, 128), F32), pltpu.VMEM((WIDTH, 128), F32), pltpu.VMEM((WIDTH, 256), BF16),
+            pltpu.VMEM((8, ROWS, WIDTH), BF16), pltpu.VMEM((1, 2, NZ, 2, PART, UNITS), BF16),
+            pltpu.VMEM((14, 8, WIDTH), F32)]
+        + TensorScatter.scratch() * 2 + PartScatter.scratch(4) * 3 + PartScatter.scratch(1)
+        + sems(7) + sems(9) + [DMA((1,))],
+        compiler_params=params(2, 60), name="backward",
+    )(rows_partial, gate_grads, up_grads, down_grads, *rest)
 
 
 def rotary_tables(length):
@@ -467,16 +571,13 @@
     positions = jnp.arange(length).astype(F32)
     frequencies = jnp.power(ROPE_BASE, -(jnp.arange(half_width).astype(F32) * 2.0 / HEAD_SIZE))
     angles = positions[:, None] * frequencies[None, :]
-    return (jnp.cos(angles)[:, None, :], jnp.sin(angles)[:, None, :])
-
-
-def apply_rotary(head_data, cosine, sine):
-    half_width = head_data.shape[-1] // 2
-    first_half = head_data[..., :half_width]
-    second_half = head_data[..., half_width:]
-    return jnp.concatenate(
-        [first_half * cosine - second_half * sine, second_half * cosine + first_half * sine], axis=-1
-    )
+    cosine, sine = jnp.cos(angles), jnp.sin(angles)
+    cosine = jnp.concatenate([cosine, cosine], axis=1)
+    sine = jnp.concatenate([-sine, sine], axis=1)
+    return jnp.stack([
+        jnp.concatenate([cosine, cosine], axis=1), jnp.concatenate([sine, sine], axis=1),
+        jnp.concatenate([cosine, jnp.ones_like(cosine)], axis=1),
+        jnp.concatenate([sine, jnp.zeros_like(sine)], axis=1)])
 
 
 def mm(a, b, spec):
@@ -492,39 +593,16 @@
     experts = gate_weight.shape[0]
     qw = query_weight.shape[1]
     kw = key_matrix.shape[1]
-    q_heads, kv_heads = qw // HEAD_SIZE, kw // HEAD_SIZE
-    group = q_heads // kv_heads
-    cosine, sine = rotary_tables(rows)
+    tables = rotary_tables(rows)
 
     small = jnp.concatenate(
         [query_weight, key_matrix, value_matrix, output_weight.T, first_gain[:, None], second_gain[:, None],
          jnp.zeros((PART, 126), BF16)], axis=1)
-    x_full, small, gate_full = first(inputs, small[None], gate_weight)
-    out_grad_full = lax.all_gather(out_grad, "tensor", axis=0, tiled=True)
-    small = small.reshape(WIDTH, UNITS)
+    (hidden, normed_two, out_grad_full, gate_full, up_full, down_full, normed, qkv, attended, log_total, small,
+     gains) = forward(inputs, small[None], gate_weight, up_weight, jnp.swapaxes(down_weight, 1, 2), out_grad, tables)
+    normed_two = normed_two.reshape(rows, WIDTH)
+    out_grad_full = out_grad_full.reshape(rows, WIDTH)
     gate_full = gate_full.reshape(experts, WIDTH, UNITS)
-    qkv_full = small[:, : qw + 2 * kw]
-    out_t = small[:, qw + 2 * kw : 2 * qw + 2 * kw]
-    gain_first = small[:, 2 * qw + 2 * kw].astype(F32)
-    gain_second = small[:, 2 * qw + 2 * kw + 1].astype(F32)
-
-    normed = rms_normed(x_full.reshape(rows, WIDTH).astype(F32), gain_first).astype(BF16)
-    qkv = mm(normed, qkv_full, "sd,dq->sq")
-    queries = apply_rotary(qkv[:, :qw].reshape(rows, q_heads, HEAD_SIZE), cosine, sine).astype(BF16)
-    keys = apply_rotary(qkv[:, qw : qw + kw].reshape(rows, kv_heads, HEAD_SIZE), cosine, sine).astype(BF16)
-    values = qkv[:, qw + kw :].astype(BF16).reshape(rows, kv_heads, HEAD_SIZE)
-    queries = queries.reshape(rows, kv_heads, group, HEAD_SIZE)
-    scores = mm(queries, keys, "qhgd,khd->hgqk") * ATT_SCALE
-    mask = jnp.arange(rows)[:, None] >= jnp.arange(rows)[None, :]
-    scores = jnp.where(mask, scores, NEG_FILL)
-    terms = jnp.exp(scores - jnp.max(scores, axis=-1, keepdims=True))
-    probs = terms / jnp.sum(terms, axis=-1, keepdims=True)
-    probs_low = probs.astype(BF16)
-    attended = mm(probs_low, values, "hgqk,khd->qhgd").astype(BF16).reshape(rows, qw)
-    partial = mm(attended, out_t, "sq,dq->sd").astype(BF16).reshape(-1, ROWS, WIDTH)
-    hidden, normed_two, up_full, down_full = second(
-        partial, inputs, gain_second[None], up_weight, jnp.swapaxes(down_weight, 1, 2))
-    normed_two = normed_two.reshape(rows, WIDTH)
     up_full = up_full.reshape(experts, WIDTH, UNITS)
     down_full = down_full.reshape(experts, WIDTH, UNITS)
 
@@ -548,32 +626,9 @@
     up_grad = mm(normed_two, up_pre, "sd,esf->edf").astype(BF16)
     down_grad = (mm(out_grad_full, hidden_units, "sd,esf->edf") * RES_SCALE).astype(BF16)
     parts = (experts, 2, NZ, 2, PART, UNITS)
-    branch_grad, state_grad, second_part, gate_grad, up_grad = third(
+    input_grad, gate_grad, up_grad, down_grad, small_grad, gains = backward(
         rows_grad.astype(BF16).reshape(-1, ROWS, WIDTH), gate_grad.reshape(parts), up_grad.reshape(parts),
-        hidden, gain_second[None], out_grad)
-    branch_grad = branch_grad.reshape(rows, WIDTH)
-
-    output_part = mm(branch_grad, attended, "sd,sq->dq")
-    attended_grad = mm(branch_grad, out_t, "sd,dq->sq").astype(BF16)
-    attended_grad = attended_grad.reshape(rows, kv_heads, group, HEAD_SIZE)
-    value_grad = mm(probs_low, attended_grad, "hgqk,qhgd->khd")
-    weight_grad = mm(attended_grad, values, "qhgd,khd->hgqk")
-    inner = jnp.sum(weight_grad * probs, axis=-1, keepdims=True)
-    score_grad = (probs * (weight_grad - inner)).astype(BF16)
-    query_grad = mm(score_grad, keys, "hgqk,khd->qhgd") * ATT_SCALE
-    key_grad = mm(score_grad, queries, "hgqk,qhgd->khd") * ATT_SCALE
-    query_pre = apply_rotary(query_grad.reshape(rows, q_heads, HEAD_SIZE), cosine, -sine)
-    key_pre = apply_rotary(key_grad, cosine, -sine)
-    pre = jnp.concatenate(
-        [query_pre.reshape(rows, -1), key_pre.reshape(rows, -1), value_grad.reshape(rows, -1)], axis=1
-    ).astype(BF16)
-    qkv_part = mm(normed, pre, "sd,sq->dq")
-    normed_grad = mm(pre, qkv_full, "sq,dq->sd").astype(BF16)
-    small_grad = jnp.concatenate(
-        [qkv_part, output_part, jnp.zeros((WIDTH, 128), F32)], axis=1).astype(BF16)
-    input_grad, down_grad, small_grad, gains = fourth(
-        normed_grad.reshape(-1, ROWS, WIDTH), down_grad.reshape(parts), small_grad.reshape((1,) + parts[1:]),
-        inputs, gain_first[None], state_grad, second_part)
+        down_grad.reshape(parts), hidden, gains, out_grad, inputs, normed, qkv, attended, log_total, small, tables)
     small_grad = small_grad[0]
     gains = lax.dynamic_slice_in_dim(gains, lax.axis_index("dp") * PART, PART, 1)
     return (

time: 422 us -> 360 us (0.85)
  matrix products: 108 us -> 81.1 us
  local copies, waits for them, and re-layouts: 54.2 us -> 31.7 us
  other arithmetic: 17.1 us -> 6.93 us
    dot_general x21 -> x9, matrix products: 108 us -> 81.1 us  [mm(): return jnp.einsum(spec, a, b, preferred_element_type=F32)]
    unnamed x100 -> x32, local copies, waits for them, and re-layouts: 17.8 us -> 6.26 us
    dot_general x2 -> x0, local copies, waits for them, and re-layouts: 6.45 us -> none  [mm(): return jnp.einsum(spec, a, b, preferred_element_type=F32)]
    reshape x4 -> x0, local copies, waits for them, and re-layouts: 5.32 us -> none  [the longest x1 1.79 us: local(): query_pre.reshape(rows, -1)]
    pallas_call x4 -> x2, Pallas kernels: 219 us -> 221 us  [the longest x1 112 us: backward(): pl.pallas_call(backward_kernel, out_shape=(shape((ROWS, WIDTH)), weight,...]
  transfers between devices with their start and end apart: 2 -> 1, of which waited for: 0 -> 0; matrix products, arithmetic and copies ran while one was open for 28% -> 17% of each run, Pallas kernels for 53% -> 32%
where the time goes in v2:
time: 360 us; the launch traced here: 355 us
  Pallas kernels  221 us (61%)
  matrix products  81.1 us (23%)
  local copies, waits for them, and re-layouts  31.7 us (9%)
  between operations  14.5 us (4%)
  other arithmetic  6.93 us (2%)
    pallas_call x1, Pallas kernels, backward(): pl.pallas_call(backward_kernel, out_shape=(shape((ROWS, WIDTH)), weight,...  112 us
    pallas_call x1, Pallas kernels, forward(): pl.pallas_call(forward_kernel, out_shape=(shape((ROWS, WIDTH), F32), rows...  109 us
    dot_general x9, matrix products, mm(): return jnp.einsum(spec, a, b, preferred_element_type=F32)  81.1 us
  transfers between devices with their start and end apart: 1, of which 0 were waited for; matrix products, arithmetic and copies ran while one was open for 17% of the time, Pallas kernels for 32%

profile of v2, /device:TPU:1, one launch (start us, length us, event | category | flops | bytes accessed | tf_op | source)
XLA Modules:
  0.0 355.4 jit_solution(9885309085871951565)
XLA Ops:
  7.3 0.1 pad.9.clone
  7.4 0.1 pad.6.clone
  7.4 0.9 select_reduce_fusion
  8.3 0.8 copy.37
  9.1 0.8 copy.38
  9.9 1.9 multiply_cosine_fusion
  11.8 0.9 maximum_bitcast_fusion
  12.7 1.5 pad_maximum_fusion.tables
  14.2 0.7 concatenate.21
  15.0 109.0 %forward.1 = (f32[128,1024]{1,0:T(8,128)}, bf16[8,128,1024]{2,1,0:T(8,128)(2,1)}, bf16[8,128,1024]{2,1,0:T(8,128)(2,1)}, bf16[4,16,64,512]{3,2,1,0:T(8,128)(2,1)...) custom-call(bf16[128,1024]{1,0:T(8,128)(2,1)} %x.3, ...), custom_call_target="tpu_custom_call" | custom-call | tf_op jit(solution)/shard_map/forward/pallas_call | solution.py:400
  124.0 10.8 %fusion.19 = f32[4,512,1024]{2,1,0:T(8,128)} fusion(bf16[4,1024,512]{2,1,0:T(8,128)(2,1)} %bitcast.124, bf16[1024,1024,1]{1,0,2:T(8,128)(2,1)} %bitcast.132), kind=kOutput, calls=%fused_computation.47 | convolution fusion | flops 4294967296 | bytes 14680064 | tf_op jit(solution)/shard_map/sd,edf->esf/dot_general | solution.py:584
  134.8 7.2 %fusion.20 = f32[4,512,1024]{2,1,0:T(8,128)} fusion(bf16[4,1024,512]{2,1,0:T(8,128)(2,1)S(1)} %bitcast.129, bf16[1024,1024,1]{1,0,2:T(8,128)(2,1)S(1)} %bitcast.130), kind=kOutput, calls=%fused_computation.48 | convolution fusion | flops 4294967296 | bytes 14680064 | tf_op jit(solution)/shard_map/sd,edf->esf/dot_general | solution.py:584
  142.0 16.1 %fusion.4 = (bf16[4,1024,512]{1,2,0:T(8,128)(2,1)}, bf16[4,1024,512]{1,2,0:T(8,128)(2,1)}, bf16[4,1024,512]{1,2,0:T(8,128)(2,1)}) fusion(f32[4,512,1024]{2,1,0:T(8,128)} %fusion.20, f32[4,1024]{1,0:T(4,128)S(1)} %broadcast_multiply_fusion, f32[4,512,1024]{2,1,0:T(8,128)} %fusion.19, f32[4,1024]{1,0:T(4,128)S(1)} %bitcast.120, ...), kind=kOutput, calls=%fused_computation.6 | convolution fusion | flops 4332716032 | bytes 35684352 | tf_op jit(solution)/shard_map/sd,edf->esf/dot_general | solution.py:584
  158.1 9.4 %bitcast_convert_fusion = bf16[1024,1024]{1,0:T(8,128)(2,1)} fusion(bf16[4,1024,512]{1,2,0:T(8,128)(2,1)} %get-tuple-element.49, bf16[4,1024,512]{2,1,0:T(8,128)(2,1)} %bitcast.128), kind=kOutput, calls=%fused_computation.21 | convolution fusion | flops 4296015872 | bytes 10485760 | tf_op jit(solution)/shard_map/esf,edf->sd/dot_general | solution.py:584
  167.5 9.5 %convert_bitcast_fusion = bf16[4,1024,512]{1,2,0:T(8,128)(2,1)} fusion(bf16[4,1024,512]{1,2,0:T(8,128)(2,1)} %get-tuple-element.47, bf16[1024,1024,1]{1,0,2:T(8,128)(2,1)} %bitcast.133), kind=kOutput, calls=%fused_computation.22 | convolution fusion | flops 4297064448 | bytes 10485760 | tf_op jit(solution)/shard_map/sd,esf->edf/dot_general | solution.py:584
  177.1 6.0 %convert_bitcast_fusion.1 = bf16[4,1024,512]{1,2,0:T(8,128)(2,1)} fusion(bf16[4,1024,512]{1,2,0:T(8,128)(2,1)S(1)} %copy-done.12, bf16[1024,1024,1]{1,0,2:T(8,128)(2,1)S(1)} %bitcast.135), kind=kOutput, calls=%fused_computation.23 | convolution fusion | flops 4297064448 | bytes 10485760 | tf_op jit(solution)/shard_map/sd,esf->edf/dot_general | solution.py:584
  183.1 6.2 %copy.45 = bf16[4,1024,512]{2,1,0:T(8,128)(2,1)} copy(bf16[4,1024,512]{1,2,0:T(8,128)(2,1)} %convert_bitcast_fusion.1) | data formatting | bytes 8388608 | tf_op jit(solution)/shard_map/convert_element_type | solution.py:625
  189.3 6.2 %copy.46 = bf16[4,1024,512]{2,1,0:T(8,128)(2,1)} copy(bf16[4,1024,512]{1,2,0:T(8,128)(2,1)} %convert_bitcast_fusion) | data formatting | bytes 8388608 | tf_op jit(solution)/shard_map/convert_element_type | solution.py:626
  195.5 8.5 %fusion.11 = bf16[4,1024,512]{1,2,0:T(8,128)(2,1)} fusion(bf16[4,1024,512]{1,2,0:T(8,128)(2,1)} %get-tuple-element.49, bf16[1024,1024,1]{1,0,2:T(8,128)(2,1)S(1)} %bitcast.131), kind=kOutput, calls=%fused_computation.18 | convolution fusion | flops 4299161600 | bytes 10485760 | tf_op jit(solution)/shard_map/sd,esf->edf/dot_general | solution.py:584
  204.0 6.3 %copy.47 = bf16[4,1024,512]{2,1,0:T(8,128)(2,1)} copy(bf16[4,1024,512]{1,2,0:T(8,128)(2,1)} %fusion.11) | data formatting | bytes 8388608 | tf_op jit(solution)/shard_map/convert_element_type | solution.py:627
  210.3 7.8 %fusion.21 = f32[1024,1024,1]{1,0,2:T(8,128)S(1)} fusion(bf16[4,1024,512]{1,2,0:T(8,128)(2,1)} %get-tuple-element.48, bf16[4,1024,512]{2,1,0:T(8,128)(2,1)} %bitcast.126), kind=kOutput, calls=%fused_computation.49 | convolution fusion | flops 4294967296 | bytes 12582912 | tf_op jit(solution)/shard_map/esf,edf->sd/dot_general | solution.py:584
  218.1 5.8 %fusion.12 = bf16[1024,1024]{1,0:T(8,128)(2,1)} fusion(f32[1024,1024,1]{1,0,2:T(8,128)S(1)} %fusion.21, bf16[4,1024,512]{1,2,0:T(8,128)(2,1)S(1)} %copy-done.13, bf16[4,1024,512]{2,1,0:T(8,128)(2,1)S(1)} %bitcast.125), kind=kOutput, calls=%fused_computation.20 | convolution fusion | flops 4297064448 | bytes 14680064 | tf_op jit(solution)/shard_map/esf,edf->sd/dot_general | solution.py:584
  223.9 112.2 %backward.1 = (bf16[128,1024]{1,0:T(8,128)(2,1)}, f32[4,64,512]{2,1,0:T(8,128)}, f32[4,64,512]{2,1,0:T(8,128)}, f32[4,64,512]{2,1,0:T(8,128)}, f32[1,64,512]{2,1,0:T(8,128)}, /*index=5*/f32[8,1024]{1,0:T(8,128)}) custom-call(bf16[8,128,1024]{2,1,0:T(8,128)(2,1)} %bitcast.114, bf16[4,2,4,2,64,512]{5,4,3,2,1,0:T(8,128)(2,1)} %bitcast.111, ...), custom_call_target="tpu_custom_call" | custom-call | tf_op jit(solution)/shard_map/backward/pallas_call | solution.py:552
  336.2 0.8 constant_dynamic-slice_fusion
  337.0 0.5 slice_bitcast_fusion.1
  337.5 1.4 slice_bitcast_fusion
  338.9 1.5 fusion.18
  340.4 1.7 add_convert_fusion
  342.2 1.7 copy.58
  343.8 1.9 copy.59
  345.7 1.9 copy.60
  347.6 0.8 copy.61
  (38 shorter events, 0.2 us)
Async XLA Ops:
  7.2 333.3 %reduce-scatter.2.cloned.1.call-start = ((), (), s32[]{:S(2)}) async-start(), calls=%async_computation.1 | async-start | bytes 2359296 | tf_op jit(solution)/shard_map/reduce_scatter | solution.py:618
  11.8 2.5 copy-start.2
  11.8 2.4 copy-start.3
  11.8 2.4 copy-start.4
  11.8 2.4 copy-start.5
  124.0 10.8 %copy-start.8 = (bf16[4,16,64,512]{3,2,1,0:T(8,128)(2,1)S(1)}, bf16[4,16,64,512]{3,2,1,0:T(8,128)(2,1)}, u32[]{:S(2)}) copy-start(bf16[4,16,64,512]{3,2,1,0:T(8,128)(2,1)} %get-tuple-element.33) | copy-start | bytes 12582916
  124.0 10.8 %copy-start.9 = (bf16[8,128,1024]{2,1,0:T(8,128)(2,1)S(1)}, bf16[8,128,1024]{2,1,0:T(8,128)(2,1)}, u32[]{:S(2)}) copy-start(bf16[8,128,1024]{2,1,0:T(8,128)(2,1)} %get-tuple-element.34) | copy-start | bytes 6291460
  134.8 7.2 %copy-start.7 = (bf16[4,16,64,512]{3,2,1,0:T(8,128)(2,1)S(1)}, bf16[4,16,64,512]{3,2,1,0:T(8,128)(2,1)}, u32[]{:S(2)}) copy-start(bf16[4,16,64,512]{3,2,1,0:T(8,128)(2,1)} %get-tuple-element.30) | copy-start | bytes 12582916
  134.8 7.2 %copy-start.10 = (bf16[8,128,1024]{2,1,0:T(8,128)(2,1)S(1)}, bf16[8,128,1024]{2,1,0:T(8,128)(2,1)}, u32[]{:S(2)}) copy-start(bf16[8,128,1024]{2,1,0:T(8,128)(2,1)} %get-tuple-element.31) | copy-start | bytes 6291460
  167.5 9.5 %copy-start.11 = (bf16[8,128,1024]{2,1,0:T(8,128)(2,1)S(1)}, bf16[8,128,1024]{2,1,0:T(8,128)(2,1)}, u32[]{:S(2)}) copy-start(bf16[8,128,1024]{2,1,0:T(8,128)(2,1)} %get-tuple-element.31) | copy-start | bytes 6291460
  167.5 9.5 %copy-start.12 = (bf16[4,1024,512]{1,2,0:T(8,128)(2,1)S(1)}, bf16[4,1024,512]{1,2,0:T(8,128)(2,1)}, u32[]{:S(2)}) copy-start(bf16[4,1024,512]{1,2,0:T(8,128)(2,1)} %get-tuple-element.48) | copy-start | bytes 12582916
  210.3 7.8 %copy-start.6 = (bf16[4,16,64,512]{3,2,1,0:T(8,128)(2,1)S(1)}, bf16[4,16,64,512]{3,2,1,0:T(8,128)(2,1)}, u32[]{:S(2)}) copy-start(bf16[4,16,64,512]{3,2,1,0:T(8,128)(2,1)} %get-tuple-element.32) | copy-start | bytes 12582916
  210.3 7.8 %copy-start.13 = (bf16[4,1024,512]{1,2,0:T(8,128)(2,1)S(1)}, bf16[4,1024,512]{1,2,0:T(8,128)(2,1)}, u32[]{:S(2)}) copy-start(bf16[4,1024,512]{1,2,0:T(8,128)(2,1)} %get-tuple-element.47) | copy-start | bytes 12582916
  223.9 116.5 %copy-start = (f32[128,1024]{1,0:T(8,128)S(1)}, f32[128,1024]{1,0:T(8,128)}, u32[]{:S(2)}) copy-start(f32[128,1024]{1,0:T(8,128)} %get-tuple-element.29.hidden) | copy-start | bytes 1572868
  336.2 11.4 %copy-start.1 = (f32[4,64,512]{2,1,0:T(8,128)S(1)}, f32[4,64,512]{2,1,0:T(8,128)}, u32[]{:S(2)}) copy-start(f32[4,64,512]{2,1,0:T(8,128)} %get-tuple-element.46) | copy-start | bytes 1572868
Sparse Core Ops, SparseCore 0:
  167.6 48.8 reduce-scatter.1

commit v3 on v2

--- a/solution.py
+++ b/solution.py
@@ -192,44 +192,40 @@
 
 
 class PartScatter:
-    SEMS = 5
-
     @staticmethod
     def scratch(n):
         return [
+            pltpu.VMEM((n, 2, NZ, 2, PART, UNITS), BF16),
             pltpu.VMEM((n, 2, NZ, PART, UNITS), BF16),
-            pltpu.VMEM((n, 2, NZ, PART, UNITS), BF16),
-            pltpu.VMEM((NZ, n, 2, PART, UNITS), BF16),
+            pltpu.VMEM((NZ - 1, n, 2, PART, UNITS), BF16),
             pltpu.VMEM((2, n, PART, UNITS), BF16),
-        ] + sems(5) + [DMA((1,))]
-
-    def __init__(self, p, grads, own, core_buf, z_buf, y_buf, send, recv, local):
+        ] + sems(5)
+
+    def __init__(self, p, grads, core_buf, z_buf, y_buf, send, recv):
         self.p, self.n = p, grads.shape[0]
-        self.own, self.core_buf, self.z_buf, self.y_buf = own, core_buf, z_buf, y_buf
+        self.grads, self.core_buf, self.z_buf, self.y_buf = grads, core_buf, z_buf, y_buf
         self.sem = (send, recv)
         self.core = push(grads.at[:, :, :, 1 - p.dc], core_buf, self.sem, 0, p.core_dev())
-        self.load = pltpu.make_async_copy(grads.at[:, :, :, p.dc], own, local.at[0])
-        self.load.start()
 
     def along(self):
         p = self.p
-        self.load.wait()
         self.core.wait_recv()
 
         def step(i, carry):
             for y in range(2):
                 for z in range(NZ):
-                    total = self.own[i, y, z].astype(F32) + self.core_buf[i, y, z].astype(F32)
-                    self.own[i, y, z] = total.astype(BF16)
+                    total = self.grads[i, y, z, p.dc].astype(F32) + self.core_buf[i, y, z].astype(F32)
+                    self.grads[i, y, z, p.dc] = total.astype(BF16)
             return carry
 
         lax.fori_loop(0, self.n, step, 0)
         self.z_copies = [
-            push(self.own.at[:, :, p.z(j)], self.z_buf.at[j], self.sem, j, p.z_dev(j)) for j in range(1, NZ)]
+            push(self.grads.at[:, :, p.z(j), p.dc], self.z_buf.at[j - 1], self.sem, j, p.z_dev(j))
+            for j in range(1, NZ)]
 
     def total(self, i, y):
-        value = self.own[i, y, self.p.dz].astype(F32)
-        for j in range(1, NZ):
+        value = self.grads[i, y, self.p.dz, self.p.dc].astype(F32)
+        for j in range(NZ - 1):
             value = value + self.z_buf[j, i, y].astype(F32)
         return value
 
@@ -245,15 +241,11 @@
         lax.fori_loop(0, self.n, step, 0)
         self.y_copy = push(self.y_buf.at[0], self.y_buf.at[1], self.sem, 4, p.y_dev())
 
-    def finish(self, out):
+    def finish(self, outs):
         p = self.p
         self.y_copy.wait_recv()
-
-        def step(i, carry):
-            out[i] = self.total(i, p.dy) + self.y_buf[1, i].astype(F32)
-            return carry
-
-        lax.fori_loop(0, self.n, step, 0)
+        for i, (out, slot) in enumerate(outs):
+            out[slot] = self.total(i, p.dy) + self.y_buf[1, i].astype(F32)
         for copy in [self.core, self.y_copy] + self.z_copies:
             copy.wait_send()
 
@@ -421,47 +413,150 @@
     return r * (w - u * jnp.mean(w * u, axis=-1, keepdims=True)), jnp.sum(grad * u, axis=0, keepdims=True)
 
 
+def experts_kernel(
+    x, out_grad_full, gate, up, down, combined, hidden, gains_in, out_grad,
+    moe_out, branch_out, state_grad, gain_part, gate_out, up_out, down_out,
+    gate_buf, up_buf, down_buf, moe, rows_acc, units, gate_pre, up_pre, rows_out, branch, *scratch,
+):
+    p = Place()
+    load_sem, scratch = scratch[0], scratch[1:]
+    sums, scratch = scratch[:5], scratch[5:]
+    parts = [scratch[6 * e : 6 * e + 6] for e in range(4)]
+    ts, tr, local = scratch[24:]
+
+    def load(e):
+        slot = e % 2
+        return [
+            pltpu.make_async_copy(ref.at[e], buf.at[slot], load_sem.at[slot, k])
+            for k, (ref, buf) in enumerate(((gate, gate_buf), (up, up_buf), (down, down_buf)))]
+
+    loads = load(0)
+    for copy in loads:
+        copy.start()
+    meet(p)
+    gain_part[...] = jnp.zeros_like(gain_part)
+    scatters = []
+    for e in range(4):
+        slot = e % 2
+        for copy in loads:
+            copy.wait()
+        if e < 3:
+            loads = load(e + 1)
+            for copy in loads:
+                copy.start()
+
+        def block(i, carry):
+            rows = pl.ds(pl.multiple_of(i * QBLOCK, QBLOCK), QBLOCK)
+            tokens = x[rows]
+            gate_part = nn(tokens, gate_buf[slot])
+            up_part = nn(tokens, up_buf[slot])
+            sig = 0.5 * jnp.tanh(0.5 * gate_part) + 0.5
+            act = gate_part * sig
+            scale = combined[rows, e : e + 1]
+            unit = (scale * (act * up_part)).astype(BF16)
+            grad = nn(out_grad_full[rows], down_buf[slot]) * (RES_SCALE * scale)
+            to_gate = (grad * up_part * (sig + act * (1.0 - sig))).astype(BF16)
+            to_up = (grad * act).astype(BF16)
+            units[rows] = unit
+            gate_pre[rows] = to_gate
+            up_pre[rows] = to_up
+            moe_part = nt(unit, down_buf[slot])
+            rows_part = nt(to_gate, gate_buf[slot]) + nt(to_up, up_buf[slot])
+            if e == 0:
+                moe[rows] = moe_part
+                rows_acc[rows] = rows_part
+            elif e < 3:
+                moe[rows] += moe_part
+                rows_acc[rows] += rows_part
+            else:
+                blocks = pl.ds(2 * i, 2)
+                moe_out[blocks] = (moe[rows] + moe_part).astype(BF16).reshape(2, ROWS, WIDTH)
+                rows_out[blocks] = (rows_acc[rows] + rows_part).astype(BF16).reshape(2, ROWS, WIDTH)
+            return carry
+
+        lax.fori_loop(0, WIDTH // QBLOCK, block, 0)
+        if e == 3:
+            rows_sum = TensorScatter(p, rows_out, *sums)
+        if e >= 1:
+            scatters[e - 1].along()
+        grads = parts[e][0]
+
+        def weigh(i, carry):
+            columns = pl.ds(pl.multiple_of(i * 256, 256), 256)
+            tokens = x[:, columns]
+            found = (
+                tn(tokens, gate_pre[...]), tn(tokens, up_pre[...]),
+                tn(out_grad_full[:, columns], units[...]) * RES_SCALE)
+            for k in range(3):
+                for r in range(4):
+                    z = (i % 2) * 2 + r // 2
+                    grads[k, i // 2, z, r % 2] = found[k][r * PART : r * PART + PART].astype(BF16)
+            return carry
+
+        lax.fori_loop(0, 4, weigh, 0)
+        scatters.append(PartScatter(p, *parts[e]))
+
+    rows_sum.exchange()
+    scatters[3].along()
+    scatters[0].pair()
+    rows_sum.arrive()
+
+    def step(i, carry):
+        rows = pl.ds(pl.multiple_of(i * 32, 32), 32)
+        pulled, part = norm_pull(hidden[rows], gains_in[1:2], rows_sum.rows(rows))
+        gain_part[1:2] += part
+        state = out_grad[rows].astype(F32) + pulled
+        state_grad[rows] = state
+        branch[rows] = (RES_SCALE * state).astype(BF16)
+        return carry
+
+    lax.fori_loop(0, ROWS // 32, step, 0)
+    gather = TensorGather(p, branch, branch_out, (ts, tr), local.at[0])
+    scatters[1].pair()
+    gather.forward()
+    scatters[2].pair()
+    scatters[0].finish(((gate_out, 0), (up_out, 0), (down_out, 0)))
+    scatters[1].finish(((gate_out, 1), (up_out, 1), (down_out, 1)))
+    scatters[3].pair()
+    scatters[2].finish(((gate_out, 2), (up_out, 2), (down_out, 2)))
+    scatters[3].finish(((gate_out, 3), (up_out, 3), (down_out, 3)))
+    rows_sum.finish()
+    gather.finish()
+
+
+def run_experts(*args):
+    weight = shape((4, PART, UNITS), F32)
+    rows = shape((8, ROWS, WIDTH))
+    return pl.pallas_call(
+        experts_kernel,
+        out_shape=(rows, rows, shape((ROWS, WIDTH), F32), shape((8, WIDTH), F32), weight, weight, weight),
+        in_specs=[VMEM, VMEM, ANY, ANY, ANY] + [VMEM] * 4, out_specs=(VMEM, ANY) + (VMEM,) * 5,
+        scratch_shapes=[pltpu.VMEM((2, WIDTH, UNITS), BF16)] * 3 + [pltpu.VMEM((WIDTH, WIDTH), F32)] * 2
+        + [pltpu.VMEM((WIDTH, UNITS), BF16)] * 3
+        + [pltpu.VMEM((8, ROWS, WIDTH), BF16), pltpu.VMEM((ROWS, WIDTH), BF16), DMA((2, 3))]
+        + TensorScatter.scratch() + PartScatter.scratch(3) * 4 + sems(7) + [DMA((1,))],
+        compiler_params=params(2, 62), name="experts",
+    )(*args)
+
+
 def backward_kernel(
-    rows_partial, gate_grads, up_grads, down_grads, hidden, gains_in, out_grad, x, normed, qkv, attended, log_total,
-    small, tables,
-    input_grad, gate_out, up_out, down_out, small_out, gains,
-    branch, branch_full, state_grad, keys, values, key_grad, value_grad, pre, partial, small_grads, gain_buf, *scratch,
+    moe_partial, branch_full, state_grad, gain_part, hidden, gains_in, x, normed, qkv, attended, log_total, small,
+    tables,
+    block_out, input_grad, small_out, gains,
+    keys, values, key_grad, value_grad, pre, partial, gain_buf, *scratch,
 ):
     p = Place()
     meet(p)
     sums, scratch = scratch[:5], scratch[5:]
     more_sums, scratch = scratch[:5], scratch[5:]
-    parts = [scratch[7 * i : 7 * i + 7] for i in range(4)]
-    ts, tr, gs, gr, local = scratch[28:]
-    rows_sum = TensorScatter(p, rows_partial, *sums)
-    gates = PartScatter(p, gate_grads, *parts[0])
-    ups = PartScatter(p, up_grads, *parts[1])
-    downs = PartScatter(p, down_grads, *parts[2])
+    part = scratch[:6]
+    small_grads = part[0]
+    gs, gr = scratch[6:]
+    moe_sum = TensorScatter(p, moe_partial, *sums)
     doubled(qkv[:, 128:], keys, values)
     key_grad[...] = jnp.zeros_like(key_grad)
     value_grad[...] = jnp.zeros_like(value_grad)
-    gains[...] = jnp.zeros_like(gains)
-    gates.along()
-    rows_sum.exchange()
-    rows_sum.arrive()
-
-    def step(i, carry):
-        rows = pl.ds(pl.multiple_of(i * 32, 32), 32)
-        pulled, part = norm_pull(hidden[rows], gains_in[1:2], rows_sum.rows(rows))
-        gains[1:2] += part
-        state = out_grad[rows].astype(F32) + pulled
-        state_grad[rows] = state
-        branch[rows] = (RES_SCALE * state).astype(BF16)
-        return carry
-
-    lax.fori_loop(0, ROWS // 32, step, 0)
-    gather = TensorGather(p, branch, branch_full, (ts, tr), local.at[0])
-    ups.along()
-    gather.forward()
-    downs.along()
-    rows_sum.finish()
-    gates.pair()
-    gather.finish()
+    gains[...] = gain_part[...]
 
     out_weight = small[0, :, :, 256:384].reshape(WIDTH, 128)
     for b in range(WIDTH // QBLOCK):
@@ -478,7 +573,6 @@
         key_grad[:length] += tn(score_grad, query)
         query_grad = unstacked(nn(score_grad, keys[:length])) * ATT_SCALE
         pre[rows, :128] = rotate(query_grad, tables[0, rows], -tables[1, rows]).astype(BF16)
-    ups.pair()
     low = lanes(WIDTH) < HEAD_SIZE
     key_sum = key_grad[...] + pltpu.roll(key_grad[...], HEAD_SIZE, 1)
     value_sum = value_grad[...] + pltpu.roll(value_grad[...], HEAD_SIZE, 1)
@@ -494,6 +588,7 @@
 
     lax.fori_loop(0, WIDTH // QBLOCK, give, 0)
     input_sum = TensorScatter(p, partial, *more_sums)
+    moe_sum.exchange()
 
     def weigh(i, carry):
         columns = pl.ds(pl.multiple_of(i * 256, 256), 256)
@@ -501,25 +596,30 @@
         of_out = tn(branch_full[:, :, columns].reshape(WIDTH, 256), attended[...]).astype(BF16)
         for r in range(4):
             z = (i % 2) * 2 + r // 2
-            part = slice(r * PART, r * PART + PART)
-            small_grads[0, i // 2, z, r % 2, :, :256] = of_qkv[part]
-            small_grads[0, i // 2, z, r % 2, :, 256:384] = of_out[part]
+            piece = slice(r * PART, r * PART + PART)
+            small_grads[0, i // 2, z, r % 2, :, :256] = of_qkv[piece]
+            small_grads[0, i // 2, z, r % 2, :, 256:384] = of_out[piece]
             small_grads[0, i // 2, z, r % 2, :, 384:] = jnp.zeros((PART, 128), BF16)
         return carry
 
     lax.fori_loop(0, 4, weigh, 0)
-    smalls = PartScatter(p, small_grads, *parts[3])
-    downs.pair()
+    smalls = PartScatter(p, *part)
+    moe_sum.arrive()
+
+    def give_block(i, carry):
+        rows = pl.ds(pl.multiple_of(i * 32, 32), 32)
+        block_out[rows] = (hidden[rows] + RES_SCALE * moe_sum.rows(rows)).astype(BF16)
+        return carry
+
+    lax.fori_loop(0, ROWS // 32, give_block, 0)
     smalls.along()
-    gates.finish(gate_out)
-    ups.finish(up_out)
     input_sum.exchange()
     input_sum.arrive()
 
     def last(i, carry):
         rows = pl.ds(pl.multiple_of(i * 32, 32), 32)
-        pulled, part = norm_pull(x[rows].astype(F32), gains_in[0:1], input_sum.rows(rows))
-        gains[0:1] += part
+        pulled, found = norm_pull(x[rows].astype(F32), gains_in[0:1], input_sum.rows(rows))
+        gains[0:1] += found
         input_grad[rows] = (state_grad[rows] + pulled).astype(BF16)
         return carry
 
@@ -530,7 +630,7 @@
     stages = (
         [p.x_dev(j) for j in range(1, NX)], [p.tensor_pair()], [p.core_dev()],
         [p.z_dev(j) for j in range(1, NZ)], [p.y_dev()])
-    between = (smalls.pair, lambda: downs.finish(down_out), lambda: smalls.finish(small_out), None, None)
+    between = (smalls.pair, lambda: smalls.finish(((small_out, 0),)), None, None, None)
     for stage, (devices, work) in enumerate(zip(stages, between)):
         gain_buf[9 + stage] = gains[...]
         now = [push(gain_buf.at[9 + stage], gain_buf.at[number + k], (gs, gr), number + k, device)
@@ -542,28 +642,25 @@
             gains[...] += gain_buf[number + k]
         number += len(devices)
         copies += now
+    moe_sum.finish()
     input_sum.finish()
     for copy in copies:
         copy.wait_send()
 
 
-def backward(rows_partial, gate_grads, up_grads, down_grads, *rest):
-    weight = shape((4, PART, UNITS), F32)
+def backward(*args):
+    rows = shape((ROWS, WIDTH))
     return pl.pallas_call(
         backward_kernel,
-        out_shape=(
-            shape((ROWS, WIDTH)), weight, weight, weight, shape((1, PART, UNITS), F32), shape((8, WIDTH), F32)),
-        in_specs=[ANY] * 4 + [VMEM] * 10, out_specs=(VMEM,) * 6,
+        out_shape=(rows, rows, shape((1, PART, UNITS), F32), shape((8, WIDTH), F32)),
+        in_specs=[ANY] + [VMEM] * 12, out_specs=(VMEM,) * 4,
         scratch_shapes=[
-            pltpu.VMEM((ROWS, WIDTH), BF16), pltpu.VMEM((8, ROWS, WIDTH), BF16), pltpu.VMEM((ROWS, WIDTH), F32),
             pltpu.VMEM((WIDTH, 128), BF16), pltpu.VMEM((WIDTH, 128), BF16),
             pltpu.VMEM((WIDTH, 128), F32), pltpu.VMEM((WIDTH, 128), F32), pltpu.VMEM((WIDTH, 256), BF16),
-            pltpu.VMEM((8, ROWS, WIDTH), BF16), pltpu.VMEM((1, 2, NZ, 2, PART, UNITS), BF16),
-            pltpu.VMEM((14, 8, WIDTH), F32)]
-        + TensorScatter.scratch() * 2 + PartScatter.scratch(4) * 3 + PartScatter.scratch(1)
-        + sems(7) + sems(9) + [DMA((1,))],
-        compiler_params=params(2, 60), name="backward",
-    )(rows_partial, gate_grads, up_grads, down_grads, *rest)
+            pltpu.VMEM((8, ROWS, WIDTH), BF16), pltpu.VMEM((14, 8, WIDTH), F32)]
+        + TensorScatter.scratch() * 2 + PartScatter.scratch(1) + sems(9),
+        compiler_params=params(3, 56), name="backward",
+    )(*args)
 
 
 def rotary_tables(length):
@@ -580,10 +677,6 @@
         jnp.concatenate([sine, jnp.zeros_like(sine)], axis=1)])
 
 
-def mm(a, b, spec):
-    return jnp.einsum(spec, a, b, preferred_element_type=F32)
-
-
 def local(
     inputs, first_gain, query_weight, key_matrix, value_matrix, output_weight, second_gain,
     gate_weight, up_weight, down_weight, expert_ids, gate_values, out_grad,
@@ -609,26 +702,11 @@
     expert_index = rank * experts + jnp.arange(experts, dtype=jnp.int32)
     combined = jnp.sum(
         jnp.where(expert_ids[:, :, None] == expert_index, gate_values[:, :, None], 0.0), axis=1)
-    gate = mm(normed_two, gate_full, "sd,edf->esf")
-    up = mm(normed_two, up_full, "sd,edf->esf")
-    sig = jax.nn.sigmoid(gate)
-    scale = combined.T[:, :, None]
-    hidden_units = (scale * (gate * sig * up)).astype(BF16)
-    moe_partial = mm(hidden_units, down_full, "esf,edf->sd")
-    moe_local = lax.psum_scatter(
-        moe_partial.astype(BF16), "tensor", scatter_dimension=0, tiled=True).astype(F32)
-    block_output = (hidden + RES_SCALE * moe_local).astype(BF16)
-    hidden_grad = mm(out_grad_full, down_full, "sd,edf->esf") * (RES_SCALE * scale)
-    gate_pre = (hidden_grad * up * sig * (1.0 + gate * (1.0 - sig))).astype(BF16)
-    up_pre = (hidden_grad * gate * sig).astype(BF16)
-    rows_grad = mm(gate_pre, gate_full, "esf,edf->sd") + mm(up_pre, up_full, "esf,edf->sd")
-    gate_grad = mm(normed_two, gate_pre, "sd,esf->edf").astype(BF16)
-    up_grad = mm(normed_two, up_pre, "sd,esf->edf").astype(BF16)
-    down_grad = (mm(out_grad_full, hidden_units, "sd,esf->edf") * RES_SCALE).astype(BF16)
-    parts = (experts, 2, NZ, 2, PART, UNITS)
-    input_grad, gate_grad, up_grad, down_grad, small_grad, gains = backward(
-        rows_grad.astype(BF16).reshape(-1, ROWS, WIDTH), gate_grad.reshape(parts), up_grad.reshape(parts),
-        down_grad.reshape(parts), hidden, gains, out_grad, inputs, normed, qkv, attended, log_total, small, tables)
+    moe_partial, branch_full, state_grad, gain_part, gate_grad, up_grad, down_grad = run_experts(
+        normed_two, out_grad_full, gate_full, up_full, down_full, combined, hidden, gains, out_grad)
+    block_output, input_grad, small_grad, gains = backward(
+        moe_partial, branch_full, state_grad, gain_part, hidden, gains, inputs, normed, qkv, attended, log_total,
+        small, tables)
     small_grad = small_grad[0]
     gains = lax.dynamic_slice_in_dim(gains, lax.axis_index("dp") * PART, PART, 1)
     return (

time: 360 us -> 304 us (0.84); the launches traced: 355 us -> 303 us
  matrix products: 81.1 us -> 0 us
  Pallas kernels: 221 us -> 283 us
  local copies, waits for them, and re-layouts: 31.7 us -> 14.2 us
  between operations: 14.5 us -> 0.73 us
    dot_general x9 -> x0, matrix products: 81.1 us -> none  [mm(): return jnp.einsum(spec, a, b, preferred_element_type=F32)]
    pallas_call x1 -> x2, Pallas kernels: 112 us -> 175 us  [the longest x1 102 us: run_experts(): pl.pallas_call(experts_kernel, out_shape=(rows, rows, shape((ROWS, WIDTH)...]
    convert_element_type x3 -> x0, local copies, waits for them, and re-layouts: 18.7 us -> none  [the longest x1 6.28 us: local(): (mm(out_grad_full, hidden_units, 'sd,esf->edf') * RES_SCALE).astype(BF16)]
  transfers between devices with their start and end apart: 1 -> 0, of which waited for: 0 -> 0; matrix products, arithmetic and copies ran while one was open for 17% -> 0% of each run, Pallas kernels for 32% -> 0%
where the time goes in v3:
time: 304 us; the launch traced here: 303 us
  Pallas kernels  283 us (93%)
  local copies, waits for them, and re-layouts  14.2 us (5%)
  other arithmetic  5.14 us (2%)
    pallas_call x1, Pallas kernels, forward(): pl.pallas_call(forward_kernel, out_shape=(shape((ROWS, WIDTH), F32), rows...  109 us
    pallas_call x1, Pallas kernels, run_experts(): pl.pallas_call(experts_kernel, out_shape=(rows, rows, shape((ROWS, WIDTH)...  102 us
    pallas_call x1, Pallas kernels, backward(): pl.pallas_call(backward_kernel, out_shape=(rows, rows, shape((1, PART, UN...  73.1 us

profile of v3, /device:TPU:1, one launch (start us, length us, event | category | flops | bytes accessed | tf_op | source)
XLA Modules:
  0.0 303.5 jit_solution(1385331499049108268)
XLA Ops:
  0.7 0.1 pad.9.clone
  0.7 0.1 pad.6.clone
  0.8 0.9 select_reduce_fusion
  1.7 0.8 copy.28
  2.5 0.8 copy.29
  3.3 1.5 concatenate.21
  4.8 1.0 copy.30.combined
  5.8 1.9 multiply_cosine_fusion
  7.7 0.9 maximum_bitcast_fusion
  8.6 1.5 pad_maximum_fusion.tables
  10.0 108.8 %forward.1 = (f32[128,1024]{1,0:T(8,128)}, bf16[8,128,1024]{2,1,0:T(8,128)(2,1)}, bf16[8,128,1024]{2,1,0:T(8,128)(2,1)}, bf16[4,16,64,512]{3,2,1,0:T(8,128)(2,1)...) custom-call(bf16[128,1024]{1,0:T(8,128)(2,1)} %x.3, ...), custom_call_target="tpu_custom_call" | custom-call | tf_op jit(solution)/shard_map/forward/pallas_call | solution.py:392
  118.8 101.5 %experts.1 = (bf16[8,128,1024]{2,1,0:T(8,128)(2,1)}, bf16[8,128,1024]{2,1,0:T(8,128)(2,1)}, f32[128,1024]{1,0:T(8,128)}, f32[8,1024]{1,0:T(8,128)}, f32[4,64,512...) custom-call(bf16[1024,1024]{1,0:T(8,128)(2,1)} %bitcast.29, bf16[1024,1024]{1,0:T(8,128)(2,1)} %bitcast.30, ...), custom_call_target="tpu_custom_call" | custom-call | tf_op jit(solution)/shard_map/experts/pallas_call | solution.py:530
  220.4 0.0 copy-start.2
  220.4 73.1 %backward.1 = (bf16[128,1024]{1,0:T(8,128)(2,1)}, bf16[128,1024]{1,0:T(8,128)(2,1)}, f32[1,64,512]{2,1,0:T(8,128)}, f32[8,1024]{1,0:T(8,128)}) custom-call(bf16[8,128,1024]{2,1,0:T(8,128)(2,1)} %get-tuple-element.41.moe_partial, bf16[8,128,1024]{2,1,0:T(8,128)(2,1)} %get-tuple-element.42.branch_full, f32[128,1024]{1,0:T(8,128)} %get-tuple-element.43.state_grad, ...), custom_call_target="tpu_custom_call" | custom-call | tf_op jit(solution)/shard_map/backward/pallas_call | solution.py:653
  293.5 0.0 copy-start.1
  293.5 0.0 copy-start
  293.5 0.8 constant_dynamic-slice_fusion
  294.3 0.5 slice_bitcast_fusion.1
  294.8 1.4 slice_bitcast_fusion
  296.2 1.5 fusion.5
  297.8 1.7 copy.36
  299.4 1.7 copy.37
  301.1 0.0 copy-done.2
  301.1 0.8 copy.38
  301.9 0.0 copy-done.1
  301.9 0.8 copy.39
  302.7 0.0 copy-done
  302.7 0.8 copy.40
  (6 shorter events, 0.0 us)
Async XLA Ops:
  220.4 80.7 %copy-start.2 = (f32[4,64,512]{2,1,0:T(8,128)S(1)}, f32[4,64,512]{2,1,0:T(8,128)}, u32[]{:S(2)}) copy-start(f32[4,64,512]{2,1,0:T(8,128)} %get-tuple-element.91) | copy-start | bytes 1572868
  293.5 8.4 %copy-start.1 = (f32[4,64,512]{2,1,0:T(8,128)S(1)}, f32[4,64,512]{2,1,0:T(8,128)}, u32[]{:S(2)}) copy-start(f32[4,64,512]{2,1,0:T(8,128)} %get-tuple-element.92) | copy-start | bytes 1572868
  293.5 9.2 %copy-start = (f32[4,64,512]{2,1,0:T(8,128)S(1)}, f32[4,64,512]{2,1,0:T(8,128)}, u32[]{:S(2)}) copy-start(f32[4,64,512]{2,1,0:T(8,128)} %get-tuple-element.56) | copy-start | bytes 1572868

commit v4 on v3

--- a/solution.py
+++ b/solution.py
@@ -2,6 +2,7 @@
 
 import jax
 import jax.numpy as jnp
+import numpy as np
 from jax import lax
 from jax.experimental import pallas as pl
 from jax.experimental.pallas import tpu as pltpu
@@ -80,58 +81,130 @@
 
 
 class TensorGather:
-    SEMS = 7
+    SEMS = 9
 
     def __init__(self, p, src, out, sem, local_sem):
         self.p, self.out, self.sem = p, out, sem
         self.copies = [push(src, out.at[p.t], sem, 0, p.tensor_pair())]
-        self.copies += [push(src, out.at[p.t], sem, j, p.x_dev(j)) for j in range(1, NX)]
+        self.copies += [push(src, out.at[p.t], sem, 1 + k, p.x_dev(j)) for k, j in enumerate((1, 3))]
         self.own = pltpu.make_async_copy(src, out.at[p.t], local_sem)
         self.own.start()
 
+    def resend(self, block, number, j):
+        self.copies.append(push(block, block, self.sem, number, self.p.x_dev(j)))
+
     def forward(self):
-        p = self.p
         self.copies[0].wait_recv()
-        self.copies += [
-            push(self.out.at[p.pair], self.out.at[p.pair], self.sem, 3 + j, p.x_dev(j)) for j in range(1, NX)]
-
-    def finish(self):
-        for copy in self.copies[1:]:
+        for k, j in enumerate((1, 3)):
+            self.resend(self.out.at[self.p.pair], 3 + k, j)
+
+    def relay(self):
+        p = self.p
+        for k, (back, on) in enumerate(((3, 1), (1, 3))):
+            for c, first in ((p.ty, 1), (1 - p.ty, 3)):
+                self.copies[first + k].wait_recv()
+                half = self.out.at[p.x(back) * NY + c, pl.ds(k * (ROWS // 2), ROWS // 2)]
+                self.resend(half, 4 + first + k, on)
+
+    def arrive(self):
+        for copy in self.copies[5:]:
             copy.wait_recv()
+
+    def sent(self):
         for copy in self.copies:
             copy.wait_send()
+
+    def finish(self):
+        self.arrive()
+        self.sent()
         self.own.wait()
 
 
 class TensorScatter:
-    SEMS = 7
+    STEPS = (2, 1, 3)
 
     @staticmethod
     def scratch():
-        return [pltpu.VMEM((NX, NY, ROWS, WIDTH), BF16), pltpu.VMEM((2, ROWS, WIDTH), BF16)] + sems(7) + [DMA((1,))]
-
-    def __init__(self, p, partial, got, pair_buf, send, recv, local):
-        self.p, self.got, self.pair_buf = p, got, pair_buf
+        half = pltpu.VMEM((2, NY, ROWS // 2, WIDTH), BF16)
+        return [pltpu.VMEM((3, NY, ROWS, WIDTH), BF16), half, half, pltpu.VMEM((2, ROWS, WIDTH), BF16)] + sems(13) + [
+            DMA((1,))]
+
+    def __init__(self, p, partial, got, via, merged, pair_buf, send, recv, local):
+        self.p, self.partial, self.got, self.pair_buf = p, partial, got, pair_buf
+        self.via, self.merged = via, merged
         self.sem = (send, recv)
-        self.copies = []
-        for half, c in enumerate((1 - p.ty, p.ty)):
-            self.copies.append([
-                push(partial.at[p.x(j) * NY + c], got.at[j, c], self.sem, half * 3 + j - 1, p.x_dev(j))
-                for j in range(1, NX)])
-        self.own = pltpu.make_async_copy(partial.at[pl.ds(p.tx * NY, NY)], got.at[0], local.at[0])
+        self.own = pltpu.make_async_copy(partial.at[pl.ds(p.tx * NY, NY)], got.at[2], local.at[0])
+
+    def half(self, k):
+        return pl.ds(k * (ROWS // 2), ROWS // 2)
+
+    def copy(self, kind, k, order):
+        p = self.p
+        c = p.ty if order else 1 - p.ty
+        number = kind * 4 + order * 2 + k
+        j = (1, 3)[k]
+        if kind == 0:
+            src, dst = self.partial.at[p.x(2) * NY + c, self.half(k)], self.via.at[k, c]
+        elif kind == 1:
+            src, dst = self.partial.at[p.x(j) * NY + c, self.half(1 - k)], self.got.at[k, c, self.half(1 - k)]
+        else:
+            src, dst = self.merged.at[k, c], self.got.at[k, c, self.half(k)]
+        return pltpu.make_async_remote_copy(
+            src_ref=src, dst_ref=dst, send_sem=self.sem[0].at[number], recv_sem=self.sem[1].at[number],
+            device_id=p.x_dev(j), device_id_type=MESH)
+
+    def send(self, j):
+        for order in range(2):
+            if j == 2:
+                self.copy(0, 0, order).start()
+                self.copy(0, 1, order).start()
+            else:
+                self.copy(1, (1, 3).index(j), order).start()
+
+    def row(self, step):
+        return self.p.x((2 + 3 * step + 3 * (step // 2) + 2 * (step // 3)) % NX)
+
+    def send_after(self, step):
+        for number, j in enumerate(self.STEPS):
+            pl.when(step == number)(functools.partial(self.send, j))
+
+    def send_all(self):
+        for j in self.STEPS:
+            self.send(j)
         self.own.start()
+
+    def relay(self):
+        p = self.p
+        for order in range(2):
+            c = p.ty if order else 1 - p.ty
+            for k in range(2):
+                self.copy(0, k, order).wait_recv()
+                block = p.x((1, 3)[k]) * NY + c
+
+                def step(i, carry):
+                    rows = pl.ds(pl.multiple_of(i * 32, 32), 32)
+                    mine = self.partial[block, pl.ds(pl.multiple_of(k * (ROWS // 2) + i * 32, 32), 32)]
+                    self.merged[k, c, rows] = (mine.astype(F32) + self.via[k, c, rows].astype(F32)).astype(BF16)
+                    return carry
+
+                lax.fori_loop(0, ROWS // 64, step, 0)
+                self.copy(2, k, order).start()
 
     def total(self, c, rows):
         value = self.got[0, c, rows].astype(F32)
-        for j in range(1, NX):
-            value = value + self.got[j, c, rows].astype(F32)
+        for k in range(1, 3):
+            value = value + self.got[k, c, rows].astype(F32)
         return value
 
+    def wait_near(self, order):
+        for k in range(2):
+            self.copy(1, k, order).wait_recv()
+            self.copy(2, k, order).wait_recv()
+
     def exchange(self):
         p = self.p
         self.own.wait()
-        for copy in self.copies[0]:
-            copy.wait_recv()
+        self.wait_near(0)
 
         def step(i, carry):
             rows = pl.ds(pl.multiple_of(i * 32, 32), 32)
@@ -139,54 +212,71 @@
             return carry
 
         lax.fori_loop(0, ROWS // 32, step, 0)
-        self.pair = push(self.pair_buf.at[0], self.pair_buf.at[1], self.sem, 6, p.tensor_pair())
+        self.pair = push(self.pair_buf.at[0], self.pair_buf.at[1], self.sem, 12, p.tensor_pair())
 
     def arrive(self):
-        for copy in self.copies[1]:
-            copy.wait_recv()
+        self.wait_near(1)
         self.pair.wait_recv()
 
     def rows(self, rows):
         return self.total(self.p.ty, rows) + self.pair_buf[1, rows].astype(F32)
 
     def finish(self):
-        for copy in self.copies[0] + self.copies[1] + [self.pair]:
-            copy.wait_send()
+        for kind in range(3):
+            for order in range(2):
+                for k in range(2):
+                    self.copy(kind, k, order).wait_send()
+        self.pair.wait_send()
 
 
 class PartGather:
-    SEMS = 15
+    SEMS = 17
 
     def __init__(self, p, shard, out, sem, local_sem):
         self.p, self.out, self.sem = p, out, sem
         mine = out.at[:, p.d]
-        self.pair = push(shard, mine, sem, 0, p.y_dev())
-        self.along = [push(shard, mine, sem, j, p.z_dev(j)) for j in range(1, NZ)]
-        self.core = [push(shard, mine, sem, 4, p.core_dev())]
+        self.copies = [push(shard, mine, sem, 0, p.y_dev())]
+        self.copies += [push(shard, mine, sem, 1 + k, p.z_dev(j)) for k, j in enumerate((1, 3))]
+        self.core = [push(shard, mine, sem, 3, p.core_dev())]
+        self.halves = []
         self.own = pltpu.make_async_copy(shard, mine, local_sem)
         self.own.start()
 
-    def resend(self, index, number, device):
-        return push(self.out.at[:, index], self.out.at[:, index], self.sem, number, device)
+    def resend(self, block, number, device):
+        return push(block, block, self.sem, number, device)
 
     def forward(self):
         p = self.p
-        self.pair.wait_recv()
-        self.along_pair = [self.resend(p.d_pair, 4 + j, p.z_dev(j)) for j in range(1, NZ)]
-        self.core.append(self.resend(p.d_pair, 8, p.core_dev()))
+        self.copies[0].wait_recv()
+        block = self.out.at[:, p.d_pair]
+        self.copies += [self.resend(block, 4 + k, p.z_dev(j)) for k, j in enumerate((1, 3))]
+        self.core.append(self.resend(block, 6, p.core_dev()))
+
+    def index(self, j, pair):
+        p = self.p
+        return p.dp(1 - p.dy if pair else p.dy, p.z(j), p.dc)
 
     def spread(self):
         p = self.p
-        for first, copies, y in ((9, self.along, p.dy), (12, self.along_pair, 1 - p.dy)):
-            for j in range(1, NZ):
-                copies[j - 1].wait_recv()
-                index = p.dp(y, (p.dz + NZ - j) % NZ, p.dc)
-                self.core.append(self.resend(index, first + j - 1, p.core_dev()))
+        for pair in range(2):
+            for k, (back, on) in enumerate(((3, 1), (1, 3))):
+                self.copies[1 + 2 * pair + k].wait_recv()
+                index = self.index(back, pair)
+                half = self.out.at[:, index, pl.ds(k * (PART // 2), PART // 2)]
+                self.halves.append(self.resend(half, 7 + 2 * pair + k, p.z_dev(on)))
+                self.core.append(self.resend(self.out.at[:, index], 11 + 2 * pair + k, p.core_dev()))
+
+    def far(self):
+        p = self.p
+        for copy in self.halves:
+            copy.wait_recv()
+        self.core += [
+            self.resend(self.out.at[:, self.index(2, pair)], 15 + pair, p.core_dev()) for pair in range(2)]
 
     def finish(self):
         for copy in self.core:
             copy.wait_recv()
-        for copy in [self.pair] + self.along + self.along_pair + self.core:
+        for copy in self.copies + self.halves + self.core:
             copy.wait_send()
         self.own.wait()
 
@@ -197,15 +287,32 @@
         return [
             pltpu.VMEM((n, 2, NZ, 2, PART, UNITS), BF16),
             pltpu.VMEM((n, 2, NZ, PART, UNITS), BF16),
-            pltpu.VMEM((NZ - 1, n, 2, PART, UNITS), BF16),
+            pltpu.VMEM((2, n, 2, PART, UNITS), BF16),
+            pltpu.VMEM((2, n, 2, PART // 2, UNITS), BF16),
             pltpu.VMEM((2, n, PART, UNITS), BF16),
-        ] + sems(5)
-
-    def __init__(self, p, grads, core_buf, z_buf, y_buf, send, recv):
+        ] + sems(8)
+
+    def __init__(self, p, grads, core_buf, z_buf, via, y_buf, send, recv):
         self.p, self.n = p, grads.shape[0]
-        self.grads, self.core_buf, self.z_buf, self.y_buf = grads, core_buf, z_buf, y_buf
+        self.grads, self.core_buf, self.z_buf, self.via, self.y_buf = grads, core_buf, z_buf, via, y_buf
         self.sem = (send, recv)
         self.core = push(grads.at[:, :, :, 1 - p.dc], core_buf, self.sem, 0, p.core_dev())
+
+    def half(self, k):
+        return pl.ds(k * (PART // 2), PART // 2)
+
+    def copy(self, kind, k):
+        p = self.p
+        j = (1, 3)[k]
+        if kind == 0:
+            src, dst = self.grads.at[:, :, p.z(2), p.dc, self.half(k)], self.via.at[k]
+        else:
+            half = self.half(1 - k if kind == 1 else k)
+            src, dst = self.grads.at[:, :, p.z(j), p.dc, half], self.z_buf.at[k, :, :, half]
+        number = 1 + kind * 2 + k
+        return pltpu.make_async_remote_copy(
+            src_ref=src, dst_ref=dst, send_sem=self.sem[0].at[number], recv_sem=self.sem[1].at[number],
+            device_id=p.z_dev(j), device_id_type=MESH)
 
     def along(self):
         p = self.p
@@ -219,34 +326,50 @@
             return carry
 
         lax.fori_loop(0, self.n, step, 0)
-        self.z_copies = [
-            push(self.grads.at[:, :, p.z(j), p.dc], self.z_buf.at[j - 1], self.sem, j, p.z_dev(j))
-            for j in range(1, NZ)]
+        for kind in range(2):
+            for k in range(2):
+                self.copy(kind, k).start()
+
+    def relay(self):
+        p = self.p
+        for k, j in enumerate((1, 3)):
+            self.copy(0, k).wait_recv()
+            z = p.z(j)
+
+            def step(i, carry):
+                for y in range(2):
+                    total = self.grads[i, y, z, p.dc, self.half(k)].astype(F32) + self.via[k, i, y].astype(F32)
+                    self.grads[i, y, z, p.dc, self.half(k)] = total.astype(BF16)
+                return carry
+
+            lax.fori_loop(0, self.n, step, 0)
+            self.copy(2, k).start()
 
     def total(self, i, y):
         value = self.grads[i, y, self.p.dz, self.p.dc].astype(F32)
-        for j in range(NZ - 1):
-            value = value + self.z_buf[j, i, y].astype(F32)
+        for k in range(2):
+            value = value + self.z_buf[k, i, y].astype(F32)
         return value
 
     def pair(self):
         p = self.p
-        for copy in self.z_copies:
-            copy.wait_recv()
+        for kind in (1, 2):
+            for k in range(2):
+                self.copy(kind, k).wait_recv()
 
         def step(i, carry):
             self.y_buf[0, i] = self.total(i, 1 - p.dy).astype(BF16)
             return carry
 
         lax.fori_loop(0, self.n, step, 0)
-        self.y_copy = push(self.y_buf.at[0], self.y_buf.at[1], self.sem, 4, p.y_dev())
+        self.y_copy = push(self.y_buf.at[0], self.y_buf.at[1], self.sem, 7, p.y_dev())
 
     def finish(self, outs):
         p = self.p
         self.y_copy.wait_recv()
         for i, (out, slot) in enumerate(outs):
             out[slot] = self.total(i, p.dy) + self.y_buf[1, i].astype(F32)
-        for copy in [self.core, self.y_copy] + self.z_copies:
+        for copy in [self.core, self.y_copy] + [self.copy(kind, k) for kind in range(3) for k in range(2)]:
             copy.wait_send()
 
 
@@ -313,7 +436,7 @@
 ):
     p = Place()
     meet(p)
-    branch_scratch, scratch = scratch[:5], scratch[5:]
+    branch_scratch, scratch = scratch[:7], scratch[7:]
     pairs = [scratch[2 * i : 2 * i + 2] for i in range(7)]
     local = scratch[14]
     smalls = PartGather(p, small, small_out, pairs[0], local.at[0])
@@ -322,14 +445,13 @@
     rows_in.forward()
     gates = PartGather(p, gate, gate_out, pairs[2], local.at[2])
     smalls.spread()
+    smalls.far()
     ups = PartGather(p, up, up_out, pairs[3], local.at[3])
+    downs = PartGather(p, down, down_out, pairs[5], local.at[5])
     smalls.finish()
     pick = (lax.broadcasted_iota(jnp.int32, (8, 128), 0) == lax.broadcasted_iota(jnp.int32, (8, 128), 1))
     gains[...] = nt(pick.astype(F32).astype(BF16), small_out[0, :, :, 384:].reshape(WIDTH, 128))
     gates.forward()
-    rows_in.finish()
-    grads = TensorGather(p, out_grad, grad_out, pairs[4], local.at[4])
-    downs = PartGather(p, down, down_out, pairs[5], local.at[5])
     qkv_weight = small_out[0, :, :, :256].reshape(WIDTH, 256)
 
     def project(i, carry):
@@ -343,11 +465,21 @@
         qkv[rows, 128:] = rotate(pre[:, 128:], tables[2, rows], tables[3, rows]).astype(BF16)
         return carry
 
-    lax.fori_loop(0, 8, project, 0)
+    rows_in.own.wait()
+    lax.fori_loop(p.tx * NY, p.tx * NY + NY, project, 0)
     ups.forward()
-    grads.forward()
+    rows_in.relay()
+    grads = TensorGather(p, out_grad, grad_out, pairs[4], local.at[4])
+    for j in (1, 3, 2):
+        if j == 2:
+            rows_in.arrive()
+            downs.forward()
+            grads.forward()
+        start = p.x(j) * NY
+        lax.fori_loop(start, start + NY, project, 0)
     doubled(qkv[:, 128:], keys, values)
     out_weight = small_out[0, :, :, 256:384].reshape(WIDTH, 128)
+    branch = TensorScatter(p, partial, *branch_scratch)
     for b in range(WIDTH // QBLOCK):
         length = (b + 1) * QBLOCK
         rows = pl.ds(b * QBLOCK, QBLOCK)
@@ -359,11 +491,17 @@
         out = unstacked(nn((terms / total).astype(BF16), values[:length])).astype(BF16)
         attended[rows] = out
         partial[2 * b : 2 * b + 2] = nt(out, out_weight).astype(BF16).reshape(2, ROWS, WIDTH)
-    branch = TensorScatter(p, partial, *branch_scratch)
-    gates.spread()
-    downs.forward()
+        for j in range(1, NX):
+            pl.when(p.x(j) == b)(functools.partial(branch.send, j))
+        if b == 1:
+            grads.relay()
+            gates.spread()
+    branch.own.start()
+    branch.relay()
+    ups.spread()
+    gates.far()
     branch.exchange()
-    ups.spread()
+    downs.spread()
     branch.arrive()
 
     def step(i, carry):
@@ -377,9 +515,12 @@
     lax.fori_loop(0, ROWS // 32, step, 0)
     gather = TensorGather(p, normed_two, normed_out, pairs[6], local.at[6])
     gather.forward()
-    downs.spread()
+    ups.far()
+    gather.relay()
+    downs.far()
     branch.finish()
     gather.finish()
+    rows_in.sent()
     grads.finish()
     gates.finish()
     ups.finish()
@@ -400,7 +541,7 @@
         scratch_shapes=[
             pltpu.VMEM((8, ROWS, WIDTH), BF16), pltpu.VMEM((WIDTH, 128), BF16), pltpu.VMEM((WIDTH, 128), BF16),
             pltpu.VMEM((8, ROWS, WIDTH), BF16), pltpu.VMEM((ROWS, WIDTH), BF16)]
-        + TensorScatter.scratch() + sems(15) + sems(7) + sems(15) + sems(15) + sems(7) + sems(15) + sems(7)
+        + TensorScatter.scratch() + sems(17) + sems(9) + sems(17) + sems(17) + sems(9) + sems(17) + sems(9)
         + [DMA((7,))],
         compiler_params=params(1, 56), name="forward",
     )(x, small, gate, up, down, out_grad, tables)
@@ -420,9 +561,9 @@
 ):
     p = Place()
     load_sem, scratch = scratch[0], scratch[1:]
-    sums, scratch = scratch[:5], scratch[5:]
-    parts = [scratch[6 * e : 6 * e + 6] for e in range(4)]
-    ts, tr, local = scratch[24:]
+    sums, scratch = scratch[:7], scratch[7:]
+    parts = [scratch[7 * e : 7 * e + 7] for e in range(4)]
+    ts, tr, local = scratch[28:]
 
     def load(e):
         slot = e % 2
@@ -436,6 +577,30 @@
     meet(p)
     gain_part[...] = jnp.zeros_like(gain_part)
     scatters = []
+    rows_sum = TensorScatter(p, rows_out, *sums)
+
+    def weigh_expert(e):
+        grads = parts[e][0]
+
+        def weigh(i, carry):
+            columns = pl.ds(pl.multiple_of(i * 256, 256), 256)
+            tokens = x[:, columns]
+            found = (
+                tn(tokens, gate_pre[e % 2]), tn(tokens, up_pre[e % 2]),
+                tn(out_grad_full[:, columns], units[e % 2]) * RES_SCALE)
+            for k in range(3):
+                for r in range(4):
+                    z = (i % 2) * 2 + r // 2
+                    grads[k, i // 2, z, r % 2] = found[k][r * PART : r * PART + PART].astype(BF16)
+            return carry
+
+        lax.fori_loop(0, 4, weigh, 0)
+        scatters.append(PartScatter(p, *parts[e]))
+        if e == 1:
+            scatters[0].relay()
+        if e == 3:
+            scatters[2].along()
+
     for e in range(4):
         slot = e % 2
         for copy in loads:
@@ -445,7 +610,8 @@
             for copy in loads:
                 copy.start()
 
-        def block(i, carry):
+        def block(step, carry):
+            i = rows_sum.row(step)
             rows = pl.ds(pl.multiple_of(i * QBLOCK, QBLOCK), QBLOCK)
             tokens = x[rows]
             gate_part = nn(tokens, gate_buf[slot])
@@ -457,9 +623,9 @@
             grad = nn(out_grad_full[rows], down_buf[slot]) * (RES_SCALE * scale)
             to_gate = (grad * up_part * (sig + act * (1.0 - sig))).astype(BF16)
             to_up = (grad * act).astype(BF16)
-            units[rows] = unit
-            gate_pre[rows] = to_gate
-            up_pre[rows] = to_up
+            units[slot, rows] = unit
+            gate_pre[slot, rows] = to_gate
+            up_pre[slot, rows] = to_up
             moe_part = nt(unit, down_buf[slot])
             rows_part = nt(to_gate, gate_buf[slot]) + nt(to_up, up_buf[slot])
             if e == 0:
@@ -472,33 +638,24 @@
                 blocks = pl.ds(2 * i, 2)
                 moe_out[blocks] = (moe[rows] + moe_part).astype(BF16).reshape(2, ROWS, WIDTH)
                 rows_out[blocks] = (rows_acc[rows] + rows_part).astype(BF16).reshape(2, ROWS, WIDTH)
+                rows_sum.send_after(step)
             return carry
 
         lax.fori_loop(0, WIDTH // QBLOCK, block, 0)
+        if e == 1 or e == 2:
+            scatters[e - 1].along()
         if e == 3:
-            rows_sum = TensorScatter(p, rows_out, *sums)
-        if e >= 1:
-            scatters[e - 1].along()
-        grads = parts[e][0]
-
-        def weigh(i, carry):
-            columns = pl.ds(pl.multiple_of(i * 256, 256), 256)
-            tokens = x[:, columns]
-            found = (
-                tn(tokens, gate_pre[...]), tn(tokens, up_pre[...]),
-                tn(out_grad_full[:, columns], units[...]) * RES_SCALE)
-            for k in range(3):
-                for r in range(4):
-                    z = (i % 2) * 2 + r // 2
-                    grads[k, i // 2, z, r % 2] = found[k][r * PART : r * PART + PART].astype(BF16)
-            return carry
-
-        lax.fori_loop(0, 4, weigh, 0)
-        scatters.append(PartScatter(p, *parts[e]))
-
+            rows_sum.own.start()
+            rows_sum.relay()
+            scatters[1].relay()
+        for done in ((0,), (1,), (), (2, 3))[e]:
+            weigh_expert(done)
+
+    scatters[0].pair()
+    scatters[3].along()
+    scatters[2].relay()
     rows_sum.exchange()
-    scatters[3].along()
-    scatters[0].pair()
+    scatters[1].pair()
     rows_sum.arrive()
 
     def step(i, carry):
@@ -512,9 +669,10 @@
 
     lax.fori_loop(0, ROWS // 32, step, 0)
     gather = TensorGather(p, branch, branch_out, (ts, tr), local.at[0])
-    scatters[1].pair()
+    scatters[3].relay()
     gather.forward()
     scatters[2].pair()
+    gather.relay()
     scatters[0].finish(((gate_out, 0), (up_out, 0), (down_out, 0)))
     scatters[1].finish(((gate_out, 1), (up_out, 1), (down_out, 1)))
     scatters[3].pair()
@@ -532,10 +690,10 @@
         out_shape=(rows, rows, shape((ROWS, WIDTH), F32), shape((8, WIDTH), F32), weight, weight, weight),
         in_specs=[VMEM, VMEM, ANY, ANY, ANY] + [VMEM] * 4, out_specs=(VMEM, ANY) + (VMEM,) * 5,
         scratch_shapes=[pltpu.VMEM((2, WIDTH, UNITS), BF16)] * 3 + [pltpu.VMEM((WIDTH, WIDTH), F32)] * 2
-        + [pltpu.VMEM((WIDTH, UNITS), BF16)] * 3
+        + [pltpu.VMEM((2, WIDTH, UNITS), BF16)] * 3
         + [pltpu.VMEM((8, ROWS, WIDTH), BF16), pltpu.VMEM((ROWS, WIDTH), BF16), DMA((2, 3))]
-        + TensorScatter.scratch() + PartScatter.scratch(3) * 4 + sems(7) + [DMA((1,))],
-        compiler_params=params(2, 62), name="experts",
+        + TensorScatter.scratch() + PartScatter.scratch(3) * 4 + sems(9) + [DMA((1,))],
+        compiler_params=params(2, 63), name="experts",
     )(*args)
 
 
@@ -547,12 +705,13 @@
 ):
     p = Place()
     meet(p)
-    sums, scratch = scratch[:5], scratch[5:]
-    more_sums, scratch = scratch[:5], scratch[5:]
-    part = scratch[:6]
+    sums, scratch = scratch[:7], scratch[7:]
+    more_sums, scratch = scratch[:7], scratch[7:]
+    part = scratch[:7]
     small_grads = part[0]
-    gs, gr = scratch[6:]
+    gs, gr = scratch[7:]
     moe_sum = TensorScatter(p, moe_partial, *sums)
+    moe_sum.send_all()
     doubled(qkv[:, 128:], keys, values)
     key_grad[...] = jnp.zeros_like(key_grad)
     value_grad[...] = jnp.zeros_like(value_grad)
@@ -560,6 +719,8 @@
 
     out_weight = small[0, :, :, 256:384].reshape(WIDTH, 128)
     for b in range(WIDTH // QBLOCK):
+        if b == 2:
+            moe_sum.relay()
         length = (b + 1) * QBLOCK
         rows = pl.ds(b * QBLOCK, QBLOCK)
         grad = stacked(nn(branch_full[2 * b : 2 * b + 2].reshape(QBLOCK, WIDTH), out_weight).astype(BF16))
@@ -581,14 +742,43 @@
 
     qkv_weight = small[0, :, :, :256].reshape(WIDTH, 256)
 
-    def give(b, carry):
+    input_sum = TensorScatter(p, partial, *more_sums)
+
+    def give(step, carry):
+        b = input_sum.row(step)
         rows = pl.ds(pl.multiple_of(b * QBLOCK, QBLOCK), QBLOCK)
-        partial[pl.ds(2 * b, 2)] = nt(pre[rows], qkv_weight).astype(BF16).reshape(2, ROWS, WIDTH)
+        found = nt(pre[rows], qkv_weight)
+        partial[pl.ds(2 * b, 2)] = found.astype(BF16).reshape(2, ROWS, WIDTH)
+        input_sum.send_after(step)
+        gains[0:1] += jnp.sum(found * normed[rows].astype(F32), axis=0, keepdims=True)
         return carry
 
     lax.fori_loop(0, WIDTH // QBLOCK, give, 0)
-    input_sum = TensorScatter(p, partial, *more_sums)
+    input_sum.own.start()
+    gains[0:1] = gains[0:1] / gains_in[0:1]
+
+    copies = []
+    stages = iter((
+        [p.x_dev(j) for j in range(1, NX)], [p.tensor_pair()], [p.core_dev()],
+        [p.z_dev(j) for j in range(1, NZ)], [p.y_dev()]))
+
+    def gains_send():
+        stage = len(copies)
+        first = sum(len(group) for group in copies)
+        gain_buf[9 + stage] = gains[...]
+        copies.append([
+            push(gain_buf.at[9 + stage], gain_buf.at[first + k], (gs, gr), first + k, device)
+            for k, device in enumerate(next(stages))])
+
+    def gains_add():
+        first = sum(len(group) for group in copies[:-1])
+        for k, copy in enumerate(copies[-1]):
+            copy.wait_recv()
+            gains[...] += gain_buf[first + k]
+
+    gains_send()
     moe_sum.exchange()
+    input_sum.relay()
 
     def weigh(i, carry):
         columns = pl.ds(pl.multiple_of(i * 256, 256), 256)
@@ -604,6 +794,8 @@
 
     lax.fori_loop(0, 4, weigh, 0)
     smalls = PartScatter(p, *part)
+    gains_add()
+    gains_send()
     moe_sum.arrive()
 
     def give_block(i, carry):
@@ -613,39 +805,31 @@
 
     lax.fori_loop(0, ROWS // 32, give_block, 0)
     smalls.along()
+    gains_add()
+    gains_send()
+    smalls.relay()
     input_sum.exchange()
+    gains_add()
+    gains_send()
+    smalls.pair()
+    gains_add()
+    gains_send()
     input_sum.arrive()
 
     def last(i, carry):
         rows = pl.ds(pl.multiple_of(i * 32, 32), 32)
-        pulled, found = norm_pull(x[rows].astype(F32), gains_in[0:1], input_sum.rows(rows))
-        gains[0:1] += found
+        pulled, _ = norm_pull(x[rows].astype(F32), gains_in[0:1], input_sum.rows(rows))
         input_grad[rows] = (state_grad[rows] + pulled).astype(BF16)
         return carry
 
     lax.fori_loop(0, ROWS // 32, last, 0)
-
-    number = 0
-    copies = []
-    stages = (
-        [p.x_dev(j) for j in range(1, NX)], [p.tensor_pair()], [p.core_dev()],
-        [p.z_dev(j) for j in range(1, NZ)], [p.y_dev()])
-    between = (smalls.pair, lambda: smalls.finish(((small_out, 0),)), None, None, None)
-    for stage, (devices, work) in enumerate(zip(stages, between)):
-        gain_buf[9 + stage] = gains[...]
-        now = [push(gain_buf.at[9 + stage], gain_buf.at[number + k], (gs, gr), number + k, device)
-               for k, device in enumerate(devices)]
-        if work is not None:
-            work()
-        for k, copy in enumerate(now):
-            copy.wait_recv()
-            gains[...] += gain_buf[number + k]
-        number += len(devices)
-        copies += now
+    gains_add()
+    smalls.finish(((small_out, 0),))
     moe_sum.finish()
     input_sum.finish()
-    for copy in copies:
-        copy.wait_send()
+    for group in copies:
+        for copy in group:
+            copy.wait_send()
 
 
 def backward(*args):
@@ -653,7 +837,7 @@
     return pl.pallas_call(
         backward_kernel,
         out_shape=(rows, rows, shape((1, PART, UNITS), F32), shape((8, WIDTH), F32)),
-        in_specs=[ANY] + [VMEM] * 12, out_specs=(VMEM,) * 4,
+        in_specs=[VMEM] * 13, out_specs=(VMEM,) * 4,
         scratch_shapes=[
             pltpu.VMEM((WIDTH, 128), BF16), pltpu.VMEM((WIDTH, 128), BF16),
             pltpu.VMEM((WIDTH, 128), F32), pltpu.VMEM((WIDTH, 128), F32), pltpu.VMEM((WIDTH, 256), BF16),
@@ -665,16 +849,17 @@
 
 def rotary_tables(length):
     half_width = HEAD_SIZE // 2
-    positions = jnp.arange(length).astype(F32)
-    frequencies = jnp.power(ROPE_BASE, -(jnp.arange(half_width).astype(F32) * 2.0 / HEAD_SIZE))
+    positions = np.arange(length).astype(np.float32)
+    frequencies = np.power(
+        np.float32(ROPE_BASE), -(np.arange(half_width).astype(np.float32) * np.float32(2.0 / HEAD_SIZE)))
     angles = positions[:, None] * frequencies[None, :]
-    cosine, sine = jnp.cos(angles), jnp.sin(angles)
-    cosine = jnp.concatenate([cosine, cosine], axis=1)
-    sine = jnp.concatenate([-sine, sine], axis=1)
-    return jnp.stack([
-        jnp.concatenate([cosine, cosine], axis=1), jnp.concatenate([sine, sine], axis=1),
-        jnp.concatenate([cosine, jnp.ones_like(cosine)], axis=1),
-        jnp.concatenate([sine, jnp.zeros_like(sine)], axis=1)])
+    cosine, sine = np.cos(angles), np.sin(angles)
+    cosine = np.concatenate([cosine, cosine], axis=1)
+    sine = np.concatenate([-sine, sine], axis=1)
+    return np.stack([
+        np.concatenate([cosine, cosine], axis=1), np.concatenate([sine, sine], axis=1),
+        np.concatenate([cosine, np.ones_like(cosine)], axis=1),
+        np.concatenate([sine, np.zeros_like(sine)], axis=1)]).astype(np.float32)
 
 
 def local(
@@ -686,7 +871,7 @@
     experts = gate_weight.shape[0]
     qw = query_weight.shape[1]
     kw = key_matrix.shape[1]
-    tables = rotary_tables(rows)
+    tables = jnp.asarray(rotary_tables(rows))
 
     small = jnp.concatenate(
         [query_weight, key_matrix, value_matrix, output_weight.T, first_gain[:, None], second_gain[:, None],

time: 304 us -> 274 us (0.901)
  Pallas kernels: 283 us -> 258 us
  other arithmetic: 5.14 us -> 0.9 us
    pallas_call x1, Pallas kernels: 73.1 us -> 59.4 us  [backward(): pl.pallas_call(backward_kernel, out_shape=(rows, rows, shape((1, PART, UN...]
    pallas_call x1, Pallas kernels: 109 us -> 100 us  [forward(): pl.pallas_call(forward_kernel, out_shape=(shape((ROWS, WIDTH), F32), rows...]
    pallas_call x1, Pallas kernels: 102 us -> 98.4 us  [run_experts(): pl.pallas_call(experts_kernel, out_shape=(rows, rows, shape((ROWS, WIDTH)...]
where the time goes in v4:
time: 274 us
  Pallas kernels  258 us (94%)
  local copies, waits for them, and re-layouts  14.1 us (5%)
    pallas_call x1, Pallas kernels, forward(): pl.pallas_call(forward_kernel, out_shape=(shape((ROWS, WIDTH), F32), rows...  100 us
    pallas_call x1, Pallas kernels, run_experts(): pl.pallas_call(experts_kernel, out_shape=(rows, rows, shape((ROWS, WIDTH)...  98.4 us
    pallas_call x1, Pallas kernels, backward(): pl.pallas_call(backward_kernel, out_shape=(rows, rows, shape((1, PART, UN...  59.4 us
    unnamed x11, local copies, waits for them, and re-layouts  5.73 us

profile of v4, /device:TPU:1, one launch (start us, length us, event | category | flops | bytes accessed | tf_op | source)
XLA Modules:
  0.0 273.6 jit_solution(1487857231466573693)
XLA Ops:
  0.7 0.9 select_reduce_fusion
  1.6 0.8 copy.29
  2.3 0.8 copy.30
  3.1 1.5 concatenate.3
  4.6 1.0 copy.31.combined
  5.6 100.2 %forward.1 = (f32[128,1024]{1,0:T(8,128)}, bf16[8,128,1024]{2,1,0:T(8,128)(2,1)}, bf16[8,128,1024]{2,1,0:T(8,128)(2,1)}, bf16[4,16,64,512]{3,2,1,0:T(8,128)(2,1)...) custom-call(bf16[128,1024]{1,0:T(8,128)(2,1)} %x.3, ...), custom_call_target="tpu_custom_call" | custom-call | tf_op jit(solution)/shard_map/forward/pallas_call | solution.py:533
  105.8 98.4 %experts.1 = (bf16[8,128,1024]{2,1,0:T(8,128)(2,1)}, bf16[8,128,1024]{2,1,0:T(8,128)(2,1)}, f32[128,1024]{1,0:T(8,128)}, f32[8,1024]{1,0:T(8,128)}, f32[4,64,512...) custom-call(bf16[1024,1024]{1,0:T(8,128)(2,1)} %bitcast.21, bf16[1024,1024]{1,0:T(8,128)(2,1)} %bitcast.22, ...), custom_call_target="tpu_custom_call" | custom-call | tf_op jit(solution)/shard_map/experts/pallas_call | solution.py:688
  204.2 0.0 copy-start.2
  204.2 59.4 %backward.1 = (bf16[128,1024]{1,0:T(8,128)(2,1)}, bf16[128,1024]{1,0:T(8,128)(2,1)}, f32[1,64,512]{2,1,0:T(8,128)}, f32[8,1024]{1,0:T(8,128)}) custom-call(bf16[8,128,1024]{2,1,0:T(8,128)(2,1)} %get-tuple-element.41.moe_partial, bf16[8,128,1024]{2,1,0:T(8,128)(2,1)} %get-tuple-element.42.branch_full, f32[128,1024]{1,0:T(8,128)} %get-tuple-element.43.state_grad, ...), custom_call_target="tpu_custom_call" | custom-call | tf_op jit(solution)/shard_map/backward/pallas_call | solution.py:837
  263.6 0.0 copy-start.1
  263.6 0.0 copy-start
  263.6 0.8 constant_dynamic-slice_fusion
  264.4 0.5 slice_bitcast_fusion.1
  265.0 1.4 slice_bitcast_fusion
  266.4 1.5 fusion
  267.9 1.7 copy.37
  269.6 1.7 copy.38
  271.2 0.0 copy-done.2
  271.2 0.8 copy.39
  272.0 0.0 copy-done.1
  272.0 0.8 copy.40
  272.8 0.0 copy-done
  272.8 0.8 copy.41
  (2 shorter events, 0.0 us)
Async XLA Ops:
  204.2 67.1 %copy-start.2 = (f32[4,64,512]{2,1,0:T(8,128)S(1)}, f32[4,64,512]{2,1,0:T(8,128)}, u32[]{:S(2)}) copy-start(f32[4,64,512]{2,1,0:T(8,128)} %get-tuple-element.82) | copy-start | bytes 1572868
  263.6 8.4 %copy-start.1 = (f32[4,64,512]{2,1,0:T(8,128)S(1)}, f32[4,64,512]{2,1,0:T(8,128)}, u32[]{:S(2)}) copy-start(f32[4,64,512]{2,1,0:T(8,128)} %get-tuple-element.83) | copy-start | bytes 1572868
  263.6 9.2 %copy-start = (f32[4,64,512]{2,1,0:T(8,128)S(1)}, f32[4,64,512]{2,1,0:T(8,128)}, u32[]{:S(2)}) copy-start(f32[4,64,512]{2,1,0:T(8,128)} %get-tuple-element.56) | copy-start | bytes 1572868

commit v5 on v4

--- a/solution.py
+++ b/solution.py
@@ -451,7 +451,6 @@
     smalls.finish()
     pick = (lax.broadcasted_iota(jnp.int32, (8, 128), 0) == lax.broadcasted_iota(jnp.int32, (8, 128), 1))
     gains[...] = nt(pick.astype(F32).astype(BF16), small_out[0, :, :, 384:].reshape(WIDTH, 128))
-    gates.forward()
     qkv_weight = small_out[0, :, :, :256].reshape(WIDTH, 256)
 
     def project(i, carry):
@@ -467,16 +466,16 @@
 
     rows_in.own.wait()
     lax.fori_loop(p.tx * NY, p.tx * NY + NY, project, 0)
-    ups.forward()
     rows_in.relay()
     grads = TensorGather(p, out_grad, grad_out, pairs[4], local.at[4])
     for j in (1, 3, 2):
         if j == 2:
+            gates.forward()
             rows_in.arrive()
-            downs.forward()
-            grads.forward()
         start = p.x(j) * NY
         lax.fori_loop(start, start + NY, project, 0)
+    grads.forward()
+    ups.forward()
     doubled(qkv[:, 128:], keys, values)
     out_weight = small_out[0, :, :, 256:384].reshape(WIDTH, 128)
     branch = TensorScatter(p, partial, *branch_scratch)
@@ -493,13 +492,14 @@
         partial[2 * b : 2 * b + 2] = nt(out, out_weight).astype(BF16).reshape(2, ROWS, WIDTH)
         for j in range(1, NX):
             pl.when(p.x(j) == b)(functools.partial(branch.send, j))
-        if b == 1:
+        if b == 0:
+            downs.forward()
+        if b == 2:
             grads.relay()
-            gates.spread()
     branch.own.start()
     branch.relay()
+    gates.spread()
     ups.spread()
-    gates.far()
     branch.exchange()
     downs.spread()
     branch.arrive()
@@ -514,10 +514,11 @@
 
     lax.fori_loop(0, ROWS // 32, step, 0)
     gather = TensorGather(p, normed_two, normed_out, pairs[6], local.at[6])
+    gates.far()
     gather.forward()
     ups.far()
+    downs.far()
     gather.relay()
-    downs.far()
     branch.finish()
     gather.finish()
     rows_in.sent()
@@ -555,9 +556,9 @@
 
 
 def experts_kernel(
-    x, out_grad_full, gate, up, down, combined, hidden, gains_in, out_grad,
+    x_in, out_grad_in, gate, up, down, combined, hidden, gains_in, out_grad,
     moe_out, branch_out, state_grad, gain_part, gate_out, up_out, down_out,
-    gate_buf, up_buf, down_buf, moe, rows_acc, units, gate_pre, up_pre, rows_out, branch, *scratch,
+    x, out_grad_full, gate_buf, up_buf, down_buf, moe, rows_acc, units, gate_pre, up_pre, rows_out, branch, *scratch,
 ):
     p = Place()
     load_sem, scratch = scratch[0], scratch[1:]
@@ -571,7 +572,8 @@
             pltpu.make_async_copy(ref.at[e], buf.at[slot], load_sem.at[slot, k])
             for k, (ref, buf) in enumerate(((gate, gate_buf), (up, up_buf), (down, down_buf)))]
 
-    loads = load(0)
+    loads = load(0) + [
+        pltpu.make_async_copy(x_in, x, load_sem.at[2, 0]), pltpu.make_async_copy(out_grad_in, out_grad_full, load_sem.at[2, 1])]
     for copy in loads:
         copy.start()
     meet(p)
@@ -586,8 +588,8 @@
             columns = pl.ds(pl.multiple_of(i * 256, 256), 256)
             tokens = x[:, columns]
             found = (
-                tn(tokens, gate_pre[e % 2]), tn(tokens, up_pre[e % 2]),
-                tn(out_grad_full[:, columns], units[e % 2]) * RES_SCALE)
+                tn(tokens, gate_pre[...]), tn(tokens, up_pre[...]),
+                tn(out_grad_full[:, columns], units[...]) * RES_SCALE)
             for k in range(3):
                 for r in range(4):
                     z = (i % 2) * 2 + r // 2
@@ -596,10 +598,6 @@
 
         lax.fori_loop(0, 4, weigh, 0)
         scatters.append(PartScatter(p, *parts[e]))
-        if e == 1:
-            scatters[0].relay()
-        if e == 3:
-            scatters[2].along()
 
     for e in range(4):
         slot = e % 2
@@ -623,9 +621,9 @@
             grad = nn(out_grad_full[rows], down_buf[slot]) * (RES_SCALE * scale)
             to_gate = (grad * up_part * (sig + act * (1.0 - sig))).astype(BF16)
             to_up = (grad * act).astype(BF16)
-            units[slot, rows] = unit
-            gate_pre[slot, rows] = to_gate
-            up_pre[slot, rows] = to_up
+            units[rows] = unit
+            gate_pre[rows] = to_gate
+            up_pre[rows] = to_up
             moe_part = nt(unit, down_buf[slot])
             rows_part = nt(to_gate, gate_buf[slot]) + nt(to_up, up_buf[slot])
             if e == 0:
@@ -642,20 +640,23 @@
             return carry
 
         lax.fori_loop(0, WIDTH // QBLOCK, block, 0)
-        if e == 1 or e == 2:
-            scatters[e - 1].along()
         if e == 3:
             rows_sum.own.start()
             rows_sum.relay()
-            scatters[1].relay()
-        for done in ((0,), (1,), (), (2, 3))[e]:
-            weigh_expert(done)
-
-    scatters[0].pair()
+        if e >= 1:
+            scatters[e - 1].along()
+        if e == 3:
+            scatters[1].pair()
+        weigh_expert(e)
+        if e == 1 or e == 2:
+            scatters[e - 1].relay()
+        if e == 2:
+            scatters[0].pair()
+
+    scatters[2].relay()
     scatters[3].along()
-    scatters[2].relay()
     rows_sum.exchange()
-    scatters[1].pair()
+    scatters[0].finish(((gate_out, 0), (up_out, 0), (down_out, 0)))
     rows_sum.arrive()
 
     def step(i, carry):
@@ -673,7 +674,6 @@
     gather.forward()
     scatters[2].pair()
     gather.relay()
-    scatters[0].finish(((gate_out, 0), (up_out, 0), (down_out, 0)))
     scatters[1].finish(((gate_out, 1), (up_out, 1), (down_out, 1)))
     scatters[3].pair()
     scatters[2].finish(((gate_out, 2), (up_out, 2), (down_out, 2)))
@@ -688,22 +688,26 @@
     return pl.pallas_call(
         experts_kernel,
         out_shape=(rows, rows, shape((ROWS, WIDTH), F32), shape((8, WIDTH), F32), weight, weight, weight),
-        in_specs=[VMEM, VMEM, ANY, ANY, ANY] + [VMEM] * 4, out_specs=(VMEM, ANY) + (VMEM,) * 5,
-        scratch_shapes=[pltpu.VMEM((2, WIDTH, UNITS), BF16)] * 3 + [pltpu.VMEM((WIDTH, WIDTH), F32)] * 2
-        + [pltpu.VMEM((2, WIDTH, UNITS), BF16)] * 3
-        + [pltpu.VMEM((8, ROWS, WIDTH), BF16), pltpu.VMEM((ROWS, WIDTH), BF16), DMA((2, 3))]
+        in_specs=[ANY] * 5 + [VMEM] * 4, out_specs=(VMEM, ANY) + (VMEM,) * 5,
+        scratch_shapes=[pltpu.VMEM((WIDTH, WIDTH), BF16)] * 2 + [pltpu.VMEM((2, WIDTH, UNITS), BF16)] * 3 + [pltpu.VMEM((WIDTH, WIDTH), F32)] * 2
+        + [pltpu.VMEM((WIDTH, UNITS), BF16)] * 3
+        + [pltpu.VMEM((8, ROWS, WIDTH), BF16), pltpu.VMEM((ROWS, WIDTH), BF16), DMA((3, 3))]
         + TensorScatter.scratch() + PartScatter.scratch(3) * 4 + sems(9) + [DMA((1,))],
         compiler_params=params(2, 63), name="experts",
     )(*args)
 
 
 def backward_kernel(
-    moe_partial, branch_full, state_grad, gain_part, hidden, gains_in, x, normed, qkv, attended, log_total, small,
-    tables,
-    block_out, input_grad, small_out, gains,
+    moe_partial, branch_full, state_grad, gain_part, hidden, gains_in, x, normed_in, qkv, attended, log_total, small,
+    tables_in,
+    block_out, input_grad, small_out, gains, normed, tables, load_sem,
     keys, values, key_grad, value_grad, pre, partial, gain_buf, *scratch,
 ):
     p = Place()
+    loads = [
+        pltpu.make_async_copy(tables_in, tables, load_sem.at[0]), pltpu.make_async_copy(normed_in, normed, load_sem.at[1])]
+    for copy in loads:
+        copy.start()
     meet(p)
     sums, scratch = scratch[:7], scratch[7:]
     more_sums, scratch = scratch[:7], scratch[7:]
@@ -718,6 +722,8 @@
     gains[...] = gain_part[...]
 
     out_weight = small[0, :, :, 256:384].reshape(WIDTH, 128)
+    for copy in loads:
+        copy.wait()
     for b in range(WIDTH // QBLOCK):
         if b == 2:
             moe_sum.relay()
@@ -759,8 +765,8 @@
 
     copies = []
     stages = iter((
-        [p.x_dev(j) for j in range(1, NX)], [p.tensor_pair()], [p.core_dev()],
-        [p.z_dev(j) for j in range(1, NZ)], [p.y_dev()]))
+        [p.core_dev()], [p.z_dev(j) for j in range(1, NZ)], [p.y_dev()],
+        [p.x_dev(j) for j in range(1, NX)], [p.tensor_pair()]))
 
     def gains_send():
         stage = len(copies)
@@ -837,8 +843,9 @@
     return pl.pallas_call(
         backward_kernel,
         out_shape=(rows, rows, shape((1, PART, UNITS), F32), shape((8, WIDTH), F32)),
-        in_specs=[VMEM] * 13, out_specs=(VMEM,) * 4,
+        in_specs=[VMEM] * 7 + [ANY] + [VMEM] * 4 + [ANY], out_specs=(VMEM,) * 4,
         scratch_shapes=[
+            pltpu.VMEM((WIDTH, WIDTH), BF16), pltpu.VMEM((4, WIDTH, 128), F32), DMA((2,)),
             pltpu.VMEM((WIDTH, 128), BF16), pltpu.VMEM((WIDTH, 128), BF16),
             pltpu.VMEM((WIDTH, 128), F32), pltpu.VMEM((WIDTH, 128), F32), pltpu.VMEM((WIDTH, 256), BF16),
             pltpu.VMEM((8, ROWS, WIDTH), BF16), pltpu.VMEM((14, 8, WIDTH), F32)]

time: 274 us -> 268 us (0.978)
  Pallas kernels: 258 us -> 251 us
    pallas_call x1, Pallas kernels: 59.4 us -> 51.5 us  [backward(): pl.pallas_call(backward_kernel, out_shape=(rows, rows, shape((1, PART, UN...]
    pallas_call x1, Pallas kernels: 98.4 us -> 102 us  [run_experts(): pl.pallas_call(experts_kernel, out_shape=(rows, rows, shape((ROWS, WIDTH)...]
where the time goes in v5:
time: 268 us; the launch traced here: 267 us
  Pallas kernels  251 us (94%)
  local copies, waits for them, and re-layouts  14.1 us (5%)
    pallas_call x1, Pallas kernels, run_experts(): pl.pallas_call(experts_kernel, out_shape=(rows, rows, shape((ROWS, WIDTH)...  102 us
    pallas_call x1, Pallas kernels, forward(): pl.pallas_call(forward_kernel, out_shape=(shape((ROWS, WIDTH), F32), rows...  97.6 us
    pallas_call x1, Pallas kernels, backward(): pl.pallas_call(backward_kernel, out_shape=(rows, rows, shape((1, PART, UN...  51.5 us
    unnamed x11, local copies, waits for them, and re-layouts  5.73 us

profile of v5, /device:TPU:1, one launch (start us, length us, event | category | flops | bytes accessed | tf_op | source)
XLA Modules:
  0.0 267.1 jit_solution(10933704018849832708)
XLA Ops:
  0.7 0.9 select_reduce_fusion
  1.6 0.8 copy.29
  2.3 0.8 copy.30
  3.1 1.5 concatenate.3
  4.6 1.0 copy.31.combined
  5.6 97.6 %forward.1 = (f32[128,1024]{1,0:T(8,128)}, bf16[8,128,1024]{2,1,0:T(8,128)(2,1)}, bf16[8,128,1024]{2,1,0:T(8,128)(2,1)}, bf16[4,16,64,512]{3,2,1,0:T(8,128)(2,1)...) custom-call(bf16[128,1024]{1,0:T(8,128)(2,1)} %x.3, ...), custom_call_target="tpu_custom_call" | custom-call | tf_op jit(solution)/shard_map/forward/pallas_call | solution.py:534
  103.2 102.3 %experts.1 = (bf16[8,128,1024]{2,1,0:T(8,128)(2,1)}, bf16[8,128,1024]{2,1,0:T(8,128)(2,1)}, f32[128,1024]{1,0:T(8,128)}, f32[8,1024]{1,0:T(8,128)}, f32[4,64,512...) custom-call(bf16[1024,1024]{1,0:T(8,128)(2,1)} %bitcast.21, bf16[1024,1024]{1,0:T(8,128)(2,1)} %bitcast.22, ...), custom_call_target="tpu_custom_call" | custom-call | tf_op jit(solution)/shard_map/experts/pallas_call | solution.py:688
  205.6 0.0 copy-start.2
  205.6 51.5 %backward.1 = (bf16[128,1024]{1,0:T(8,128)(2,1)}, bf16[128,1024]{1,0:T(8,128)(2,1)}, f32[1,64,512]{2,1,0:T(8,128)}, f32[8,1024]{1,0:T(8,128)}) custom-call(bf16[8,128,1024]{2,1,0:T(8,128)(2,1)} %get-tuple-element.41.moe_partial, bf16[8,128,1024]{2,1,0:T(8,128)(2,1)} %get-tuple-element.42.branch_full, f32[128,1024]{1,0:T(8,128)} %get-tuple-element.43.state_grad, ...), custom_call_target="tpu_custom_call" | custom-call | tf_op jit(solution)/shard_map/backward/pallas_call | solution.py:843
  257.0 0.0 copy-start.1
  257.1 0.0 copy-start
  257.1 0.8 constant_dynamic-slice_fusion
  257.9 0.5 slice_bitcast_fusion.1
  258.4 1.4 slice_bitcast_fusion
  259.8 1.5 fusion
  261.4 1.7 copy.37
  263.0 1.7 copy.38
  264.7 0.0 copy-done.2
  264.7 0.8 copy.39
  265.5 0.0 copy-done.1
  265.5 0.8 copy.40
  266.3 0.0 copy-done
  266.3 0.8 copy.41
  (2 shorter events, 0.0 us)
Async XLA Ops:
  205.6 59.1 %copy-start.2 = (f32[4,64,512]{2,1,0:T(8,128)S(1)}, f32[4,64,512]{2,1,0:T(8,128)}, u32[]{:S(2)}) copy-start(f32[4,64,512]{2,1,0:T(8,128)} %get-tuple-element.82) | copy-start | bytes 1572868
  257.0 8.4 %copy-start.1 = (f32[4,64,512]{2,1,0:T(8,128)S(1)}, f32[4,64,512]{2,1,0:T(8,128)}, u32[]{:S(2)}) copy-start(f32[4,64,512]{2,1,0:T(8,128)} %get-tuple-element.83) | copy-start | bytes 1572868
  257.1 9.2 %copy-start = (f32[4,64,512]{2,1,0:T(8,128)S(1)}, f32[4,64,512]{2,1,0:T(8,128)}, u32[]{:S(2)}) copy-start(f32[4,64,512]{2,1,0:T(8,128)} %get-tuple-element.56) | copy-start | bytes 1572868

commit v6 on v5

--- a/solution.py
+++ b/solution.py
@@ -430,11 +430,22 @@
 
 
 def forward_kernel(
-    x, small, gate, up, down, out_grad, tables,
-    hidden, normed_out, grad_out, gate_out, up_out, down_out, normed, qkv, attended, log_total, small_out, gains,
-    x_buf, keys, values, partial, normed_two, *scratch,
+    x, query, key, value, output, gain_pair, gate, up, down, out_grad, tables,
+    hidden, normed_out, grad_out, gate_out, up_out, down_out, normed_hbm, qkv_hbm, attended_hbm, log_total, small_out,
+    gains,
+    small, normed, qkv, attended, keep_sem, x_buf, keys, values, partial, normed_two, *scratch,
 ):
     p = Place()
+    small[0, :, :128] = query[...]
+    small[0, :, 128:256] = jnp.concatenate([key[...], value[...]], axis=1)
+    small[0, :, 256:384] = output[...]
+    row = lax.broadcasted_iota(jnp.int32, (PART, PART), 0)
+    same = row == lax.broadcasted_iota(jnp.int32, (PART, PART), 1)
+    gain_lanes = jnp.zeros((PART, 128), F32)
+    for k in range(2):
+        column = jnp.sum(jnp.where(same, gain_pair[k : k + 1].astype(F32), 0.0), axis=1, keepdims=True)
+        gain_lanes = jnp.where(lanes(PART) == k, column, gain_lanes)
+    small[0, :, 384:] = gain_lanes.astype(BF16)
     meet(p)
     branch_scratch, scratch = scratch[:7], scratch[7:]
     pairs = [scratch[2 * i : 2 * i + 2] for i in range(7)]
@@ -497,6 +508,11 @@
         if b == 2:
             grads.relay()
     branch.own.start()
+    keep = [
+        pltpu.make_async_copy(src, dst, keep_sem.at[k])
+        for k, (src, dst) in enumerate(((normed, normed_hbm), (qkv, qkv_hbm), (attended, attended_hbm)))]
+    for copy in keep:
+        copy.start()
     branch.relay()
     gates.spread()
     ups.spread()
@@ -522,13 +538,15 @@
     branch.finish()
     gather.finish()
     rows_in.sent()
+    for copy in keep:
+        copy.wait()
     grads.finish()
     gates.finish()
     ups.finish()
     downs.finish()
 
 
-def forward(x, small, gate, up, down, out_grad, tables):
+def forward(*args):
     full = shape((4, 16, PART, UNITS))
     rows = shape((8, ROWS, WIDTH))
     return pl.pallas_call(
@@ -537,15 +555,17 @@
             shape((ROWS, WIDTH), F32), rows, rows, full, full, full, shape((WIDTH, WIDTH)), shape((WIDTH, 256)),
             shape((WIDTH, 128)), shape((WIDTH // QBLOCK, 2 * QBLOCK, 1), F32), shape((1, 16, PART, UNITS)),
             shape((8, WIDTH), F32)),
-        in_specs=[VMEM, VMEM, ANY, ANY, ANY, ANY, VMEM],
-        out_specs=(VMEM,) + (ANY,) * 5 + (VMEM,) * 6,
+        in_specs=[VMEM] * 6 + [ANY] * 4 + [VMEM],
+        out_specs=(VMEM,) + (ANY,) * 8 + (VMEM,) * 3,
         scratch_shapes=[
+            pltpu.VMEM((1, PART, UNITS), BF16), pltpu.VMEM((WIDTH, WIDTH), BF16), pltpu.VMEM((WIDTH, 256), BF16),
+            pltpu.VMEM((WIDTH, 128), BF16), DMA((3,)),
             pltpu.VMEM((8, ROWS, WIDTH), BF16), pltpu.VMEM((WIDTH, 128), BF16), pltpu.VMEM((WIDTH, 128), BF16),
             pltpu.VMEM((8, ROWS, WIDTH), BF16), pltpu.VMEM((ROWS, WIDTH), BF16)]
         + TensorScatter.scratch() + sems(17) + sems(9) + sems(17) + sems(17) + sems(9) + sems(17) + sems(9)
         + [DMA((7,))],
         compiler_params=params(1, 56), name="forward",
-    )(x, small, gate, up, down, out_grad, tables)
+    )(*args)
 
 
 def norm_pull(state, gain, grad):
@@ -608,9 +628,11 @@
             for copy in loads:
                 copy.start()
 
+        size = QBLOCK if e == 3 else 2 * QBLOCK
+
         def block(step, carry):
-            i = rows_sum.row(step)
-            rows = pl.ds(pl.multiple_of(i * QBLOCK, QBLOCK), QBLOCK)
+            i = rows_sum.row(step) if e == 3 else step
+            rows = pl.ds(pl.multiple_of(i * size, size), size)
             tokens = x[rows]
             gate_part = nn(tokens, gate_buf[slot])
             up_part = nn(tokens, up_buf[slot])
@@ -639,7 +661,7 @@
                 rows_sum.send_after(step)
             return carry
 
-        lax.fori_loop(0, WIDTH // QBLOCK, block, 0)
+        lax.fori_loop(0, WIDTH // size, block, 0)
         if e == 3:
             rows_sum.own.start()
             rows_sum.relay()
@@ -880,11 +902,10 @@
     kw = key_matrix.shape[1]
     tables = jnp.asarray(rotary_tables(rows))
 
-    small = jnp.concatenate(
-        [query_weight, key_matrix, value_matrix, output_weight.T, first_gain[:, None], second_gain[:, None],
-         jnp.zeros((PART, 126), BF16)], axis=1)
     (hidden, normed_two, out_grad_full, gate_full, up_full, down_full, normed, qkv, attended, log_total, small,
-     gains) = forward(inputs, small[None], gate_weight, up_weight, jnp.swapaxes(down_weight, 1, 2), out_grad, tables)
+     gains) = forward(
+        inputs, query_weight, key_matrix, value_matrix, output_weight.T, jnp.stack([first_gain, second_gain]),
+        gate_weight, up_weight, jnp.swapaxes(down_weight, 1, 2), out_grad, tables)
     normed_two = normed_two.reshape(rows, WIDTH)
     out_grad_full = out_grad_full.reshape(rows, WIDTH)
     gate_full = gate_full.reshape(experts, WIDTH, UNITS)

time: 268 us -> 265 us (0.989)
  local copies, waits for them, and re-layouts: 14.1 us -> 11 us
where the time goes in v6:
time: 265 us
  Pallas kernels  251 us (95%)
  local copies, waits for them, and re-layouts  11 us (4%)
    pallas_call x1, Pallas kernels, run_experts(): pl.pallas_call(experts_kernel, out_shape=(rows, rows, shape((ROWS, WIDTH)...  102 us
    pallas_call x1, Pallas kernels, forward(): pl.pallas_call(forward_kernel, out_shape=(shape((ROWS, WIDTH), F32), rows...  96.9 us
    pallas_call x1, Pallas kernels, backward(): pl.pallas_call(backward_kernel, out_shape=(rows, rows, shape((1, PART, UN...  51.5 us
    unnamed x11, local copies, waits for them, and re-layouts  5.73 us

profile of v6, /device:TPU:1, one launch (start us, length us, event | category | flops | bytes accessed | tf_op | source)
XLA Modules:
  0.0 264.6 jit_solution(12919425505292647475)
XLA Ops:
  0.7 1.2 pad_maximum_fusion.gain_pair
  1.9 0.9 select_reduce_fusion
  2.7 1.0 copy.27.combined
  3.8 96.9 %forward.1 = (f32[128,1024]{1,0:T(8,128)}, bf16[8,128,1024]{2,1,0:T(8,128)(2,1)}, bf16[8,128,1024]{2,1,0:T(8,128)(2,1)}, bf16[4,16,64,512]{3,2,1,0:T(8,128)(2,1)...) custom-call(bf16[128,1024]{1,0:T(8,128)(2,1)} %x.3, ...), custom_call_target="tpu_custom_call" | custom-call | tf_op jit(solution)/shard_map/forward/pallas_call | solution.py:552
  100.7 102.3 %experts.1 = (bf16[8,128,1024]{2,1,0:T(8,128)(2,1)}, bf16[8,128,1024]{2,1,0:T(8,128)(2,1)}, f32[128,1024]{1,0:T(8,128)}, f32[8,1024]{1,0:T(8,128)}, f32[4,64,512...) custom-call(bf16[1024,1024]{1,0:T(8,128)(2,1)} %bitcast.20, bf16[1024,1024]{1,0:T(8,128)(2,1)} %bitcast.21, ...), custom_call_target="tpu_custom_call" | custom-call | tf_op jit(solution)/shard_map/experts/pallas_call | solution.py:710
  203.0 0.0 copy-start.2
  203.0 51.5 %backward.1 = (bf16[128,1024]{1,0:T(8,128)(2,1)}, bf16[128,1024]{1,0:T(8,128)(2,1)}, f32[1,64,512]{2,1,0:T(8,128)}, f32[8,1024]{1,0:T(8,128)}) custom-call(bf16[8,128,1024]{2,1,0:T(8,128)(2,1)} %get-tuple-element.41.moe_partial, bf16[8,128,1024]{2,1,0:T(8,128)(2,1)} %get-tuple-element.42.branch_full, f32[128,1024]{1,0:T(8,128)} %get-tuple-element.43.state_grad, ...), custom_call_target="tpu_custom_call" | custom-call | tf_op jit(solution)/shard_map/backward/pallas_call | solution.py:865
  254.6 0.0 copy-start.1
  254.6 0.0 copy-start
  254.6 0.8 constant_dynamic-slice_fusion
  255.4 0.5 slice_bitcast_fusion.1
  255.9 1.4 slice_bitcast_fusion
  257.3 1.5 fusion
  258.9 1.7 copy.33
  260.5 1.7 copy.34
  262.2 0.0 copy-done.2
  262.2 0.8 copy.35
  263.0 0.0 copy-done.1
  263.0 0.8 copy.36
  263.8 0.0 copy-done
  263.8 0.8 copy.37
  (1 shorter events, 0.0 us)
Async XLA Ops:
  203.0 59.2 %copy-start.2 = (f32[4,64,512]{2,1,0:T(8,128)S(1)}, f32[4,64,512]{2,1,0:T(8,128)}, u32[]{:S(2)}) copy-start(f32[4,64,512]{2,1,0:T(8,128)} %get-tuple-element.82) | copy-start | bytes 1572868
  254.6 8.4 %copy-start.1 = (f32[4,64,512]{2,1,0:T(8,128)S(1)}, f32[4,64,512]{2,1,0:T(8,128)}, u32[]{:S(2)}) copy-start(f32[4,64,512]{2,1,0:T(8,128)} %get-tuple-element.83) | copy-start | bytes 1572868
  254.6 9.2 %copy-start = (f32[4,64,512]{2,1,0:T(8,128)S(1)}, f32[4,64,512]{2,1,0:T(8,128)}, u32[]{:S(2)}) copy-start(f32[4,64,512]{2,1,0:T(8,128)} %get-tuple-element.56) | copy-start | bytes 1572868
